TPU v7x, 32 devices: a whole 2x2x4 slice. The times are simulated.
32 devices in a mesh: dp: 8 (over z, core), seq: 4 (over y, x).
Axes of the slice: x: 2, y: 2, z: 4, core: 2. Of those that a mesh axis runs over, the one named last changes fastest.
Arguments:
- inputs: bfloat16 [16, 1024, 768], P('dp', 'seq'), may hold values from -6 to 6
- w_query: bfloat16 [768, 768], P('seq'), may hold values from -0.109375 to 0.109375
- w_key: bfloat16 [768, 768], P('seq'), may hold values from -0.109375 to 0.109375
- w_value: bfloat16 [768, 768], P('seq'), may hold values from -0.21875 to 0.21875
- w_out: bfloat16 [768, 768], P('seq'), may hold values from -0.875 to 0.875
- w_ffn_in: bfloat16 [768, 3072], P('seq'), may hold values from -0.21875 to 0.21875
- w_ffn_out: bfloat16 [3072, 768], P('seq'), may hold values from -0.15625 to 0.15625
- attn_gain: bfloat16 [768], P('seq'), may hold values from 0.099609375 to 1.8984375
- ffn_gain: bfloat16 [768], P('seq'), may hold values from 0.099609375 to 1.8984375
- rel_bias: bfloat16 [32, 12], P('seq'), may hold values from -3 to 3
- doc_lengths: int32 [16], P('dp'), may hold values from 64 to 1024, as said below
- cotangent: bfloat16 [16, 1024, 768], P('dp', 'seq'), may hold values from -6 to 6
Outputs:
- pooled: float32 [16, 768], P('dp')
- grad_input: float32 [16, 1024, 768], P('dp', 'seq')
- grad_query: float32 [768, 768], P('seq')
- grad_key: float32 [768, 768], P('seq')
- grad_value: float32 [768, 768], P('seq')
- grad_out_proj: float32 [768, 768], P('seq')
- grad_ffn_in: float32 [768, 3072], P('seq')
- grad_ffn_out: float32 [3072, 768], P('seq')
- grad_attn_gain: float32 [768], P('seq')
- grad_ffn_gain: float32 [768], P('seq')
- grad_rel_bias: float32 [32, 12], P('seq')
Inputs may be any that keep to these rules, and one draw needn't show every extreme that they name: `doc_lengths`: each length is one of 64, 128, 256, 512 and 1024; some document has length 1024.
All inputs are finite; a program needn't handle non-finite values.
Results may differ from a plain program's by a relative error of at most 0.028.
Values may be sent and summed in bfloat16 or wider, within the bound.
A program may use at most 256 MiB of HBM per device.

v0:
```python
import math

import jax
import jax.numpy as jnp
from jax import lax
from jax.sharding import PartitionSpec as P

EPS = 1e-06
THRESHOLDS = (12, 16, 23, 32, 46, 64, 91)
NEGATIVE = -1000000000.0
GELU_C = math.sqrt(2.0 / math.pi)
GELU_K = 0.044715


def bucket_ids(query_pos, key_pos):
    offset = key_pos[None, :] - query_pos[:, None]
    distance = jnp.abs(offset)
    upper = jnp.where(offset > 0, 16, 0).astype(jnp.int32)
    beyond = jnp.full(distance.shape, 8, jnp.int32)
    for threshold in THRESHOLDS:
        beyond = beyond + (distance >= threshold).astype(jnp.int32)
    return upper + jnp.where(distance < 8, distance, beyond)


def gelu_slope(value):
    inner = GELU_C * (value + GELU_K * value * value * value)
    tangent = jnp.tanh(inner)
    return 0.5 * (1.0 + tangent) + 0.5 * value * (1.0 - tangent * tangent) * GELU_C * (
        1.0 + 3.0 * GELU_K * value * value
    )


def outer_sum(left, right):
    return lax.dot_general(
        left, right, (((0,), (0,)), ((), ())), preferred_element_type=jnp.float32
    )


def back_project(grad, weight):
    return lax.dot_general(
        grad, weight, (((1,), (1,)), ((), ())), preferred_element_type=jnp.float32
    )


def norm_backward(source, scale, gain, grad_normed):
    grad_gain = jnp.sum(grad_normed * source * scale, 0)
    grad_scaled = grad_normed * gain
    grad_source = scale * grad_scaled - source * scale * scale * scale * jnp.mean(
        grad_scaled * source, -1, keepdims=True
    )
    return (grad_gain, grad_source)


def on_device(
    inputs,
    w_query,
    w_key,
    w_value,
    w_out,
    w_ffn_in,
    w_ffn_out,
    attn_gain,
    ffn_gain,
    rel_bias,
    doc_lengths,
    cotangent,
):
    blocks, shard_len, width = inputs.shape
    heads = rel_bias.shape[1]
    head_dim = width // heads
    full_len = shard_len * lax.axis_size("seq")
    total_rows = blocks * shard_len
    gathered = (
        lax.all_gather(w_query, "seq", axis=0, tiled=True),
        lax.all_gather(w_key, "seq", axis=0, tiled=True),
        lax.all_gather(w_value, "seq", axis=0, tiled=True),
        lax.all_gather(w_out, "seq", axis=0, tiled=True),
        lax.all_gather(w_ffn_in, "seq", axis=0, tiled=True),
        lax.all_gather(w_ffn_out, "seq", axis=0, tiled=True),
        lax.all_gather(attn_gain, "seq", axis=0, tiled=True),
        lax.all_gather(ffn_gain, "seq", axis=0, tiled=True),
        lax.all_gather(rel_bias, "seq", axis=0, tiled=True),
    )
    (
        full_query,
        full_key,
        full_value,
        full_out,
        full_in,
        full_down,
        gain_one,
        gain_two,
        bias_table,
    ) = gathered
    gain_one = gain_one.astype(jnp.float32)
    gain_two = gain_two.astype(jnp.float32)
    bucket_range = jnp.arange(bias_table.shape[0], dtype=jnp.int32)
    query_pos = lax.axis_index("seq") * shard_len + jnp.arange(shard_len, dtype=jnp.int32)
    key_pos = jnp.arange(full_len, dtype=jnp.int32)
    onehot = (bucket_ids(query_pos, key_pos)[:, :, None] == bucket_range).astype(jnp.bfloat16)
    bias_heads = jnp.einsum("qkn,nh->hqk", onehot, bias_table, preferred_element_type=jnp.float32)
    key_valid = key_pos[None, :] < doc_lengths[:, None]
    query_valid = (query_pos[None, :] < doc_lengths[:, None]).astype(jnp.float32)
    flat = inputs.astype(jnp.float32).reshape(total_rows, width)
    scale_one = lax.rsqrt(jnp.mean(flat * flat, -1, keepdims=True) + EPS)
    normed_one = (flat * scale_one * gain_one).astype(jnp.bfloat16)
    queries = jnp.dot(normed_one, full_query, preferred_element_type=jnp.float32).astype(
        jnp.bfloat16
    )
    keys_local = jnp.dot(normed_one, full_key, preferred_element_type=jnp.float32).astype(
        jnp.bfloat16
    )
    values_local = jnp.dot(normed_one, full_value, preferred_element_type=jnp.float32).astype(
        jnp.bfloat16
    )
    queries_heads = queries.reshape(blocks, shard_len, heads, head_dim)
    keys_all, values_all = (
        lax.all_gather(keys_local.reshape(blocks, shard_len, width), "seq", axis=1, tiled=True),
        lax.all_gather(values_local.reshape(blocks, shard_len, width), "seq", axis=1, tiled=True),
    )
    scores = jnp.einsum(
        "bqhe,bkhe->bhqk",
        queries_heads,
        keys_all.reshape(blocks, full_len, heads, head_dim),
        preferred_element_type=jnp.float32,
    )
    logits = jnp.where(key_valid[:, None, None, :], scores + bias_heads[None], NEGATIVE)
    highest = jnp.max(logits, -1, keepdims=True)
    log_total = highest + jnp.log(jnp.sum(jnp.exp(logits - highest), -1, keepdims=True))
    probs_low = jnp.exp(logits - log_total).astype(jnp.bfloat16)
    mixed = jnp.einsum(
        "bhqk,bkhe->bqhe",
        probs_low,
        values_all.reshape(blocks, full_len, heads, head_dim),
        preferred_element_type=jnp.float32,
    )
    mixed = mixed.astype(jnp.bfloat16).reshape(total_rows, width)
    hidden = flat + jnp.dot(mixed, full_out, preferred_element_type=jnp.float32)
    scale_two = lax.rsqrt(jnp.mean(hidden * hidden, -1, keepdims=True) + EPS)
    normed_two = (hidden * scale_two * gain_two).astype(jnp.bfloat16)
    pre_act = jnp.dot(normed_two, full_in, preferred_element_type=jnp.float32)
    active = jax.nn.gelu(pre_act, approximate=True).astype(jnp.bfloat16)
    outputs = hidden + jnp.dot(active, full_down, preferred_element_type=jnp.float32)
    partial_pool = jnp.sum(outputs.reshape(blocks, shard_len, width) * query_valid[:, :, None], 1)
    pooled = lax.psum(partial_pool, "seq") / doc_lengths[:, None].astype(jnp.float32)
    regathered = (
        lax.all_gather(w_query, "seq", axis=0, tiled=True),
        lax.all_gather(w_key, "seq", axis=0, tiled=True),
        lax.all_gather(w_value, "seq", axis=0, tiled=True),
        lax.all_gather(w_out, "seq", axis=0, tiled=True),
        lax.all_gather(w_ffn_in, "seq", axis=0, tiled=True),
        lax.all_gather(w_ffn_out, "seq", axis=0, tiled=True),
        lax.all_gather(attn_gain, "seq", axis=0, tiled=True),
        lax.all_gather(ffn_gain, "seq", axis=0, tiled=True),
    )
    full_query, full_key, full_value, full_out, full_in, full_down, gain_back_one, gain_back_two = (
        regathered
    )
    gain_one = gain_back_one.astype(jnp.float32)
    gain_two = gain_back_two.astype(jnp.float32)
    grad_out = (cotangent.astype(jnp.float32) * query_valid[:, :, None]).reshape(total_rows, width)
    grad_branch = grad_out.astype(jnp.bfloat16)
    grad_down = outer_sum(active, grad_branch)
    grad_pre = (back_project(grad_branch, full_down) * gelu_slope(pre_act)).astype(jnp.bfloat16)
    grad_in = outer_sum(normed_two, grad_pre)
    grad_normed_two = back_project(grad_pre, full_in)
    grad_gain_two, grad_hidden_norm = norm_backward(hidden, scale_two, gain_two, grad_normed_two)
    grad_hidden = grad_out + grad_hidden_norm
    grad_attended = grad_hidden.astype(jnp.bfloat16)
    grad_out_proj = outer_sum(mixed, grad_attended)
    grad_mixed = (
        back_project(grad_attended, full_out)
        .astype(jnp.bfloat16)
        .reshape(blocks, shard_len, heads, head_dim)
    )
    keys_back, values_back = (keys_all, values_all)
    probs = jnp.exp(logits - log_total)
    grad_probs = jnp.einsum(
        "bqhe,bkhe->bhqk",
        grad_mixed,
        values_back.reshape(blocks, full_len, heads, head_dim),
        preferred_element_type=jnp.float32,
    )
    inner_term = jnp.sum(probs * grad_probs, -1, keepdims=True)
    grad_logits = (probs * (grad_probs - inner_term)).astype(jnp.bfloat16)
    grad_queries = jnp.einsum(
        "bhqk,bkhe->bqhe",
        grad_logits,
        keys_back.reshape(blocks, full_len, heads, head_dim),
        preferred_element_type=jnp.float32,
    )
    grad_queries = grad_queries.astype(jnp.bfloat16).reshape(total_rows, width)
    grad_table = jnp.einsum("bhqk,qkn->nh", grad_logits, onehot, preferred_element_type=jnp.float32)
    key_terms = jnp.einsum(
        "bhqk,bqhe->bkhe", grad_logits, queries_heads, preferred_element_type=jnp.float32
    ).reshape(blocks, full_len, width)
    value_terms = jnp.einsum(
        "bhqk,bqhe->bkhe", probs_low, grad_mixed, preferred_element_type=jnp.float32
    ).reshape(blocks, full_len, width)
    grad_keys, grad_values = (
        lax.psum_scatter(
            key_terms.astype(jnp.bfloat16), "seq", scatter_dimension=1, tiled=True
        ).astype(jnp.float32),
        lax.psum_scatter(
            value_terms.astype(jnp.bfloat16), "seq", scatter_dimension=1, tiled=True
        ).astype(jnp.float32),
    )
    grad_keys = grad_keys.astype(jnp.bfloat16).reshape(total_rows, width)
    grad_values = grad_values.astype(jnp.bfloat16).reshape(total_rows, width)
    grad_query_w = outer_sum(normed_one, grad_queries)
    grad_key_w = outer_sum(normed_one, grad_keys)
    grad_value_w = outer_sum(normed_one, grad_values)
    grad_normed_one = (
        back_project(grad_queries, full_query)
        + back_project(grad_keys, full_key)
        + back_project(grad_values, full_value)
    )
    grad_gain_one, grad_input_norm = norm_backward(flat, scale_one, gain_one, grad_normed_one)
    grad_input = (grad_hidden + grad_input_norm).reshape(blocks, shard_len, width)
    shards = (
        lax.psum_scatter(
            grad_query_w.astype(jnp.bfloat16), "seq", scatter_dimension=0, tiled=True
        ).astype(jnp.float32),
        lax.psum_scatter(
            grad_key_w.astype(jnp.bfloat16), "seq", scatter_dimension=0, tiled=True
        ).astype(jnp.float32),
        lax.psum_scatter(
            grad_value_w.astype(jnp.bfloat16), "seq", scatter_dimension=0, tiled=True
        ).astype(jnp.float32),
        lax.psum_scatter(
            grad_out_proj.astype(jnp.bfloat16), "seq", scatter_dimension=0, tiled=True
        ).astype(jnp.float32),
        lax.psum_scatter(
            grad_in.astype(jnp.bfloat16), "seq", scatter_dimension=0, tiled=True
        ).astype(jnp.float32),
        lax.psum_scatter(
            grad_down.astype(jnp.bfloat16), "seq", scatter_dimension=0, tiled=True
        ).astype(jnp.float32),
        lax.psum_scatter(
            grad_gain_one.astype(jnp.bfloat16), "seq", scatter_dimension=0, tiled=True
        ).astype(jnp.float32),
        lax.psum_scatter(
            grad_gain_two.astype(jnp.bfloat16), "seq", scatter_dimension=0, tiled=True
        ).astype(jnp.float32),
        lax.psum_scatter(
            grad_table.astype(jnp.bfloat16), "seq", scatter_dimension=0, tiled=True
        ).astype(jnp.float32),
    )
    totals = (
        lax.psum(shards[0].astype(jnp.bfloat16), "dp").astype(jnp.float32),
        lax.psum(shards[1].astype(jnp.bfloat16), "dp").astype(jnp.float32),
        lax.psum(shards[2].astype(jnp.bfloat16), "dp").astype(jnp.float32),
        lax.psum(shards[3].astype(jnp.bfloat16), "dp").astype(jnp.float32),
        lax.psum(shards[4].astype(jnp.bfloat16), "dp").astype(jnp.float32),
        lax.psum(shards[5].astype(jnp.bfloat16), "dp").astype(jnp.float32),
        lax.psum(shards[6].astype(jnp.bfloat16), "dp").astype(jnp.float32),
        lax.psum(shards[7].astype(jnp.bfloat16), "dp").astype(jnp.float32),
        lax.psum(shards[8].astype(jnp.bfloat16), "dp").astype(jnp.float32),
    )
    return (
        pooled,
        grad_input,
        totals[0],
        totals[1],
        totals[2],
        totals[3],
        totals[4],
        totals[5],
        totals[6],
        totals[7],
        totals[8],
    )


def solution(mesh):
    in_specs = (
        P("dp", "seq", None),
        P("seq", None),
        P("seq", None),
        P("seq", None),
        P("seq", None),
        P("seq", None),
        P("seq", None),
        P("seq"),
        P("seq"),
        P("seq", None),
        P("dp"),
        P("dp", "seq", None),
    )
    out_specs = (
        P("dp", None),
        P("dp", "seq", None),
        P("seq", None),
        P("seq", None),
        P("seq", None),
        P("seq", None),
        P("seq", None),
        P("seq", None),
        P("seq"),
        P("seq"),
        P("seq", None),
    )
    return jax.shard_map(
        on_device, mesh=mesh, in_specs=in_specs, out_specs=out_specs, check_vma=False
    )
```

profile of v0, /device:TPU:0, one launch (start us, length us, event | category | flops | bytes accessed | tf_op | source)
XLA Modules:
  0.0 839.5 jit_solution(7142781641178754827)
XLA Ops:
  13.1 11.4 %all-reduce.8 = (bf16[768]{0:T(1024)(128)(2,1)S(1)}, bf16[768]{0:T(1024)(128)(2,1)S(1)}) all-reduce(bf16[768]{0:T(1024)(128)(2,1)S(1)} %dynamic-update-slice, bf16[768]{0:T(1024)(128)(2,1)S(1)} %dynamic-update-slice.1), channel_id=1, replica_groups=mesh['dp'=8,'seq'=4] {'seq'}, use_global_device_ids=true, to_apply=%add | all-reduce | flops 1536 | bytes 6144
  28.5 11.8 %all-gather.15.cloned.1.call-done = bf16[768,768]{1,0:T(8,128)(2,1)} async-done(((bf16[192,768]{1,0:T(8,128)(2,1)}), bf16[768,768]{1,0:T(8,128)(2,1)}) %all-gather.15.cloned.1.call-update) | async-done | bytes 1179664 | tf_op jit(solution)/shard_map/all_gather | solution.py:75
  43.3 26.6 %all-gather.9.cloned.1.call-done = bf16[768,768]{1,0:T(8,128)(2,1)} async-done(((bf16[192,768]{1,0:T(8,128)(2,1)}), bf16[768,768]{1,0:T(8,128)(2,1)}) %all-gather.9.cloned.1.call-update) | async-done | bytes 1179664 | tf_op jit(solution)/shard_map/all_gather | solution.py:76
  92.4 46.5 %copy.55 = pred[256,1024,32]{1,2,0:T(32,128)(4,1)} copy(pred[256,1024,32]{0,2,1:T(32,128)(4,1)} %iota_compare_fusion) | data formatting | bytes 16777216 | tf_op jit(solution)/shard_map/eq | solution.py:100
  138.9 13.1 %convolution_bitcast_fusion = f32[12,256,1024]{2,0,1:T(8,128)} fusion(pred[256,1024,32]{1,2,0:T(32,128)(4,1)} %copy.55, bf16[32,12]{1,0:T(8,128)(2,1)S(1)} %all_gather.47), kind=kOutput, calls=%fused_computation.12 | convolution fusion | flops 201326592 | bytes 20972288 | tf_op jit(solution)/shard_map/qkn,nh->hqk/dot_general | solution.py:101
  152.0 18.3 %copy.56 = f32[12,256,1024]{2,1,0:T(8,128)} copy(f32[12,256,1024]{2,0,1:T(8,128)} %convolution_bitcast_fusion) | data formatting | bytes 25165824 | tf_op jit(solution)/shard_map/qkn,nh->hqk/dot_general | solution.py:101
  177.1 14.8 %fusion = (f32[2,12,256]{2,1,0:T(8,128)S(1)}, f32[2,12,256,1024]{3,2,1,0:T(8,128)}) fusion(f32[12,256,1024]{2,1,0:T(8,128)} %copy.56, pred[2,1024]{1,0:T(4,128)(4,1)S(1)} %iota_compare_fusion.1, bf16[2,1024,12,64]{1,3,2,0:T(8,128)(2,1)S(1)} %bitcast.122, bf16[2,256,12,64]{1,0,3,2:T(2,128)(2,1)} %reshape.250), kind=kOutput, calls=%fused_computation.7 | convolution fusion | flops 824174592 | bytes 41707520 | tf_op jit(solution)/shard_map/bqhe,bkhe->bhqk/dot_general | solution.py:121
  195.3 14.3 %exponential_reduce_fusion = f32[2,12,256]{2,1,0:T(8,128)S(1)} fusion(f32[2,12,256,1024]{3,2,1,0:T(8,128)} %get-tuple-element.38, f32[2,12,256]{2,1,0:T(8,128)S(1)} %get-tuple-element.37, f32[12,256,1024]{2,1,0:T(8,128)} %copy.56, pred[2,1024]{1,0:T(4,128)(4,1)S(1)} %iota_compare_fusion.1), kind=kLoop, calls=%fused_computation.5 | loop fusion | flops 25159680 | bytes 37799936 | tf_op jit(solution)/shard_map/reduce_sum | solution.py:129
  214.8 12.5 %fusion.1 = bf16[2,12,256,1024]{3,2,1,0:T(8,128)(2,1)} fusion(f32[2,12,256,1024]{3,2,1,0:T(8,128)S(1)} %copy-done, f32[2,12,256]{2,1,0:T(8,128)S(1)} %log_add_fusion, f32[12,256,1024]{2,1,0:T(8,128)} %copy.56, pred[2,1024]{1,0:T(4,128)(4,1)S(1)} %iota_compare_fusion.1), kind=kLoop, calls=%fused_computation.8 | loop fusion | flops 25165824 | bytes 50358272 | tf_op jit(solution)/shard_map/convert_element_type | solution.py:130
  242.2 38.3 %all-gather.21.cloned.1.call-done = bf16[768,3072]{1,0:T(8,128)(2,1)} async-done(((bf16[192,3072]{1,0:T(8,128)(2,1)}), bf16[768,3072]{1,0:T(8,128)(2,1)}) %all-gather.21.cloned.1.call-update) | async-done | bytes 4718608 | tf_op jit(solution)/shard_map/all_gather | solution.py:78
  288.7 50.7 %all-gather.23.cloned.1.call-done = bf16[3072,768]{1,0:T(8,128)(2,1)} async-done(((bf16[768,768]{1,0:T(8,128)(2,1)}), bf16[3072,768]{1,0:T(8,128)(2,1)}) %all-gather.23.cloned.1.call-update) | async-done | bytes 4718608 | tf_op jit(solution)/shard_map/all_gather | solution.py:79
  379.3 23.2 %multiply_reduce_fusion = (f32[2,12,256]{2,1,0:T(8,128)S(1)}, f32[2,12,256,1024]{3,2,1,0:T(8,128)}) fusion(f32[2,12,256,1024]{3,2,1,0:T(8,128)} %get-tuple-element.38, f32[2,12,256]{2,1,0:T(8,128)S(1)} %log_add_fusion, f32[12,256,1024]{2,1,0:T(8,128)} %copy.56, pred[2,1024]{1,0:T(4,128)(4,1)S(1)} %iota_compare_fusion.1, ...), kind=kOutput, calls=%fused_computation.3 | convolution fusion | flops 836757504 | bytes 66897920 | tf_op jit(solution)/shard_map/bqhe,bkhe->bhqk/dot_general | solution.py:178
  402.5 30.5 %convert_reduce_fusion = (bf16[12,256,1024]{2,1,0:T(8,128)(2,1)}, bf16[2,12,256,1024]{3,2,1,0:T(8,128)(2,1)}) fusion(f32[2,12,256,1024]{3,2,1,0:T(8,128)} %get-tuple-element.43, f32[2,12,256]{2,1,0:T(8,128)S(1)} %get-tuple-element.42, f32[2,12,256]{2,1,0:T(8,128)S(1)} %log_add_fusion, f32[2,12,256,1024]{3,2,1,0:T(8,128)} %get-tuple-element.38, ...), kind=kLoop, calls=%fused_computation.1 | loop fusion | flops 47185920 | bytes 81840128 | tf_op jit(solution)/shard_map/bhqk,qkn->nh/reduce_sum | solution.py:193
  463.7 23.2 %reduce-scatter.9.cloned.1.call-done = bf16[2,256,768]{2,1,0:T(8,128)(2,1)} async-done(((bf16[2,1024,768]{2,1,0:T(8,128)(2,1)}), bf16[2,256,768]{2,1,0:T(8,128)(2,1)}) %reduce-scatter.9.cloned.1.call-update) | async-done | bytes 786448 | tf_op jit(solution)/shard_map/reduce_scatter | solution.py:201
  508.0 12.2 %copy.67 = bf16[12,256,1024]{1,0,2:T(8,128)(2,1)} copy(bf16[12,256,1024]{2,1,0:T(8,128)(2,1)} %get-tuple-element.29) | data formatting | bytes 12582912 | tf_op jit(solution)/shard_map/bhqk,qkn->nh/reduce_sum | solution.py:193
  520.2 9.3 %psum.70 = f32[2,768]{1,0:T(2,128)S(1)} all-reduce(f32[2,768]{1,0:T(2,128)S(1)} %get-tuple-element.34), channel_id=1, replica_groups=mesh['dp'=8,'seq'=4] {'seq'}, use_global_device_ids=true, to_apply=%region_5.6 | all-reduce | flops 1536 | bytes 12288 | tf_op jit(solution)/shard_map/psum | solution.py:145
  536.4 13.9 %reduce-scatter.13.cloned.1.call-done = bf16[192,768]{1,0:T(8,128)(2,1)} async-done(((bf16[768,768]{1,0:T(8,128)(2,1)}), bf16[192,768]{1,0:T(8,128)(2,1)}) %reduce-scatter.13.cloned.1.call-update) | async-done | bytes 294928 | tf_op jit(solution)/shard_map/reduce_scatter | solution.py:221
  550.3 31.5 %reduce-scatter.17.cloned.1.call-done = bf16[192,768]{1,0:T(8,128)(2,1)} async-done(((bf16[768,768]{1,0:T(8,128)(2,1)}), bf16[192,768]{1,0:T(8,128)(2,1)}) %reduce-scatter.17.cloned.1.call-update) | async-done | bytes 294928 | tf_op jit(solution)/shard_map/reduce_scatter | solution.py:227
  581.8 31.3 %reduce-scatter.15.cloned.1.call-done = bf16[192,768]{1,0:T(8,128)(2,1)} async-done(((bf16[768,768]{1,0:T(8,128)(2,1)}), bf16[192,768]{1,0:T(8,128)(2,1)}) %reduce-scatter.15.cloned.1.call-update) | async-done | bytes 294928 | tf_op jit(solution)/shard_map/reduce_scatter | solution.py:224
  613.1 59.9 %reduce-scatter.23.cloned.1.call-done = bf16[768,768]{1,0:T(8,128)(2,1)} async-done(((bf16[3072,768]{1,0:T(8,128)(2,1)}), bf16[768,768]{1,0:T(8,128)(2,1)}) %reduce-scatter.23.cloned.1.call-update) | async-done | bytes 1179664 | tf_op jit(solution)/shard_map/reduce_scatter | solution.py:236
  673.0 60.0 %reduce-scatter.21.cloned.1.call-done = bf16[192,3072]{1,0:T(8,128)(2,1)} async-done(((bf16[768,3072]{1,0:T(8,128)(2,1)}), bf16[192,3072]{1,0:T(8,128)(2,1)}) %reduce-scatter.21.cloned.1.call-update) | async-done | bytes 1179664 | tf_op jit(solution)/shard_map/reduce_scatter | solution.py:233
  739.2 15.0 %all-reduce.7 = (bf16[768]{0:T(1024)(128)(2,1)S(1)}, bf16[768]{0:T(1024)(128)(2,1)S(1)}, bf16[32,12]{1,0:T(8,128)(2,1)S(1)}) all-reduce(bf16[768]{0:T(1024)(128)(2,1)S(1)} %get-tuple-element.13, bf16[768]{0:T(1024)(128)(2,1)S(1)} %get-tuple-element.11, bf16[32,12]{1,0:T(8,128)(2,1)S(1)} %fusion.32), channel_id=10, replica_groups=mesh['dp'=8,'seq'=4] {'seq'}, use_global_device_ids=true, to_apply=%region_24.25.clone | all-reduce | flops 1920 | bytes 7680
  754.3 14.6 %all-reduce.5 = (bf16[192]{0:T(256)(128)(2,1)S(1)}, bf16[192]{0:T(256)(128)(2,1)S(1)}, bf16[8,12]{1,0:T(8,128)(2,1)S(1)}) all-reduce(bf16[192]{0:T(256)(128)(2,1)S(1)} %dynamic-slice.3, bf16[192]{0:T(256)(128)(2,1)S(1)} %dynamic-slice.5, bf16[8,12]{1,0:T(8,128)(2,1)S(1)} %constant_dynamic-slice_fusion), channel_id=1, replica_groups=mesh['dp'=8,'seq'=4] {'dp'}, use_global_device_ids=true, to_apply=%region_25.26 | all-reduce | flops 480 | bytes 1920 | tf_op jit(solution)/shard_map/psum | solution.py:256
  773.8 48.3 %all-reduce.11.cloned.1.call-done = (bf16[192,768]{1,0:T(8,128)(2,1)}, bf16[192,768]{1,0:T(8,128)(2,1)}, bf16[192,768]{1,0:T(8,128)(2,1)}, bf16[192,768]{1,0:T(8...) async-done(((bf16[192,768]{1,0:T(8,128)(2,1)}, bf16[192,768]{1,0:T(8,128)(2,1)}, bf16[192,768]{1,0:T(8,128)(2,1)}, bf16[192,768]{1,0:T(8,128)(2,1)}, ...) | async-done | bytes 3538960 | tf_op jit(solution)/shard_map/psum | solution.py:250
  (185 shorter events, 191.7 us)
Async XLA Ops:
  7.2 33.1 %all-gather.15.cloned.1.call-start = ((), (), s32[]{:S(2)}) async-start(), calls=%async_computation.11 | async-start | bytes 1474560 | tf_op jit(solution)/shard_map/all_gather | solution.py:75
  7.9 62.0 %all-gather.9.cloned.1.call-start = ((), (), s32[]{:S(2)}) async-start(), calls=%async_computation.8 | async-start | bytes 1474560 | tf_op jit(solution)/shard_map/all_gather | solution.py:76
  8.7 161.6 %all-gather.13.cloned.1.call-start = ((), (), s32[]{:S(2)}) async-start(), calls=%async_computation.10 | async-start | bytes 1474560 | tf_op jit(solution)/shard_map/all_gather | solution.py:74
  9.4 164.5 %all-gather.17.cloned.1.call-start = ((), (), s32[]{:S(2)}) async-start(), calls=%async_computation.12 | async-start | bytes 3932160 | tf_op jit(solution)/shard_map/all_gather | solution.py:118
  43.3 31.7 %copy-start.27 = (s32[2]{0:T(128)S(1)}, s32[2]{0:T(128)}, u32[]{:S(2)}) copy-start(s32[2]{0:T(128)} %param.22) | copy-start | bytes 28
  43.3 148.8 %all-gather.11.cloned.1.call-start = ((), (), s32[]{:S(2)}) async-start(), calls=%async_computation.9 | async-start | bytes 3932160 | tf_op jit(solution)/shard_map/all_gather | solution.py:119
  72.9 165.6 %all-gather.19.cloned.1.call-start = ((), (), s32[]{:S(2)}) async-start(), calls=%async_computation.13 | async-start | bytes 1474560 | tf_op jit(solution)/shard_map/all_gather | solution.py:77
  73.4 207.0 %all-gather.21.cloned.1.call-start = ((), (), s32[]{:S(2)}) async-start(), calls=%async_computation.14 | async-start | bytes 5898240 | tf_op jit(solution)/shard_map/all_gather | solution.py:78
  74.2 265.2 %all-gather.23.cloned.1.call-start = ((), (), s32[]{:S(2)}) async-start(), calls=%async_computation.15 | async-start | bytes 5898240 | tf_op jit(solution)/shard_map/all_gather | solution.py:79
  74.9 385.4 %reduce-scatter.11.cloned.1.call-start = ((), (), s32[]{:S(2)}) async-start(), calls=%async_computation.17 | async-start | bytes 3932160 | tf_op jit(solution)/shard_map/reduce_scatter | solution.py:204
  195.3 19.5 %copy-start = (f32[2,12,256,1024]{3,2,1,0:T(8,128)S(1)}, f32[2,12,256,1024]{3,2,1,0:T(8,128)}, u32[]{:S(2)}) copy-start(f32[2,12,256,1024]{3,2,1,0:T(8,128)} %get-tuple-element.38) | copy-start | bytes 75497472
  379.3 107.6 %reduce-scatter.9.cloned.1.call-start = ((), (), s32[]{:S(2)}) async-start(), calls=%async_computation.16 | async-start | bytes 3932160 | tf_op jit(solution)/shard_map/reduce_scatter | solution.py:201
  402.5 30.5 %copy-start.9 = (bf16[2,256,12,64]{1,0,3,2:T(2,128)(2,1)S(1)}, bf16[2,256,12,64]{1,0,3,2:T(2,128)(2,1)}, u32[]{:S(2)}) copy-start(bf16[2,256,12,64]{1,0,3,2:T(2,128)(2,1)} %reshape.250) | copy-start | bytes 2359300
  442.8 93.7 %reduce-scatter.19.cloned.1.call-start = ((), (), s32[]{:S(2)}) async-start(), calls=%async_computation.21 | async-start | bytes 1474560 | tf_op jit(solution)/shard_map/reduce_scatter | solution.py:230
  446.4 103.8 %reduce-scatter.13.cloned.1.call-start = ((), (), s32[]{:S(2)}) async-start(), calls=%async_computation.18 | async-start | bytes 1474560 | tf_op jit(solution)/shard_map/reduce_scatter | solution.py:221
  460.2 26.7 %copy-start.18 = (bf16[2,256,768]{2,1,0:T(8,128)(2,1)S(1)}, bf16[2,256,768]{2,1,0:T(8,128)(2,1)}, u32[]{:S(2)}) copy-start(bf16[2,256,768]{2,1,0:T(8,128)(2,1)} %copy-done.17) | copy-start | bytes 2359300
  460.2 121.5 %reduce-scatter.17.cloned.1.call-start = ((), (), s32[]{:S(2)}) async-start(), calls=%async_computation.20 | async-start | bytes 1474560 | tf_op jit(solution)/shard_map/reduce_scatter | solution.py:227
  463.6 26.3 %copy-start.20 = (bf16[512,768]{1,0:T(8,128)(2,1)S(1)}, bf16[512,768]{1,0:T(8,128)(2,1)}, u32[]{:S(2)}) copy-start(bf16[512,768]{1,0:T(8,128)(2,1)} %copy-done.19) | copy-start | bytes 2359300
  463.6 149.5 %reduce-scatter.15.cloned.1.call-start = ((), (), s32[]{:S(2)}) async-start(), calls=%async_computation.19 | async-start | bytes 1474560 | tf_op jit(solution)/shard_map/reduce_scatter | solution.py:224
  489.8 183.2 %reduce-scatter.23.cloned.1.call-start = ((), (), s32[]{:S(2)}) async-start(), calls=%async_computation.23 | async-start | bytes 5898240 | tf_op jit(solution)/shard_map/reduce_scatter | solution.py:236
  498.2 234.8 %reduce-scatter.21.cloned.1.call-start = ((), (), s32[]{:S(2)}) async-start(), calls=%async_computation.22 | async-start | bytes 5898240 | tf_op jit(solution)/shard_map/reduce_scatter | solution.py:233
  506.1 316.0 %all-reduce.11.cloned.1.call-start = ((), (), s32[]{:S(2)}) async-start(), calls=%async_computation.24 | async-start | bytes 7077888 | tf_op jit(solution)/shard_map/psum | solution.py:250
  508.0 21.5 %copy-start.12 = (s32[256,1024]{0,1:T(8,128)S(1)}, s32[256,1024]{0,1:T(8,128)}, u32[]{:S(2)}) copy-start(s32[256,1024]{0,1:T(8,128)} %copy-done.11) | copy-start | bytes 3145732
  736.9 33.8 %copy-start.6 = (f32[512,768]{1,0:T(8,128)S(1)}, f32[512,768]{1,0:T(8,128)}, u32[]{:S(2)}) copy-start(f32[512,768]{1,0:T(8,128)} %copy-done.5) | copy-start | bytes 4718596
  (28 other events, 142.9 us)
Sparse Core Ops, SparseCore 0:
  9.8 30.4 all-gather.14
  42.1 27.7 all-gather.8
  71.7 27.7 all-gather.12
  101.8 43.9 all-gather.16
  148.1 43.9 all-gather.10
  193.8 27.7 all-gather.18
  223.4 57.0 all-gather.20
  282.3 57.0 all-gather.22
  379.4 43.9 reduce-scatter.10
  442.8 43.9 reduce-scatter.8
  489.8 28.5 reduce-scatter.18
  521.7 28.5 reduce-scatter.12
  553.2 28.5 reduce-scatter.16
  584.5 28.5 reduce-scatter.14
  615.9 57.0 reduce-scatter.22
  675.9 57.0 reduce-scatter.20
  735.7 86.2 all-reduce.10
where the time goes:
time: 845 us; the launch traced here: 840 us
  waiting for transfers between devices  400 us (47%)
  matrix products  163 us (19%)
  local copies, waits for them, and re-layouts  112 us (13%)
  other arithmetic  87.8 us (10%)
  blocking collectives  58.6 us (7%)
  between operations  16.7 us (2%)
    reduce_scatter x1, waiting for transfers between devices, on_device(): lax.psum_scatter(grad_in.astype(jnp.bfloat16), 'seq', scatter_dimension=0...  60 us
    reduce_scatter x1, waiting for transfers between devices, on_device(): lax.psum_scatter(grad_down.astype(jnp.bfloat16), 'seq', scatter_dimension...  59.9 us
    all_gather x1, waiting for transfers between devices, on_device(): lax.all_gather(w_ffn_out, 'seq', axis=0, tiled=True)  50.7 us
    psum x1, waiting for transfers between devices, on_device(): lax.psum(shards[0].astype(jnp.bfloat16), 'dp').astype(jnp.float32)  48.3 us
    eq x1, local copies, waits for them, and re-layouts, on_device(): bucket_ids(query_pos, key_pos)[:, :, None] == bucket_range  46.5 us
    all_gather x1, waiting for transfers between devices, on_device(): lax.all_gather(w_ffn_in, 'seq', axis=0, tiled=True)  38.3 us
    reduce_scatter x1, waiting for transfers between devices, on_device(): lax.psum_scatter(grad_value_w.astype(jnp.bfloat16), 'seq', scatter_dimens...  31.5 us
    reduce_scatter x1, waiting for transfers between devices, on_device(): lax.psum_scatter(grad_key_w.astype(jnp.bfloat16), 'seq', scatter_dimensio...  31.3 us
  transfers between devices with their start and end apart: 17, of which 12 were waited for; matrix products, arithmetic and copies ran while one was open for 36% of the time, Pallas kernels for 0%

commit v1 on v0

--- a/solution.py
+++ b/solution.py
@@ -3,6 +3,8 @@
 import jax
 import jax.numpy as jnp
 from jax import lax
+from jax.experimental import pallas as pl
+from jax.experimental.pallas import tpu as pltpu
 from jax.sharding import PartitionSpec as P
 
 EPS = 1e-06
@@ -49,6 +51,1029 @@
         grad_scaled * source, -1, keepdims=True
     )
     return (grad_gain, grad_source)
+
+
+SEQ, CORES, DEPTH = 4, 2, 4
+BLK = 128
+MESH = pl.DeviceIdType.MESH
+F32 = jnp.float32
+BF16 = jnp.bfloat16
+
+
+VMEM_LIMIT = 60 << 20
+
+
+def contract(left, right, left_dim, right_dim):
+    return lax.dot_general(
+        left, right, (((left_dim,), (right_dim,)), ((), ())), preferred_element_type=F32
+    )
+
+
+def await_copy(ref, sem):
+    pltpu.make_async_copy(ref, ref, sem).wait()
+
+
+def tile(index, size):
+    return pl.ds(pl.multiple_of(index * size, size), size)
+
+
+def bucket_of(offset):
+    distance = jnp.abs(offset)
+    beyond = jnp.full(distance.shape, 8, jnp.int32)
+    for threshold in THRESHOLDS:
+        beyond = beyond + (distance >= threshold).astype(jnp.int32)
+    return jnp.where(offset > 0, 16, 0) + jnp.where(distance < 8, distance, beyond)
+
+
+def full_sum(value):
+    return jnp.sum(jnp.sum(value, 0, keepdims=True), 1, keepdims=True)
+
+
+def fused_kernel(
+    inputs,
+    cotangent,
+    w_query,
+    w_key,
+    w_value,
+    w_out,
+    w_in,
+    w_down,
+    small,
+    pooled_o,
+    gx_o,
+    gq_o,
+    gk_o,
+    gv_o,
+    go_o,
+    gi_o,
+    gd_o,
+    gs_o,
+    xown,
+    grads,
+    nrm1,
+    wqkv,
+    qkv,
+    mixed,
+    wo,
+    psend,
+    precv,
+    hid,
+    nrm2,
+    wi,
+    wd,
+    act,
+    gpre,
+    gn,
+    strip,
+    vecs,
+    maskc,
+    lse,
+    flip,
+    dqkv,
+    gmix,
+    dk_acc,
+    dv_acc,
+    ds_buf,
+    near,
+    far,
+    gqkv,
+    rs_d,
+    rs_i,
+    rs_o,
+    rs_q,
+    za_d,
+    za_i,
+    za_o,
+    za_q,
+    zb_d,
+    zb_i,
+    zb_o,
+    zb_q,
+    zc_d,
+    zc_i,
+    zc_o,
+    zc_q,
+    gx_send,
+    gx_recv,
+    small_all,
+    gains,
+    asum,
+    pp,
+    pool_recv,
+    sg,
+    sg_plane,
+    sg_depth,
+    small_ss,
+    small_rs,
+    x_ss,
+    x_rs,
+    c_ss,
+    c_rs,
+    wqkv_ss,
+    wqkv_rs,
+    wo_ss,
+    wo_rs,
+    wi_ss,
+    wi_rs,
+    wd_ss,
+    wd_rs,
+    n1_ss,
+    n1_rs,
+    g_ss,
+    g_rs,
+    part_ss,
+    part_rs,
+    n2_ss,
+    n2_rs,
+    gn2_ss,
+    gn2_rs,
+    gat_ss,
+    gat_rs,
+    gn1_ss,
+    gn1_rs,
+    gx_ss,
+    gx_rs,
+    rsd_ss,
+    rsd_rs,
+    rsi_ss,
+    rsi_rs,
+    rso_ss,
+    rso_rs,
+    rsq_ss,
+    rsq_rs,
+    z_ss,
+    z_rs,
+    pool_ss,
+    pool_rs,
+    sgp_ss,
+    sgp_rs,
+    sgz_ss,
+    sgz_rs,
+    out_ss,
+):
+    dp = lax.axis_index("dp")
+    chip = lax.axis_index("seq")
+    depth, core = lax.div(dp, 2), lax.rem(dp, 2)
+    row, col = lax.div(chip, 2), lax.rem(chip, 2)
+    other = (depth * 2 + 1 - core, chip)
+    tokens, width = nrm1.shape
+    half = width // 2
+    rows_w = w_query.shape[0]
+    ff_part = act.shape[1]
+
+    def remote(src, dst, send, recv, device):
+        return pltpu.make_async_remote_copy(
+            src_ref=src,
+            dst_ref=dst,
+            send_sem=send,
+            recv_sem=recv,
+            device_id=device,
+            device_id_type=MESH,
+        )
+
+    def ahead(step):
+        return lax.rem(chip + step, SEQ)
+
+    pending = []
+
+    barrier = pltpu.get_barrier_semaphore()
+    for step in range(SEQ):
+        if step:
+            pl.semaphore_signal(barrier, inc=1, device_id=(dp, ahead(step)), device_id_type=MESH)
+        pl.semaphore_signal(
+            barrier, inc=1, device_id=(other[0], ahead(step)), device_id_type=MESH
+        )
+    for step in range(1, DEPTH):
+        pl.semaphore_signal(
+            barrier,
+            inc=1,
+            device_id=(lax.rem(depth + step, DEPTH) * 2 + core, chip),
+            device_id_type=MESH,
+        )
+    pl.semaphore_wait(barrier, 2 * SEQ - 1 + DEPTH - 1)
+
+    local = pltpu.make_async_copy(small, small_all.at[0], small_rs.at[0])
+    local.start()
+    for step in range(1, SEQ):
+        copy = remote(
+            small, small_all.at[step], small_ss.at[step], small_rs.at[step], (dp, ahead(step))
+        )
+        copy.start()
+        pending.append(copy)
+    copy = remote(small, small_all.at[SEQ], small_ss.at[SEQ], small_rs.at[SEQ], other)
+    copy.start()
+    pending.append(copy)
+
+    def spread(source, dest_of, send, recv):
+        for doc in range(2):
+            for to in range(2):
+                block = source.at[doc, pl.ds(to * BLK, BLK)]
+                target = core * 2 + doc
+                own = (target == chip) & (core == to)
+
+                @pl.when(own)
+                def _():
+                    pltpu.make_async_copy(block, dest_of(), recv.at[chip]).start()
+
+                @pl.when(jnp.logical_not(own))
+                def _():
+                    remote(
+                        block,
+                        dest_of(),
+                        send.at[doc * 2 + to],
+                        recv.at[chip],
+                        (depth * 2 + to, target),
+                    ).start()
+
+    def spread_done(source, dest_of, send, recv):
+        for doc in range(2):
+            for to in range(2):
+                block = source.at[doc, pl.ds(to * BLK, BLK)]
+                target = core * 2 + doc
+
+                @pl.when(jnp.logical_not((target == chip) & (core == to)))
+                def _():
+                    remote(
+                        block,
+                        dest_of(),
+                        send.at[doc * 2 + to],
+                        recv.at[chip],
+                        (depth * 2 + to, target),
+                    ).wait_send()
+
+    x_slot = lambda: xown.at[chip]
+    spread(inputs, x_slot, x_ss, x_rs)
+
+    def gather(src, dst, send, recv):
+        pltpu.make_async_copy(src, dst, recv.at[0]).start()
+        for step in range(1, SEQ):
+            copy = remote(src, dst, send.at[step], recv.at[step], (dp, ahead(step)))
+            copy.start()
+            pending.append(copy)
+
+    own_rows = tile(chip, rows_w)
+    core_cols = tile(core, half)
+    for i, w in enumerate((w_query, w_key, w_value)):
+        gather(
+            w.at[:, core_cols],
+            wqkv.at[own_rows, pl.ds(i * half, half)],
+            wqkv_ss.at[i],
+            wqkv_rs.at[i],
+        )
+
+    wo_part = rows_w // 2
+    wo_src = w_out.at[tile(core, wo_part)]
+    wo_dst = wo.at[tile(col * 2 + core, wo_part)]
+
+    def wo_each(action):
+        for to in range(SEQ):
+            own = (chip == to) & (core == row)
+            copy = remote(
+                wo_src, wo_dst, wo_ss.at[to], wo_rs.at[col * 2 + core], (depth * 2 + row, to)
+            )
+            if action == "start":
+
+                @pl.when(own)
+                def _():
+                    pltpu.make_async_copy(wo_src, wo_dst, wo_rs.at[col * 2 + core]).start()
+
+            @pl.when(jnp.logical_not(own))
+            def _():
+                if action == "start":
+                    copy.start()
+                else:
+                    copy.wait_send()
+
+    wo_each("start")
+    for f in range(SEQ):
+        gather(
+            w_in.at[:, tile(f * 2 + core, ff_part)],
+            wi.at[own_rows, pl.ds(f * ff_part, ff_part)],
+            wi_ss.at[f],
+            wi_rs.at[f],
+        )
+    c_slot = lambda: grads.at[chip * 2 + core]
+    for doc in range(2):
+        for to in range(2):
+            block = cotangent.at[doc, pl.ds(to * BLK, BLK)]
+            target = core * 2 + doc
+            own = (target == chip) & (core == to)
+
+            @pl.when(own)
+            def _():
+                pltpu.make_async_copy(block, grads.at[chip * 2 + to], c_rs.at[chip]).start()
+
+            @pl.when(jnp.logical_not(own))
+            def _():
+                remote(
+                    block,
+                    grads.at[chip * 2 + to],
+                    c_ss.at[doc * 2 + to],
+                    c_rs.at[chip],
+                    (depth * 2 + to, target),
+                ).start()
+
+    gather(w_down.at[tile(core, ff_part)], wd.at[tile(chip, ff_part)], wd_ss, wd_rs)
+
+    for step in range(SEQ + 1):
+        await_copy(small_all.at[step], small_rs.at[step])
+    summed = small_all[0] + small_all[1] + small_all[2] + small_all[3]
+    for which in range(2):
+        gains[which : which + 1, :] = jnp.concatenate(
+            [summed[8 * which + i : 8 * which + i + 1, :] for i in range(width // BLK)], axis=1
+        )
+    length_row = jnp.where(row == core, small_all[0, 6:7, :], small_all[SEQ, 6:7, :])
+    length = jnp.where(col == 0, length_row[:, 0:1], length_row[:, 1:2])
+    own_lengths = small_all[0, 6:7, 0:2]
+    table = summed[16:48, :].astype(BF16)
+    lane = lax.broadcasted_iota(jnp.int32, (1, 2 * BLK), 1)
+    minus = jnp.where(lane < BLK, lane, lane - 2 * BLK)
+    for off in (-1, 0, 1):
+        ids = bucket_of(off * BLK - minus)
+        onehot = (lax.broadcasted_iota(jnp.int32, (32, 2 * BLK), 0) == ids).astype(BF16)
+        vecs[off + 1] = contract(table, onehot, 0, 0)[0:16, :]
+
+    @pl.loop(0, 6)
+    def _(h):
+        values = [vecs[i, pl.ds(core * 6 + h, 1), :] for i in range(3)]
+        left = jnp.broadcast_to(values[0][:, BLK - 1 : BLK], (BLK, BLK))
+        right = jnp.broadcast_to(values[2][:, BLK + 1 : BLK + 2], (BLK, BLK))
+        for i in range(6):
+            strip[h, i * BLK : (i + 1) * BLK, :] = left
+            strip[h, (i + 9) * BLK : (i + 10) * BLK, :] = right
+        for i in range(3):
+            skewed = pltpu.roll(
+                jnp.broadcast_to(values[i], (BLK, 2 * BLK)), 0, 1, stride=1, stride_axis=0
+            )
+            strip[h, (i + 6) * BLK : (i + 7) * BLK, :] = skewed[:, :BLK]
+
+    maskc[...] = jnp.where(
+        lax.broadcasted_iota(jnp.int32, maskc.shape, 0).astype(F32) < length, 0.0, NEGATIVE
+    )
+
+    def block_valid(b):
+        pos = lax.broadcasted_iota(jnp.int32, (BLK, 1), 0) + b * BLK
+        return (pos.astype(F32) < length).astype(F32)
+
+    def n1_copy(i):
+        block = nrm1.at[tile(2 * i + core, BLK)]
+        return remote(block, block, n1_ss.at[i], n1_rs.at[i], other)
+
+    @pl.loop(0, SEQ)
+    def _(i):
+        await_copy(xown.at[i], x_rs.at[i])
+        source = xown[i].astype(F32)
+        scale = lax.rsqrt(jnp.mean(source * source, -1, keepdims=True) + EPS)
+        nrm1[tile(2 * i + core, BLK), :] = (source * scale * gains[0:1, :]).astype(BF16)
+        n1_copy(i).start()
+
+    for i in range(3):
+        for step in range(SEQ):
+            await_copy(wqkv.at[pl.ds(0, rows_w), pl.ds(0, half)], wqkv_rs.at[i, step])
+    for i in range(SEQ):
+        n1_copy(i).wait_recv()
+
+    quarter = tokens // 4
+
+    @pl.loop(0, 4)
+    def _(i):
+        rows = tile(i, quarter)
+        qkv[rows, :] = contract(nrm1[rows, :], wqkv[...], 1, 0).astype(BF16)
+
+    lane_pair = lax.broadcasted_iota(jnp.int32, (1, BLK), 1)
+    flip[BLK : BLK + 16, :] = jnp.ones((16, tokens), BF16)
+
+    def scores(pair, qb, h):
+        keys = qkv[:, tile(3 + pair, BLK)]
+        queries = qkv[tile(qb, quarter), tile(pair, BLK)]
+        queries = jnp.where((lane_pair < 64) == (h == 0), queries, jnp.zeros_like(queries))
+        raw = contract(keys, queries, 1, 1)
+        head = pair * 2 + h
+        biases = [
+            strip[head, pl.ds(pl.multiple_of((7 - 2 * qb - i) * BLK, BLK), tokens), :]
+            + maskc[...]
+            for i in range(2)
+        ]
+        return raw + jnp.concatenate(biases, axis=1), queries
+
+    @pl.loop(0, 3)
+    def _(pair):
+        flip[0:BLK, :] = jnp.transpose(qkv[:, tile(6 + pair, BLK)])
+
+        @pl.loop(0, 4)
+        def _(qb):
+            parts = []
+            for h in range(2):
+                logits, _ = scores(pair, qb, h)
+                highest = jnp.max(logits, 0, keepdims=True)
+                raised = jnp.exp(logits - highest).astype(BF16)
+                result = contract(flip[...], raised, 1, 0)
+                total = result[BLK : BLK + 1, :]
+                lse[pl.ds(pair * 2 + h, 1), tile(qb, quarter)] = highest + jnp.log(total)
+                parts.append(result[64 * h : 64 * h + 64, :] / total)
+            mixed[tile(qb, quarter), tile(pair, BLK)] = jnp.transpose(
+                jnp.concatenate(parts, axis=0)
+            ).astype(BF16)
+
+    def swap_copy(i, send, recv):
+        return remote(psend.at[i], precv.at[i], send.at[i], recv.at[i], other)
+
+    for k in range(4):
+        await_copy(wo.at[pl.ds(k * wo_part, wo_part)], wo_rs.at[k])
+
+    @pl.loop(0, SEQ)
+    def _(i):
+        psend[i] = contract(mixed[tile(2 * i + 1 - core, BLK), :], wo[...], 1, 0)
+        swap_copy(i, part_ss, part_rs).start()
+
+    def n2_copy(i, send, recv):
+        block = nrm2.at[tile(2 * i + core, BLK)]
+        return remote(block, block, send.at[i], recv.at[i], other)
+
+    pp[...] = jnp.zeros_like(pp)
+
+    @pl.loop(0, SEQ)
+    def _(i):
+        hidden = xown[i].astype(F32) + contract(
+            mixed[tile(2 * i + core, BLK), :], wo[...], 1, 0
+        )
+        swap_copy(i, part_ss, part_rs).wait_recv()
+        hidden = hidden + precv[i]
+        hid[i] = hidden
+        scale = lax.rsqrt(jnp.mean(hidden * hidden, -1, keepdims=True) + EPS)
+        nrm2[tile(2 * i + core, BLK), :] = (hidden * scale * gains[1:2, :]).astype(BF16)
+        n2_copy(i, n2_ss, n2_rs).start()
+        pp[0:1, :] += jnp.sum(hidden * block_valid(2 * i + core), 0, keepdims=True)
+
+    def g_copy(i):
+        block = grads.at[2 * i + core]
+        return remote(block, block, g_ss.at[i], g_rs.at[i], other)
+
+    for f in range(SEQ):
+        for step in range(SEQ):
+            await_copy(wi.at[pl.ds(0, rows_w), pl.ds(0, ff_part)], wi_rs.at[f, step])
+
+    @pl.loop(0, SEQ)
+    def _(i):
+        b = 2 * i + core
+        await_copy(grads.at[b], c_rs.at[i])
+        grads[b] = (grads[b].astype(F32) * block_valid(b)).astype(BF16)
+        g_copy(i).start()
+
+    for step in range(SEQ):
+        await_copy(wd.at[pl.ds(0, ff_part)], wd_rs.at[step])
+    for i in range(SEQ):
+        n2_copy(i, n2_ss, n2_rs).wait_recv()
+        g_copy(i).wait_recv()
+
+    def rsd_copy(step):
+        return remote(
+            wd.at[tile(ahead(step), ff_part)],
+            rs_d.at[step - 1],
+            rsd_ss.at[step - 1],
+            rsd_rs.at[step - 1],
+            (dp, ahead(step)),
+        )
+
+    def rsi_copy(part, step):
+        return remote(
+            wi.at[tile(ahead(step), rows_w), tile(part, ff_part)],
+            rs_i.at[step - 1, :, tile(part, ff_part)],
+            rsi_ss.at[part, step - 1],
+            rsi_rs.at[part, step - 1],
+            (dp, ahead(step)),
+        )
+
+    @pl.loop(0, SEQ)
+    def _(turn):
+        f = lax.rem(chip + turn, SEQ)
+        f_cols = tile(f, ff_part)
+        asum[...] = jnp.zeros_like(asum)
+
+        @pl.loop(0, 4)
+        def _(i):
+            rows = tile(i, quarter)
+            value = contract(nrm2[rows, :], wi[:, f_cols], 1, 0)
+            square = value * value
+            tangent = jnp.tanh(GELU_C * (value + GELU_K * value * square))
+            half_up = 0.5 * (1.0 + tangent)
+            active = (value * half_up).astype(BF16)
+            slope = half_up + 0.5 * value * (1.0 - tangent * tangent) * GELU_C * (
+                1.0 + 3.0 * GELU_K * square
+            )
+            upstream = grads[pl.ds(2 * i, 2)].reshape(quarter, width)
+            grad = (contract(upstream, wd[f_cols, :], 1, 1) * slope).astype(BF16)
+            act[rows, :] = active
+            gpre[rows, :] = grad
+            pos = lax.broadcasted_iota(jnp.int32, (8, quarter), 1) + i * quarter
+            valid = (pos.astype(F32) < length).astype(BF16)
+            asum[...] += contract(valid, active, 1, 0)
+            back = contract(grad, wi[:, f_cols], 1, 1)
+
+            @pl.when(turn == 0)
+            def _():
+                gn[rows, :] = back
+
+            @pl.when(turn > 0)
+            def _():
+                gn[rows, :] += back
+
+        total = asum[0:1, :]
+        high = total.astype(BF16)
+        rest = total - high.astype(F32)
+        middle = rest.astype(BF16)
+        low = (rest - middle.astype(F32)).astype(BF16)
+        for piece in (high, middle, low):
+            pp[0:1, :] += contract(
+                jnp.broadcast_to(piece, (16, ff_part)), wd[f_cols, :], 1, 0
+            )[0:1, :]
+
+        @pl.loop(0, ff_part // BLK)
+        def _(i):
+            down = contract(act[:, tile(i, BLK)], grads[...].reshape(tokens, width), 0, 0)
+            wd[pl.ds(pl.multiple_of(f * ff_part + i * BLK, BLK), BLK), :] = down.astype(BF16)
+
+        for step in range(1, SEQ):
+
+            @pl.when(turn == step)
+            def _():
+                rsd_copy(step).start()
+
+        @pl.loop(0, width // BLK)
+        def _(i):
+            wi[tile(i, BLK), f_cols] = contract(nrm2[:, tile(i, BLK)], gpre[...], 0, 0).astype(
+                BF16
+            )
+
+        for step in range(1, SEQ):
+            rsi_copy(f, step).start()
+
+    def pool_each(action):
+        for to in range(SEQ):
+            own = (chip == to) & (core == row)
+            dst = pool_recv.at[col * 2 + core]
+            copy = remote(pp, dst, pool_ss.at[to], pool_rs.at[col * 2 + core], (depth * 2 + row, to))
+            if action == "start":
+
+                @pl.when(own)
+                def _():
+                    pltpu.make_async_copy(pp, dst, pool_rs.at[col * 2 + core]).start()
+
+            @pl.when(jnp.logical_not(own))
+            def _():
+                if action == "start":
+                    copy.start()
+                else:
+                    copy.wait_send()
+
+    pool_each("start")
+
+    for i in range(SEQ):
+        swap_copy(i, part_ss, part_rs).wait_send()
+        n2_copy(i, n2_ss, n2_rs).wait_send()
+
+    @pl.loop(0, SEQ)
+    def _(i):
+        psend[i] = gn[tile(2 * i + 1 - core, BLK), :]
+        swap_copy(i, gn2_ss, gn2_rs).start()
+
+    sg[...] = jnp.zeros_like(sg)
+
+    def add_gain(first, value):
+        for i in range(width // BLK):
+            sg[first + i : first + i + 1, :] += value[:, i * BLK : (i + 1) * BLK]
+
+    @pl.loop(0, SEQ)
+    def _(i):
+        b = 2 * i + core
+        swap_copy(i, gn2_ss, gn2_rs).wait_recv()
+        normed = gn[tile(b, BLK), :] + precv[i]
+        hidden = hid[i]
+        scale = lax.rsqrt(jnp.mean(hidden * hidden, -1, keepdims=True) + EPS)
+        add_gain(8, jnp.sum(normed * hidden * scale, 0, keepdims=True))
+        scaled = normed * gains[1:2, :]
+        inner = jnp.mean(scaled * hidden, -1, keepdims=True)
+        result = grads[b].astype(F32) + scale * scaled - hidden * (scale * scale * scale) * inner
+        hid[i] = result
+        nrm2[tile(b, BLK), :] = result.astype(BF16)
+        n2_copy(i, gat_ss, gat_rs).start()
+
+    for i in range(SEQ):
+        n2_copy(i, gat_ss, gat_rs).wait_recv()
+
+    @pl.loop(0, 4)
+    def _(i):
+        rows = tile(i, quarter)
+        gmix[rows, :] = contract(nrm2[rows, :], wo[...], 1, 1).astype(BF16)
+
+    wo_each("wait")
+
+    @pl.loop(0, half // BLK)
+    def _(i):
+        wo[tile(i, BLK), :] = contract(mixed[:, tile(i, BLK)], nrm2[...], 0, 0).astype(BF16)
+
+    def rso_each(action):
+        for k in range(2):
+            for to in range(2):
+                target = core * 2 + k
+                own = (chip == target) & (core == to)
+                src = wo.at[pl.ds((2 * k + to) * wo_part, wo_part)]
+                dst = rs_o.at[chip]
+                copy = remote(
+                    src, dst, rso_ss.at[2 * k + to], rso_rs.at[chip], (depth * 2 + to, target)
+                )
+                if action == "start":
+
+                    @pl.when(own)
+                    def _():
+                        pltpu.make_async_copy(src, dst, rso_rs.at[chip]).start()
+
+                @pl.when(jnp.logical_not(own))
+                def _():
+                    if action == "start":
+                        copy.start()
+                    else:
+                        copy.wait_send()
+
+    rso_each("start")
+
+    sub = lax.broadcasted_iota(jnp.int32, (16, tokens), 0)
+    key_block = lax.div(lax.broadcasted_iota(jnp.int32, (16, tokens), 1), BLK)
+    flip[BLK : BLK + 16, :] = (sub == key_block).astype(BF16)
+    near[...] = jnp.zeros_like(near)
+    far[...] = jnp.zeros_like(far)
+    ds_buf[0:BLK, :] = jnp.zeros((BLK, quarter), BF16)
+    ds_buf[tokens + BLK :, :] = jnp.zeros((BLK, quarter), BF16)
+
+    def rsq_copy(pair, step):
+        return remote(
+            gqkv.at[pair, tile(ahead(step), rows_w)],
+            rs_q.at[pair, step - 1],
+            rsq_ss.at[pair, step - 1],
+            rsq_rs.at[pair, step - 1],
+            (dp, ahead(step)),
+        )
+
+    @pl.loop(0, 3)
+    def _(pair):
+        flip[0:BLK, :] = jnp.transpose(qkv[:, tile(3 + pair, BLK)])
+        dk_acc[...] = jnp.zeros_like(dk_acc)
+        dv_acc[...] = jnp.zeros_like(dv_acc)
+
+        @pl.loop(0, 4)
+        def _(qb):
+            rows = tile(qb, quarter)
+            cols = tile(pair, BLK)
+            upstream = gmix[rows, cols]
+            product = jnp.transpose(upstream.astype(F32) * mixed[rows, cols].astype(F32))
+            parts = []
+            for h in range(2):
+                head = pair * 2 + h
+                logits, queries = scores(pair, qb, h)
+                probs = jnp.exp(logits - lse[pl.ds(head, 1), rows])
+                masked = jnp.where((lane_pair < 64) == (h == 0), upstream, jnp.zeros_like(upstream))
+                grad_probs = contract(qkv[:, tile(6 + pair, BLK)], masked, 1, 1)
+                inner = jnp.sum(product[64 * h : 64 * h + 64, :], 0, keepdims=True)
+                grad_logits = (probs * (grad_probs - inner)).astype(BF16)
+                dv_acc[...] += contract(probs.astype(BF16), masked, 1, 0)
+                dk_acc[...] += contract(grad_logits, queries, 1, 0)
+                ds_buf[BLK : tokens + BLK, :] = grad_logits
+                result = contract(flip[...], grad_logits, 1, 0)
+                parts.append(result[64 * h : 64 * h + 64, :])
+                sums = result[BLK : BLK + 8, :]
+                block_row = lax.broadcasted_iota(jnp.int32, sums.shape, 0)
+                query_block = 2 * qb + lax.div(
+                    lax.broadcasted_iota(jnp.int32, sums.shape, 1), BLK
+                )
+                gap = block_row - query_block
+                far[head, 0:8, :] += jnp.where(gap <= -2, sums, 0.0)
+                far[head, 8:16, :] += jnp.where(gap >= 2, sums, 0.0)
+                for i in range(2):
+                    for off in range(3):
+                        start = pl.multiple_of((2 * qb + i + off) * BLK, BLK)
+                        near[head * 3 + off] += ds_buf[
+                            pl.ds(start, BLK), i * BLK : (i + 1) * BLK
+                        ].astype(F32)
+            dqkv[rows, cols] = jnp.transpose(jnp.concatenate(parts, axis=0)).astype(BF16)
+
+        dqkv[:, tile(3 + pair, BLK)] = dk_acc[...].astype(BF16)
+        dqkv[:, tile(6 + pair, BLK)] = dv_acc[...].astype(BF16)
+
+        @pl.loop(0, width // BLK)
+        def _(i):
+            source = nrm1[:, tile(i, BLK)]
+            for j in range(3):
+                gqkv[pair, tile(i, BLK), j * BLK : (j + 1) * BLK] = contract(
+                    source, dqkv[:, tile(3 * j + pair, BLK)], 0, 0
+                ).astype(BF16)
+
+        for step in range(1, SEQ):
+            rsq_copy(pair, step).start()
+
+    for i in range(SEQ):
+        swap_copy(i, gn2_ss, gn2_rs).wait_send()
+
+    @pl.loop(0, SEQ)
+    def _(i):
+        psend[i] = contract(dqkv[tile(2 * i + 1 - core, BLK), :], wqkv[...], 1, 1)
+        swap_copy(i, gn1_ss, gn1_rs).start()
+
+    def gx_each(i, action):
+        own = (chip == i) & (core == row)
+        dst = gx_recv.at[col * 2 + core]
+        copy = remote(
+            gx_send.at[i], dst, gx_ss.at[i], gx_rs.at[col * 2 + core], (depth * 2 + row, i)
+        )
+        if action == "start":
+
+            @pl.when(own)
+            def _():
+                pltpu.make_async_copy(gx_send.at[i], dst, gx_rs.at[col * 2 + core]).start()
+
+        @pl.when(jnp.logical_not(own))
+        def _():
+            if action == "start":
+                copy.start()
+            else:
+                copy.wait_send()
+
+    @pl.loop(0, SEQ)
+    def _(i):
+        own = contract(dqkv[tile(2 * i + core, BLK), :], wqkv[...], 1, 1)
+        swap_copy(i, gn1_ss, gn1_rs).wait_recv()
+        normed = own + precv[i]
+        source = xown[i].astype(F32)
+        scale = lax.rsqrt(jnp.mean(source * source, -1, keepdims=True) + EPS)
+        add_gain(0, jnp.sum(normed * source * scale, 0, keepdims=True))
+        scaled = normed * gains[0:1, :]
+        inner = jnp.mean(scaled * source, -1, keepdims=True)
+        result = hid[i] + scale * scaled - source * (scale * scale * scale) * inner
+        gx_send[i] = result.astype(BF16)
+        gx_each(i, "start")
+
+    diag_row = lax.broadcasted_iota(jnp.int32, (BLK, BLK), 0)
+    diag_col = lax.broadcasted_iota(jnp.int32, (BLK, BLK), 1)
+    upper = diag_col >= diag_row
+    mirror = (diag_row + diag_col == BLK - 1).astype(F32)
+    shift = lax.broadcasted_iota(jnp.int32, (1, BLK), 1) + 1
+    shift = jnp.where(shift == BLK, 0, shift)
+    ids = bucket_of(jnp.concatenate([-shift, BLK - shift], axis=1))
+    onehot = (lax.broadcasted_iota(jnp.int32, (BLK, 2 * BLK), 0) == ids).astype(F32)
+    bucket_lane = lax.broadcasted_iota(jnp.int32, (1, BLK), 1)
+
+    @pl.loop(0, 6)
+    def _(h):
+        def skew(x):
+            mirrored = lax.dot_general(
+                mirror,
+                x,
+                (((1,), (0,)), ((), ())),
+                preferred_element_type=F32,
+                precision=lax.Precision.HIGHEST,
+            )
+            return pltpu.roll(mirrored, 0, 1, stride=1, stride_axis=0)
+
+        tiles = [near[h * 3 + i] for i in range(3)]
+        at = [
+            jnp.sum(
+                skew(jnp.where(upper, tiles[i + 1], 0.0) + jnp.where(upper, 0.0, tiles[i])),
+                0,
+                keepdims=True,
+            )
+            for i in range(2)
+        ]
+        below = full_sum(jnp.where(upper, tiles[0], 0.0)) + full_sum(far[h, 0:8, :])
+        above = full_sum(jnp.where(upper, 0.0, tiles[2])) + full_sum(far[h, 8:16, :])
+        sums = lax.dot_general(
+            jnp.broadcast_to(jnp.concatenate(at, axis=1), (8, 2 * BLK)),
+            onehot,
+            (((1,), (1,)), ((), ())),
+            preferred_element_type=F32,
+            precision=lax.Precision.HIGHEST,
+        )[0:1, :]
+        sums = sums + jnp.where(bucket_lane == 15, below, 0.0)
+        sums = sums + jnp.where(bucket_lane == 31, above, 0.0)
+        sg[pl.ds(16 + core * 8 + h, 1), :] = sums
+
+    place = core * SEQ + chip
+
+    def sgp_each(action):
+        for step in range(SEQ):
+            for cross in range(2):
+                if step == 0 and cross == 0:
+                    continue
+                to = ahead(step)
+                to_core = lax.rem(core + cross, 2)
+                copy = remote(
+                    sg,
+                    sg_plane.at[place],
+                    sgp_ss.at[step * 2 + cross],
+                    sgp_rs.at[place],
+                    (depth * 2 + to_core, to),
+                )
+                if action == "start":
+                    copy.start()
+                else:
+                    copy.wait_send()
+
+    sgp_each("start")
+    pltpu.make_async_copy(sg, sg_plane.at[place], sgp_rs.at[place]).start()
+
+    inner_z = (depth == 1) | (depth == 2)
+    end_z = jnp.logical_not(inner_z)
+    toward = jnp.where(depth == 0, 1, 2)
+    outward = jnp.where(depth == 1, 0, 3)
+    across = jnp.where(depth == 1, 2, 1)
+
+    def z_dev(z):
+        return (z * 2 + core, chip)
+
+    items = []
+
+    def item(reduced, za, zb, final, zc):
+        index = len(items)
+        sem = lambda i: (z_ss.at[index, i], z_rs.at[index, i])
+        items.append(
+            dict(
+                reduced=reduced,
+                za=za,
+                zb=zb,
+                final=final,
+                zc=zc,
+                to_inner=remote(reduced, za, *sem(0), z_dev(toward)),
+                swap=remote(reduced, zb, *sem(1), z_dev(across)),
+                to_end=remote(final, final, *sem(2), z_dev(outward)),
+                to_core=remote(final, zc, *sem(3), other),
+            )
+        )
+
+    def stage_first(it):
+        @pl.when(end_z)
+        def _():
+            it["to_inner"].start()
+
+    def stage_second(it):
+        @pl.when(inner_z)
+        def _():
+            it["to_inner"].wait_recv()
+            it["reduced"][...] = (
+                it["reduced"][...].astype(F32) + it["za"][...].astype(F32)
+            ).astype(BF16)
+            it["swap"].start()
+
+    def stage_third(it):
+        @pl.when(inner_z)
+        def _():
+            it["swap"].wait_recv()
+            it["final"][...] = (
+                it["reduced"][...].astype(F32) + it["zb"][...].astype(F32)
+            ).astype(BF16)
+            it["to_end"].start()
+
+    def stage_fourth(it):
+        @pl.when(end_z)
+        def _():
+            it["to_end"].wait_recv()
+
+        it["to_core"].start()
+
+    def add_up(dest, sources):
+        total = sources[0][...].astype(F32)
+        for more in sources[1:]:
+            total = total + more[...].astype(F32)
+        dest[...] = total.astype(BF16)
+
+    for step in range(1, SEQ):
+        rsd_copy(step).wait_recv()
+    own_down = wd.at[tile(chip, ff_part)]
+    add_up(rs_d.at[0], [own_down, rs_d.at[0], rs_d.at[1], rs_d.at[2]])
+    item(rs_d.at[0], za_d, zb_d, rs_d.at[1], zc_d)
+    stage_first(items[0])
+    for part in range(SEQ):
+        for step in range(1, SEQ):
+            rsi_copy(part, step).wait_recv()
+    add_up(rs_i.at[0], [wi.at[tile(chip, rows_w)], rs_i.at[0], rs_i.at[1], rs_i.at[2]])
+    item(rs_i.at[0], za_i, zb_i, rs_i.at[1], zc_i)
+    stage_first(items[1])
+    stage_second(items[0])
+    for i in range(SEQ):
+        await_copy(rs_o.at[i], rso_rs.at[i])
+    add_up(rs_o.at[0], [rs_o.at[0], rs_o.at[1], rs_o.at[2], rs_o.at[3]])
+    item(rs_o.at[0], za_o, zb_o, rs_o.at[1], zc_o)
+    stage_first(items[2])
+    stage_second(items[1])
+    stage_third(items[0])
+    for pair in range(3):
+        for step in range(1, SEQ):
+            rsq_copy(pair, step).wait_recv()
+        q = rs_q.at[pair]
+        add_up(q.at[0], [gqkv.at[pair, tile(chip, rows_w)], q.at[0], q.at[1], q.at[2]])
+        item(q.at[0], za_q.at[pair], zb_q.at[pair], q.at[1], zc_q.at[pair])
+        stage_first(items[3 + pair])
+        stage_second(items[2 + pair])
+        stage_third(items[1 + pair])
+        stage_fourth(items[pair])
+    for i in range(8):
+        await_copy(sg_plane.at[i], sgp_rs.at[i])
+    total = sg_plane[0]
+    for i in range(1, 8):
+        total = total + sg_plane[i]
+    sg_depth[depth] = total
+
+    def sgz_copy(step):
+        return remote(
+            sg_depth.at[depth],
+            sg_depth.at[depth],
+            sgz_ss.at[step],
+            sgz_rs.at[depth],
+            z_dev(lax.rem(depth + step, DEPTH)),
+        )
+
+    for step in range(1, DEPTH):
+        sgz_copy(step).start()
+    stage_second(items[5])
+    stage_third(items[4])
+    stage_fourth(items[3])
+    stage_third(items[5])
+    stage_fourth(items[4])
+    stage_fourth(items[5])
+
+    for i in range(4):
+        await_copy(gx_recv.at[i], gx_rs.at[i])
+    for i in range(4):
+        hid[i] = gx_recv[i].astype(F32)
+    out_copies = []
+    for i in range(4):
+        copy = pltpu.make_async_copy(
+            hid.at[i], gx_o.at[i // 2, pl.ds((i % 2) * BLK, BLK)], out_ss.at[i]
+        )
+        copy.start()
+        out_copies.append(copy)
+    for i in range(4):
+        await_copy(pool_recv.at[i], pool_rs.at[i])
+    for doc in range(2):
+        pooled_o[doc : doc + 1, :] = (
+            pool_recv[2 * doc, 0:1, :] + pool_recv[2 * doc + 1, 0:1, :]
+        ) / own_lengths[:, doc : doc + 1]
+
+    for it in items:
+        it["to_core"].wait_recv()
+    other_core = 1 - core
+    for k, (src, c) in enumerate(((rs_d.at[1], core), (zc_d, other_core))):
+        for i in range(ff_part // BLK):
+            rows = pl.ds(pl.multiple_of(c * ff_part + i * BLK, BLK), BLK)
+            gn[rows, :] = src[i * BLK : (i + 1) * BLK, :].astype(F32)
+    copy = pltpu.make_async_copy(gn.at[pl.ds(0, 2 * ff_part)], gd_o, out_ss.at[4])
+    copy.start()
+    out_copies.append(copy)
+    for src, c in ((rs_i.at[1], core), (zc_i, other_core)):
+        for f in range(SEQ):
+            gi_o[:, tile(2 * f + c, ff_part)] = src[:, f * ff_part : (f + 1) * ff_part].astype(F32)
+    for src, c in ((rs_o.at[1], core), (zc_o, other_core)):
+        go_o[tile(c, wo_part), :] = src[...].astype(F32)
+    for pair in range(3):
+        for src, c in ((rs_q.at[pair, 1], core), (zc_q.at[pair], other_core)):
+            for j, out in enumerate((gq_o, gk_o, gv_o)):
+                out[:, tile(c * 3 + pair, BLK)] = src[:, j * BLK : (j + 1) * BLK].astype(F32)
+    for step in range(1, DEPTH):
+        z = lax.rem(depth + DEPTH - step, DEPTH)
+        await_copy(sg_depth.at[z], sgz_rs.at[z])
+    gs_o[...] = sg_depth[0] + sg_depth[1] + sg_depth[2] + sg_depth[3]
+
+    for copy in out_copies:
+        copy.wait()
+    for copy in pending:
+        copy.wait_send()
+    spread_done(inputs, x_slot, x_ss, x_rs)
+    spread_done(cotangent, c_slot, c_ss, c_rs)
+    pool_each("wait")
+    rso_each("wait")
+    sgp_each("wait")
+    for i in range(SEQ):
+        n1_copy(i).wait_send()
+        g_copy(i).wait_send()
+        n2_copy(i, gat_ss, gat_rs).wait_send()
+        swap_copy(i, gn1_ss, gn1_rs).wait_send()
+        gx_each(i, "wait")
+    for step in range(1, SEQ):
+        rsd_copy(step).wait_send()
+        sgz_copy(step).wait_send()
+        for part in range(SEQ):
+            rsi_copy(part, step).wait_send()
+        for pair in range(3):
+            rsq_copy(pair, step).wait_send()
+    for it in items:
+
+        @pl.when(end_z)
+        def _():
+            it["to_inner"].wait_send()
+
+        @pl.when(inner_z)
+        def _():
+            it["swap"].wait_send()
+            it["to_end"].wait_send()
+
+        it["to_core"].wait_send()
 
 
 def on_device(
@@ -272,6 +1297,166 @@
     )
 
 
+def fused_on_device(
+    inputs,
+    w_query,
+    w_key,
+    w_value,
+    w_out,
+    w_ffn_in,
+    w_ffn_out,
+    attn_gain,
+    ffn_gain,
+    rel_bias,
+    doc_lengths,
+    cotangent,
+):
+    docs, shard_len, width = inputs.shape
+    rows_w, hidden_units = w_ffn_in.shape
+    tokens = shard_len * SEQ
+    half = width // 2
+    part = hidden_units // (2 * SEQ)
+    blocks = tokens // BLK
+    pairs = half // BLK
+    buckets, heads = rel_bias.shape[0] * SEQ, rel_bias.shape[1]
+    chip = lax.axis_index("seq")
+    here = (jnp.arange(SEQ, dtype=jnp.int32) == chip).astype(F32)
+
+    def placed(value):
+        value = value.astype(F32)
+        return (here.reshape((SEQ,) + (1,) * value.ndim) * value).reshape(
+            (-1,) + value.shape[1:]
+        )
+
+    lengths = jnp.pad(doc_lengths.astype(F32).reshape(1, docs), ((0, 1), (0, BLK - docs)))
+    small = jnp.concatenate(
+        [
+            placed(attn_gain).reshape(width // BLK, BLK),
+            lengths,
+            placed(ffn_gain).reshape(width // BLK, BLK),
+            jnp.zeros((2, BLK), F32),
+            jnp.pad(placed(rel_bias), ((0, 0), (0, BLK - heads))),
+        ],
+        axis=0,
+    )
+    anywhere = pl.BlockSpec(memory_space=pl.ANY)
+    vmem = pl.BlockSpec(memory_space=pltpu.VMEM)
+    shape = jax.ShapeDtypeStruct
+    out_shape = (
+        shape((docs, width), F32),
+        shape((docs, shard_len, width), F32),
+        shape((rows_w, width), F32),
+        shape((rows_w, width), F32),
+        shape((rows_w, width), F32),
+        shape((rows_w, width), F32),
+        shape((rows_w, hidden_units), F32),
+        shape((2 * part, width), F32),
+        shape((32, BLK), F32),
+    )
+    out_specs = (vmem, anywhere, vmem, vmem, vmem, vmem, vmem, anywhere, vmem)
+    quarter = tokens // 4
+    out_part = rows_w // 2
+    scratch = [
+        ((SEQ, BLK, width), BF16),
+        ((blocks, BLK, width), BF16),
+        ((tokens, width), BF16),
+        ((width, 3 * half), BF16),
+        ((tokens, 3 * half), BF16),
+        ((tokens, half), BF16),
+        ((half, width), BF16),
+        ((SEQ, BLK, width), F32),
+        ((SEQ, BLK, width), F32),
+        ((SEQ, BLK, width), F32),
+        ((tokens, width), BF16),
+        ((width, SEQ * part), BF16),
+        ((SEQ * part, width), BF16),
+        ((tokens, part), BF16),
+        ((tokens, part), BF16),
+        ((tokens, width), F32),
+        ((2 * pairs, 2 * tokens - BLK, BLK), F32),
+        ((3, 16, 2 * BLK), F32),
+        ((tokens, BLK), F32),
+        ((8, tokens), F32),
+        ((BLK + 16, tokens), BF16),
+        ((tokens, 3 * half), BF16),
+        ((tokens, half), BF16),
+        ((tokens, BLK), F32),
+        ((tokens, BLK), F32),
+        ((tokens + 2 * BLK, quarter), BF16),
+        ((6 * pairs, BLK, BLK), F32),
+        ((2 * pairs, 16, quarter), F32),
+        ((pairs, width, 3 * BLK), BF16),
+        ((3, part, width), BF16),
+        ((3, rows_w, SEQ * part), BF16),
+        ((SEQ, out_part, width), BF16),
+        ((pairs, 3, rows_w, 3 * BLK), BF16),
+    ]
+    for _ in range(3):
+        scratch += [
+            ((part, width), BF16),
+            ((rows_w, SEQ * part), BF16),
+            ((out_part, width), BF16),
+            ((pairs, rows_w, 3 * BLK), BF16),
+        ]
+    scratch += [
+        ((SEQ, BLK, width), BF16),
+        ((SEQ, BLK, width), BF16),
+        ((SEQ + 1, 48, BLK), F32),
+        ((8, width), F32),
+        ((8, part), F32),
+        ((8, width), F32),
+        ((4, 8, width), F32),
+        ((32, BLK), F32),
+        ((8, 32, BLK), F32),
+        ((4, 32, BLK), F32),
+    ]
+    scratch = [pltpu.VMEM(*s) for s in scratch]
+    pair_of = lambda *dims: [pltpu.SemaphoreType.DMA(dims)] * 2
+    semaphores = (
+        pair_of(5)
+        + pair_of(4)
+        + pair_of(4)
+        + pair_of(3, 4)
+        + pair_of(4)
+        + pair_of(4, 4)
+        + pair_of(4)
+        + pair_of(4) * 8
+        + pair_of(3)
+        + pair_of(4, 3)
+        + pair_of(4)
+        + pair_of(3, 3)
+        + pair_of(6, 4)
+        + pair_of(4)
+        + pair_of(8)
+        + pair_of(4)
+        + [pltpu.SemaphoreType.DMA((5,))]
+    )
+    pooled, gx, gq, gk, gv, go, gi, gd, gs = pl.pallas_call(
+        fused_kernel,
+        out_shape=out_shape,
+        in_specs=[anywhere] * 9,
+        out_specs=out_specs,
+        scratch_shapes=scratch + semaphores,
+        compiler_params=pltpu.CompilerParams(
+            collective_id=0, has_side_effects=True, vmem_limit_bytes=VMEM_LIMIT
+        ),
+        name="block",
+    )(inputs, cotangent, w_query, w_key, w_value, w_out, w_ffn_in, w_ffn_out, small)
+
+    def own_part(value, axis, size):
+        return lax.dynamic_slice_in_dim(value, chip * size, size, axis)
+
+    gain_one = own_part(gs[0 : width // BLK].reshape(width), 0, rows_w)
+    gain_two = own_part(gs[8 : 8 + width // BLK].reshape(width), 0, rows_w)
+    per_core = jnp.concatenate([gs[16 : 16 + 2 * pairs], gs[24 : 24 + 2 * pairs]], axis=0)
+    table = own_part(per_core[:, :buckets].T, 0, buckets // SEQ)
+    return (pooled, gx, gq, gk, gv, go, gi, gd, gain_one, gain_two, table)
+
+
+def fits(mesh):
+    return mesh.shape["dp"] == CORES * DEPTH and mesh.shape["seq"] == SEQ
+
+
 def solution(mesh):
     in_specs = (
         P("dp", "seq", None),
@@ -301,5 +1486,5 @@
         P("seq", None),
     )
     return jax.shard_map(
-        on_device, mesh=mesh, in_specs=in_specs, out_specs=out_specs, check_vma=False
-    )
+        fused_on_device if fits(mesh) else on_device, mesh=mesh, in_specs=in_specs, out_specs=out_specs, check_vma=False
+    )

time: 845 us -> 277 us (0.33)
  waiting for transfers between devices: 400 us -> 0 us
  Pallas kernels: 0 us -> 256 us
  matrix products: 163 us -> 0 us
  local copies, waits for them, and re-layouts: 112 us -> 16.1 us
  other arithmetic: 87.8 us -> 2.88 us
  blocking collectives: 58.6 us -> 0 us
  between operations: 16.7 us -> 0.7 us
    pallas_call x0 -> x1, Pallas kernels: none -> 256 us  [fused_on_device(): pl.pallas_call(fused_kernel, out_shape=out_shape, in_specs=[anywhere] * 9...]
    reduce_scatter x8 -> x0, waiting for transfers between devices: 220 us -> none  [the longest x1 60 us: on_device(): lax.psum_scatter(grad_in.astype(jnp.bfloat16), 'seq', scatter_dimension=0...]
    dot_general x26 -> x0, matrix products: 163 us -> none  [the longest x6 26.4 us: outer_sum(): lax.dot_general(left, right, (((0,), (0,)), ((), ())), preferred_element_...]
    all_gather x8 -> x0, waiting for transfers between devices: 128 us -> none  [the longest x1 50.7 us: on_device(): lax.all_gather(w_ffn_out, 'seq', axis=0, tiled=True)]
    psum x1 -> x0, waiting for transfers between devices: 48.3 us -> none  [on_device(): lax.psum(shards[0].astype(jnp.bfloat16), 'dp').astype(jnp.float32)]
    eq x1 -> x0, local copies, waits for them, and re-layouts: 46.5 us -> none  [on_device(): bucket_ids(query_pos, key_pos)[:, :, None] == bucket_range]
    reduce_sum x3 -> x0, other arithmetic: 46.1 us -> none  [the longest x1 30.5 us: on_device(): jnp.einsum('bhqk,qkn->nh', grad_logits, onehot, preferred_element_type=jn...]
    unnamed x2 -> x0, blocking collectives: 26.4 us -> none
  transfers between devices with their start and end apart: 17 -> 0, of which waited for: 12 -> 0; matrix products, arithmetic and copies ran while one was open for 36% -> 0% of each run, Pallas kernels for 0% -> 0%
where the time goes in v1:
time: 277 us; the launch traced here: 276 us
  Pallas kernels  256 us (92%)
  local copies, waits for them, and re-layouts  16.1 us (6%)
  other arithmetic  2.88 us (1%)
    pallas_call x1, Pallas kernels, fused_on_device(): pl.pallas_call(fused_kernel, out_shape=out_shape, in_specs=[anywhere] * 9...  256 us
    unnamed x21, local copies, waits for them, and re-layouts  11.9 us

profile of v1, /device:TPU:0, one launch (start us, length us, event | category | flops | bytes accessed | tf_op | source)
XLA Modules:
  0.0 275.5 jit_solution(11281922483731993908)
XLA Ops:
  0.7 0.7 convert_bitcast_fusion
  1.3 0.7 convert_element_type.28
  2.0 0.7 convert_element_type.30
  2.7 0.1 mul.67
  2.8 0.7 convert_element_type.31
  3.5 0.1 broadcast_multiply_fusion
  3.6 0.1 mul.65
  3.6 0.1 mul.62
  3.8 1.8 concatenate.6.small
  5.6 255.9 %block.1 = (f32[2,768]{1,0:T(2,128)}, f32[2,256,768]{2,1,0:T(8,128)}, f32[192,768]{1,0:T(8,128)}, f32[192,768]{1,0:T(8,128)}, f32[192,768]{1,0:T(8,128)}, /*inde...) custom-call(bf16[2,256,768]{2,1,0:T(8,128)(2,1)} %inputs.1, ...), custom_call_target="tpu_custom_call" | custom-call | tf_op jit(solution)/shard_map/block/pallas_call | solution.py:1434
  261.5 0.8 fusion.1
  262.3 0.1 fusion
  262.4 0.7 copy.23
  263.0 0.6 dynamic_slice.10
  263.7 0.6 dynamic_slice.9
  264.3 1.3 copy.32
  265.6 2.7 copy.33
  268.3 0.8 copy.34
  269.1 0.8 copy.35
  270.0 0.8 copy.36
  270.8 0.8 copy.37
  271.6 1.4 copy.38
  273.0 1.1 copy-done
  274.1 1.4 copy.39
  (17 shorter events, 0.2 us)
Async XLA Ops:
  261.5 6.8 %copy-start.5 = (f32[192,768]{1,0:T(8,128)S(1)}, f32[192,768]{1,0:T(8,128)}, u32[]{:S(2)}) copy-start(f32[192,768]{1,0:T(8,128)} %get-tuple-element.59) | copy-start | bytes 1769476
  261.5 7.6 %copy-start.4 = (f32[192,768]{1,0:T(8,128)S(1)}, f32[192,768]{1,0:T(8,128)}, u32[]{:S(2)}) copy-start(f32[192,768]{1,0:T(8,128)} %get-tuple-element.60) | copy-start | bytes 1769476
  265.6 4.4 %copy-start.3 = (f32[192,768]{1,0:T(8,128)S(1)}, f32[192,768]{1,0:T(8,128)}, u32[]{:S(2)}) copy-start(f32[192,768]{1,0:T(8,128)} %get-tuple-element.61) | copy-start | bytes 1769476
  268.3 2.5 copy-start.2
  268.3 3.3 %copy-start.1 = (f32[192,3072]{1,0:T(8,128)S(1)}, f32[192,3072]{1,0:T(8,128)}, u32[]{:S(2)}) copy-start(f32[192,3072]{1,0:T(8,128)} %get-tuple-element.63) | copy-start | bytes 7077892
  271.6 2.5 copy-start

commit v2 on v0

--- a/solution.py
+++ b/solution.py
@@ -3,6 +3,8 @@
 import jax
 import jax.numpy as jnp
 from jax import lax
+from jax.experimental import pallas as pl
+from jax.experimental.pallas import tpu as pltpu
 from jax.sharding import PartitionSpec as P
 
 EPS = 1e-06
@@ -49,6 +51,1230 @@
         grad_scaled * source, -1, keepdims=True
     )
     return (grad_gain, grad_source)
+
+
+SEQ, CORES, DEPTH = 4, 2, 4
+BLK = 128
+MESH = pl.DeviceIdType.MESH
+F32 = jnp.float32
+BF16 = jnp.bfloat16
+VMEM_LIMIT = 60 << 20
+
+
+def contract(left, right, left_dim, right_dim):
+    return lax.dot_general(
+        left, right, (((left_dim,), (right_dim,)), ((), ())), preferred_element_type=F32
+    )
+
+
+def exact(left, right, left_dim, right_dim):
+    return lax.dot_general(
+        left,
+        right,
+        (((left_dim,), (right_dim,)), ((), ())),
+        preferred_element_type=F32,
+        precision=lax.Precision.HIGHEST,
+    )
+
+
+def await_copy(ref, sem):
+    pltpu.make_async_copy(ref, ref, sem).wait()
+
+
+def tile(index, size):
+    return pl.ds(pl.multiple_of(index * size, size), size)
+
+
+def bucket_of(offset):
+    distance = jnp.abs(offset)
+    beyond = jnp.full(distance.shape, 8, jnp.int32)
+    for threshold in THRESHOLDS:
+        beyond = beyond + (distance >= threshold).astype(jnp.int32)
+    return jnp.where(offset > 0, 16, 0) + jnp.where(distance < 8, distance, beyond)
+
+
+def full_sum(value):
+    return jnp.sum(jnp.sum(value, 0, keepdims=True), 1, keepdims=True)
+
+
+def fused_kernel(
+    inputs,
+    cotangent,
+    w_query,
+    w_key,
+    w_value,
+    w_out,
+    w_in,
+    w_down,
+    gains_in,
+    bias_in,
+    lengths_in,
+    pooled_o,
+    small_o,
+    table_o,
+    gx_o,
+    gq_o,
+    gk_o,
+    gv_o,
+    go_o,
+    gi_o,
+    gd_o,
+    xown,
+    grads,
+    nrm1,
+    wqkv,
+    qkv,
+    mixed,
+    wo,
+    psend,
+    precv,
+    hid,
+    nrm2,
+    wi,
+    wd,
+    act,
+    slope,
+    gpre,
+    gn,
+    strip,
+    vecs,
+    maskc,
+    kaug,
+    lse,
+    flip,
+    dqkv,
+    dpair,
+    gmix,
+    dk_acc,
+    dv_acc,
+    ds_buf,
+    near,
+    far,
+    gqkv,
+    gdn,
+    d_dx,
+    d_dy,
+    d_rx,
+    d_ry,
+    d_za,
+    d_zb,
+    i_dx,
+    i_dy,
+    i_rx,
+    i_ry,
+    i_za,
+    i_zb,
+    q_dx,
+    q_dy,
+    q_rx,
+    q_ry,
+    q_za,
+    q_zb,
+    rs_o,
+    o_za,
+    o_zb,
+    gx_send,
+    small_all,
+    wide,
+    gains,
+    asum,
+    pp,
+    pool_recv,
+    sg,
+    sg_plane,
+    sg_depth,
+    turned,
+    small_ss,
+    small_rs,
+    x_ss,
+    x_rs,
+    c_ss,
+    c_rs,
+    wg_ss,
+    wg_rs,
+    wo_ss,
+    wo_rs,
+    n1_ss,
+    n1_rs,
+    g_ss,
+    g_rs,
+    part_ss,
+    part_rs,
+    n2_ss,
+    n2_rs,
+    gn2_ss,
+    gn2_rs,
+    gat_ss,
+    gat_rs,
+    gn1_ss,
+    gn1_rs,
+    gx_ss,
+    gx_rs,
+    rs_ss,
+    rs_rs,
+    rso_ss,
+    rso_rs,
+    z_ss,
+    z_rs,
+    pool_ss,
+    pool_rs,
+    sgp_ss,
+    sgp_rs,
+    sgz_ss,
+    sgz_rs,
+    out_s,
+):
+    dp = lax.axis_index("dp")
+    chip = lax.axis_index("seq")
+    depth, core = lax.div(dp, 2), lax.rem(dp, 2)
+    row, col = lax.div(chip, 2), lax.rem(chip, 2)
+    other = (depth * 2 + 1 - core, chip)
+    xn = row * 2 + 1 - col
+    yn = (1 - row) * 2 + col
+    dn = (1 - row) * 2 + 1 - col
+    tokens, width = nrm1.shape
+    half = width // 2
+    rows_w = w_query.shape[0]
+    ff_part = gpre.shape[1]
+    quarter = tokens // 4
+
+    def remote(src, dst, send, recv, device):
+        return pltpu.make_async_remote_copy(
+            src_ref=src,
+            dst_ref=dst,
+            send_sem=send,
+            recv_sem=recv,
+            device_id=device,
+            device_id_type=MESH,
+        )
+
+    def ahead(step):
+        return lax.rem(chip + step, SEQ)
+
+    pending = []
+
+    def send_now(*args):
+        copy = remote(*args)
+        copy.start()
+        pending.append(copy)
+
+    lane = lax.broadcasted_iota(jnp.int32, (1, BLK), 1)
+    wide[...] = jnp.zeros_like(wide)
+    wide[0:2, 0:rows_w] = gains_in[...]
+    turned_gains = pltpu.roll(wide[...], chip * rows_w, 1)
+    small_all[0] = jnp.zeros_like(small_all[0])
+    for which in range(2):
+        for i in range(width // BLK):
+            small_all[0, 8 * which + i : 8 * which + i + 1, :] = turned_gains[
+                which : which + 1, i * BLK : (i + 1) * BLK
+            ]
+    small_all[0, 6:7, :] = jnp.where(
+        lane == 0, lengths_in[0].astype(F32), lengths_in[1].astype(F32)
+    )
+    small_all[0, tile(2 + chip, 8), 0 : bias_in.shape[1]] = bias_in[...].astype(F32)
+
+    barrier = pltpu.get_barrier_semaphore()
+    for step in range(SEQ):
+        if step:
+            pl.semaphore_signal(barrier, inc=1, device_id=(dp, ahead(step)), device_id_type=MESH)
+        pl.semaphore_signal(
+            barrier, inc=1, device_id=(other[0], ahead(step)), device_id_type=MESH
+        )
+    for step in range(1, DEPTH):
+        pl.semaphore_signal(
+            barrier,
+            inc=1,
+            device_id=(lax.rem(depth + step, DEPTH) * 2 + core, chip),
+            device_id_type=MESH,
+        )
+    pl.semaphore_wait(barrier, 2 * SEQ - 1 + DEPTH - 1)
+
+    mine = small_all.at[0]
+    for step in range(1, SEQ):
+        send_now(
+            mine, small_all.at[step], small_ss.at[step], small_rs.at[step], (dp, ahead(step))
+        )
+    send_now(mine, small_all.at[SEQ], small_ss.at[SEQ], small_rs.at[SEQ], other)
+
+    def spread(source, dest_of, send, recv, action):
+        for doc in range(2):
+            for to in range(2):
+                block = source.at[doc, pl.ds(to * BLK, BLK)]
+                target = core * 2 + doc
+                own = (target == chip) & (core == to)
+                copy = remote(
+                    block,
+                    dest_of(to),
+                    send.at[doc * 2 + to],
+                    recv.at[chip],
+                    (depth * 2 + to, target),
+                )
+                if action == "start":
+
+                    @pl.when(own)
+                    def _():
+                        pltpu.make_async_copy(block, dest_of(to), recv.at[chip]).start()
+
+                @pl.when(jnp.logical_not(own))
+                def _():
+                    if action == "start":
+                        copy.start()
+                    else:
+                        copy.wait_send()
+
+    x_slot = lambda to: xown.at[chip]
+    c_slot = lambda to: grads.at[chip * 2 + to]
+    spread(inputs, x_slot, x_ss, x_rs, "start")
+
+    class Gather:
+        def __init__(self, index, pieces, place):
+            self.index, self.pieces, self.place = index, pieces, place
+            self.bind()
+
+        def half_of(self, owner, which):
+            ref = self.place(owner)
+            size = ref.shape[0] // 2
+            return ref.at[pl.ds(which * size, size)]
+
+        def bind(self):
+            k = self.index
+            self.local, self.one, self.two = [], [], []
+            for src, cut in self.pieces:
+                dst = cut(self.place(chip))
+                self.local.append(pltpu.make_async_copy(src, dst, wg_rs.at[k, 0]))
+                self.one.append(remote(src, dst, wg_ss.at[k, 0], wg_rs.at[k, 1], (dp, xn)))
+                self.one.append(remote(src, dst, wg_ss.at[k, 1], wg_rs.at[k, 2], (dp, yn)))
+            via_x, via_y = self.half_of(xn, 1), self.half_of(yn, 0)
+            self.two = [
+                remote(via_x, via_x, wg_ss.at[k, 2], wg_rs.at[k, 3], (dp, yn)),
+                remote(via_y, via_y, wg_ss.at[k, 3], wg_rs.at[k, 4], (dp, xn)),
+            ]
+            self.from_x, self.from_y = self.place(xn), self.place(yn)
+            self.last = [self.half_of(dn, 1), self.half_of(dn, 0)]
+            self.own = self.place(chip)
+
+        def first(self):
+            for copy in self.local + self.one:
+                copy.start()
+
+        def second(self):
+            k = self.index
+            await_copy(self.from_x, wg_rs.at[k, 1])
+            self.two[0].start()
+            await_copy(self.from_y, wg_rs.at[k, 2])
+            self.two[1].start()
+
+        def done(self):
+            k = self.index
+            await_copy(self.own, wg_rs.at[k, 0])
+            await_copy(self.last[0], wg_rs.at[k, 3])
+            await_copy(self.last[1], wg_rs.at[k, 4])
+
+        def sent(self):
+            k = self.index
+            for copy in self.two:
+                copy.wait_send()
+            await_copy(self.own, wg_ss.at[k, 0])
+            await_copy(self.own, wg_ss.at[k, 1])
+
+    core_cols = tile(core, half)
+    whole = lambda ref: ref
+    row_half = rows_w // 2
+
+    def qkv_item(index, part):
+        return Gather(
+            index,
+            [
+                (
+                    w.at[pl.ds(part * row_half, row_half), core_cols],
+                    lambda ref, i=i: ref.at[:, pl.ds(i * half, half)],
+                )
+                for i, w in enumerate((w_query, w_key, w_value))
+            ],
+            lambda owner: wqkv.at[
+                pl.ds(pl.multiple_of(owner * rows_w + part * row_half, row_half), row_half)
+            ],
+        )
+
+    def in_item(index, part):
+        return Gather(
+            index,
+            [
+                (
+                    w_in.at[:, tile((2 * part + f) * 2 + core, ff_part)],
+                    lambda ref, f=f: ref.at[:, pl.ds(f * ff_part, ff_part)],
+                )
+                for f in range(2)
+            ],
+            lambda owner: wi.at[tile(owner, rows_w), pl.ds(part * 2 * ff_part, 2 * ff_part)],
+        )
+
+    def down_item(index, part):
+        size = ff_part // 2
+        return Gather(
+            index,
+            [(w_down.at[pl.ds(pl.multiple_of(core * ff_part + part * size, size), size)], whole)],
+            lambda owner: wd.at[
+                pl.ds(pl.multiple_of(owner * ff_part + part * size, size), size)
+            ],
+        )
+
+    qkv_items = [qkv_item(0, 0), qkv_item(1, 1)]
+    in_items = [in_item(2, 0), in_item(3, 1)]
+    down_items = [down_item(4, 0), down_item(5, 1)]
+    for it in qkv_items:
+        it.first()
+
+    wo_part = rows_w // 2
+    wo_src = w_out.at[tile(core, wo_part)]
+    wo_dst = wo.at[tile(col * 2 + core, wo_part)]
+
+    def wo_each(action):
+        for to in range(SEQ):
+            own = (chip == to) & (core == row)
+            copy = remote(
+                wo_src, wo_dst, wo_ss.at[to], wo_rs.at[col * 2 + core], (depth * 2 + row, to)
+            )
+            if action == "start":
+
+                @pl.when(own)
+                def _():
+                    pltpu.make_async_copy(wo_src, wo_dst, wo_rs.at[col * 2 + core]).start()
+
+            @pl.when(jnp.logical_not(own))
+            def _():
+                if action == "start":
+                    copy.start()
+                else:
+                    copy.wait_send()
+
+    for step in range(1, SEQ + 1):
+        await_copy(small_all.at[step], small_rs.at[step])
+    summed = small_all[0] + small_all[1] + small_all[2] + small_all[3]
+    for which in range(2):
+        gains[which : which + 1, :] = jnp.concatenate(
+            [summed[8 * which + i : 8 * which + i + 1, :] for i in range(width // BLK)], axis=1
+        )
+    length_row = jnp.where(row == core, small_all[0, 6:7, :], small_all[SEQ, 6:7, :])
+    length = jnp.where(col == 0, length_row[:, 0:1], length_row[:, 1:2])
+    own_lengths = small_all[0, 6:7, 0:2]
+    table = summed[16:48, :].astype(BF16)
+    lane_two = lax.broadcasted_iota(jnp.int32, (1, 2 * BLK), 1)
+    minus = jnp.where(lane_two < BLK, lane_two, lane_two - 2 * BLK)
+    for off in (-1, 0, 1):
+        ids = bucket_of(off * BLK - minus)
+        onehot = (lax.broadcasted_iota(jnp.int32, (32, 2 * BLK), 0) == ids).astype(BF16)
+        vecs[off + 1] = contract(table, onehot, 0, 0)[0:16, :]
+
+    @pl.loop(0, 6)
+    def _(h):
+        values = [vecs[i, pl.ds(core * 6 + h, 1), :] for i in range(3)]
+        left = jnp.broadcast_to(values[0][:, BLK - 1 : BLK], (BLK, BLK))
+        right = jnp.broadcast_to(values[2][:, BLK + 1 : BLK + 2], (BLK, BLK))
+        for i in range(6):
+            strip[h, i * BLK : (i + 1) * BLK, :] = left
+            strip[h, (i + 9) * BLK : (i + 10) * BLK, :] = right
+        for i in range(3):
+            skewed = pltpu.roll(
+                jnp.broadcast_to(values[i], (BLK, 2 * BLK)), 0, 1, stride=1, stride_axis=0
+            )
+            strip[h, (i + 6) * BLK : (i + 7) * BLK, :] = skewed[:, :BLK]
+
+    maskc[...] = jnp.where(
+        lax.broadcasted_iota(jnp.int32, maskc.shape, 0).astype(F32) < length, 0.0, NEGATIVE
+    ).astype(BF16)
+
+    def block_valid(b):
+        pos = lax.broadcasted_iota(jnp.int32, (BLK, 1), 0) + b * BLK
+        return (pos.astype(F32) < length).astype(F32)
+
+    def n1_copy(i):
+        block = nrm1.at[tile(2 * i + core, BLK)]
+        return remote(block, block, n1_ss.at[i], n1_rs.at[i], other)
+
+    @pl.loop(0, SEQ)
+    def _(i):
+        await_copy(xown.at[i], x_rs.at[i])
+        source = xown[i].astype(F32)
+        scale = lax.rsqrt(jnp.mean(source * source, -1, keepdims=True) + EPS)
+        nrm1[tile(2 * i + core, BLK), :] = (source * scale * gains[0:1, :]).astype(BF16)
+        n1_copy(i).start()
+
+    for it in qkv_items:
+        it.second()
+    wo_each("start")
+    for it in in_items:
+        it.first()
+    for it in qkv_items:
+        it.done()
+    for i in range(SEQ):
+        n1_copy(i).wait_recv()
+
+    @pl.loop(0, 4)
+    def _(i):
+        rows = tile(i, quarter)
+        qkv[rows, :] = contract(nrm1[rows, :], wqkv[...], 1, 0).astype(BF16)
+
+    flip[BLK : BLK + 16, :] = jnp.ones((16, tokens), BF16)
+    mine_lanes = [lane < 64, lane >= 64]
+    spare = [lane == 64, lane == 0]
+
+    def prepare_keys(pair):
+        keys = qkv[:, tile(3 + pair, BLK)]
+        for h in range(2):
+            kaug[h] = jnp.where(mine_lanes[h], keys, jnp.where(spare[h], maskc[...], 0))
+
+    def scores(pair, qb, h):
+        queries = qkv[tile(qb, quarter), tile(pair, BLK)]
+        plain = jnp.where(mine_lanes[h], queries, jnp.zeros_like(queries))
+        raised = jnp.where(spare[h], jnp.ones_like(queries), plain)
+        raw = contract(kaug[h], raised, 1, 1)
+        head = pair * 2 + h
+        biases = [
+            strip[head, pl.ds(pl.multiple_of((7 - 2 * qb - i) * BLK, BLK), tokens), :]
+            for i in range(2)
+        ]
+        return raw + jnp.concatenate(biases, axis=1), plain
+
+    def serve(now, table):
+        for when, actions in table.items():
+
+            @pl.when(now == when)
+            def _():
+                for action in actions:
+                    action()
+
+    def forward_in_tail():
+        in_items[1].second()
+        spread(cotangent, c_slot, c_ss, c_rs, "start")
+        for it in down_items:
+            it.first()
+
+    @pl.loop(0, 12)
+    def _(now):
+        pair, qb = lax.div(now, 4), lax.rem(now, 4)
+
+        @pl.when(qb == 0)
+        def _():
+            flip[0:BLK, :] = jnp.transpose(qkv[:, tile(6 + pair, BLK)])
+            prepare_keys(pair)
+
+        parts = []
+        for h in range(2):
+            logits, _ = scores(pair, qb, h)
+            highest = jnp.max(logits, 0, keepdims=True)
+            raised = jnp.exp(logits - highest).astype(BF16)
+            result = contract(flip[...], raised, 1, 0)
+            total = result[BLK : BLK + 1, :]
+            lse[pl.ds(pair * 2 + h, 1), tile(qb, quarter)] = highest + jnp.log(total)
+            parts.append(result[64 * h : 64 * h + 64, :] / total)
+        mixed[tile(qb, quarter), tile(pair, BLK)] = jnp.transpose(
+            jnp.concatenate(parts, axis=0)
+        ).astype(BF16)
+        serve(now, {5: [in_items[0].second], 9: [forward_in_tail]})
+
+    def swap_copy(i, send, recv):
+        return remote(psend.at[i], precv.at[i], send.at[i], recv.at[i], other)
+
+    for k in range(4):
+        await_copy(wo.at[pl.ds(k * wo_part, wo_part)], wo_rs.at[k])
+
+    def blocks_of(ref, i, parity):
+        return jnp.concatenate(
+            [ref[tile(2 * (2 * i + j) + parity, BLK), :] for j in range(2)], axis=0
+        )
+
+    @pl.loop(0, 2)
+    def _(i):
+        result = contract(blocks_of(mixed, i, 1 - core), wo[...], 1, 0)
+        for j in range(2):
+            psend[2 * i + j] = result[j * BLK : (j + 1) * BLK, :]
+            swap_copy(2 * i + j, part_ss, part_rs).start()
+
+    def n2_copy(i, send, recv):
+        block = nrm2.at[tile(2 * i + core, BLK)]
+        return remote(block, block, send.at[i], recv.at[i], other)
+
+    pp[...] = jnp.zeros_like(pp)
+
+    @pl.loop(0, 2)
+    def _(k):
+        result = contract(blocks_of(mixed, k, core), wo[...], 1, 0)
+        for j in range(2):
+            i = 2 * k + j
+            hidden = xown[i].astype(F32) + result[j * BLK : (j + 1) * BLK, :]
+            swap_copy(i, part_ss, part_rs).wait_recv()
+            hidden = hidden + precv[i]
+            hid[i] = hidden
+            scale = lax.rsqrt(jnp.mean(hidden * hidden, -1, keepdims=True) + EPS)
+            nrm2[tile(2 * i + core, BLK), :] = (hidden * scale * gains[1:2, :]).astype(BF16)
+            n2_copy(i, n2_ss, n2_rs).start()
+            pp[0:1, :] += jnp.sum(hidden * block_valid(2 * i + core), 0, keepdims=True)
+
+    for it in in_items:
+        it.done()
+    for i in range(SEQ):
+        n2_copy(i, n2_ss, n2_rs).wait_recv()
+
+    def g_copy(i):
+        block = grads.at[2 * i + core]
+        return remote(block, block, g_ss.at[i], g_rs.at[i], other)
+
+    def take_cotangent():
+        @pl.loop(0, SEQ)
+        def _(i):
+            b = 2 * i + core
+            await_copy(grads.at[b], c_rs.at[i])
+            grads[b] = (grads[b].astype(F32) * block_valid(b)).astype(BF16)
+            g_copy(i).start()
+
+    asum[...] = jnp.zeros_like(asum)
+
+    @pl.loop(0, 16)
+    def _(now):
+        f, i = lax.div(now, 4), lax.rem(now, 4)
+        rows, f_cols = tile(i, quarter), tile(f, ff_part)
+        value = contract(nrm2[rows, :], wi[:, f_cols], 1, 0)
+        square = value * value
+        tangent = jnp.tanh(GELU_C * (value + GELU_K * value * square))
+        half_up = 0.5 * (1.0 + tangent)
+        active = (value * half_up).astype(BF16)
+        act[rows, f_cols] = active
+        slope[rows, f_cols] = (
+            half_up
+            + 0.5
+            * value
+            * (1.0 - tangent * tangent)
+            * GELU_C
+            * (1.0 + 3.0 * GELU_K * square)
+        ).astype(BF16)
+        pos = lax.broadcasted_iota(jnp.int32, (8, quarter), 1) + i * quarter
+        valid = (pos.astype(F32) < length).astype(BF16)
+        asum[:, f_cols] += contract(valid, active, 1, 0)
+        serve(now, {11: [take_cotangent], 15: [down_items[0].second]})
+
+    for i in range(SEQ):
+        g_copy(i).wait_recv()
+    g_all = lambda: grads[...].reshape(tokens, width)
+
+    class Chunk:
+        made = 0
+
+        def __init__(self, src, dx, dy, rx, ry, za, zb, outs):
+            self.index = Chunk.made
+            Chunk.made += 1
+            self.src, self.dx, self.dy, self.rx, self.ry = src, dx, dy, rx, ry
+            self.za, self.zb, self.outs = za, zb, outs
+            self.bind()
+
+        def bind(self):
+            k = self.index
+            size = self.dx.shape[0]
+            cut = lambda ref, which: ref.at[pl.ds(which * size, size)]
+            ss, rs = (lambda i: rs_ss.at[k, i]), (lambda i: rs_rs.at[k, i])
+            to_x, to_y = (dp, xn), (dp, yn)
+            self.one = [
+                remote(cut(self.src(dn), 1), self.dx, ss(0), rs(0), to_x),
+                remote(cut(self.src(dn), 0), self.dy, ss(1), rs(1), to_y),
+                remote(cut(self.src(xn), 1), cut(self.rx, 1), ss(2), rs(2), to_x),
+                remote(cut(self.src(yn), 0), cut(self.ry, 0), ss(3), rs(3), to_y),
+            ]
+            self.sum_y, self.sum_x = cut(self.src(yn), 1), cut(self.src(xn), 0)
+            self.two = [
+                remote(self.sum_y, cut(self.ry, 1), ss(4), rs(4), to_y),
+                remote(self.sum_x, cut(self.rx, 0), ss(5), rs(5), to_x),
+            ]
+            self.bind_z(self.rx, self.ry)
+
+        def bind_z(self, reduced, final):
+            k = self.index
+            self.reduced, self.final = reduced, final
+            sem = lambda i: (z_ss.at[k, i], z_rs.at[k, i])
+            self.to_inner = remote(reduced, self.za, *sem(0), z_dev(toward))
+            self.swap = remote(reduced, self.zb, *sem(1), z_dev(across))
+            self.to_end = remote(final, final, *sem(2), z_dev(outward))
+
+        def start(self):
+            for copy in self.one:
+                copy.start()
+
+        def middle(self):
+            for at, sent, sums, copy in (
+                (0, self.dx, self.sum_y, self.two[0]),
+                (1, self.dy, self.sum_x, self.two[1]),
+            ):
+                self.one[at].wait_recv()
+                sums[...] = (sums[...].astype(F32) + sent[...].astype(F32)).astype(BF16)
+                copy.start()
+
+        def total(self):
+            for copy in (self.one[2], self.one[3], *self.two):
+                copy.wait_recv()
+            self.rx[...] = (
+                self.src(chip)[...].astype(F32)
+                + self.rx[...].astype(F32)
+                + self.ry[...].astype(F32)
+            ).astype(BF16)
+
+        def z_one(self):
+            self.total()
+
+            @pl.when(end_z)
+            def _():
+                self.to_inner.start()
+
+        def z_two(self):
+            @pl.when(inner_z)
+            def _():
+                self.to_inner.wait_recv()
+                self.reduced[...] = (
+                    self.reduced[...].astype(F32) + self.za[...].astype(F32)
+                ).astype(BF16)
+                self.swap.start()
+
+        def z_three(self):
+            @pl.when(inner_z)
+            def _():
+                self.swap.wait_recv()
+                self.final[...] = (
+                    self.reduced[...].astype(F32) + self.zb[...].astype(F32)
+                ).astype(BF16)
+                self.to_end.start()
+
+        def each_out(self, act_on):
+            k = self.index
+            for n, (cols, place) in enumerate(self.outs):
+                src = self.final if cols is None else self.final.at[:, cols]
+                act_on(
+                    remote(src, place(core), z_ss.at[k, 3 + n], z_rs.at[k, 3 + n], other),
+                    pltpu.make_async_copy(src, place(core), out_s.at[k, n]),
+                )
+
+        def z_four(self):
+            @pl.when(end_z)
+            def _():
+                self.to_end.wait_recv()
+
+            self.each_out(lambda there, here: (there.start(), here.start()))
+
+        def finish(self):
+            self.each_out(
+                lambda there, here: (there.wait_recv(), there.wait_send(), here.wait())
+            )
+
+            @pl.when(end_z)
+            def _():
+                self.to_inner.wait_send()
+
+            @pl.when(inner_z)
+            def _():
+                self.swap.wait_send()
+                self.to_end.wait_send()
+
+            for copy in self.plane_sends():
+                copy.wait_send()
+
+        def plane_sends(self):
+            return self.one + self.two
+
+    inner_z = (depth == 1) | (depth == 2)
+    end_z = jnp.logical_not(inner_z)
+    toward = jnp.where(depth == 0, 1, 2)
+    outward = jnp.where(depth == 1, 0, 3)
+    across = jnp.where(depth == 1, 2, 1)
+
+    def z_dev(z):
+        return (z * 2 + core, chip)
+
+    d_chunks = [
+        Chunk(
+            lambda owner, i=i: gdn.at[i, owner],
+            d_dx.at[i],
+            d_dy.at[i],
+            d_rx.at[i],
+            d_ry.at[i],
+            d_za.at[i],
+            d_zb.at[i],
+            [
+                (
+                    None,
+                    lambda c, i=i: gd_o.at[
+                        pl.ds(pl.multiple_of(c * ff_part + i * BLK, BLK), BLK)
+                    ],
+                )
+            ],
+        )
+        for i in range(ff_part // BLK)
+    ]
+
+    for i in range(ff_part // BLK):
+        columns = jnp.concatenate(
+            [act[:, f * ff_part + i * BLK : f * ff_part + (i + 1) * BLK] for f in range(SEQ)],
+            axis=1,
+        )
+        gdn[i] = contract(columns, g_all(), 0, 0).astype(BF16).reshape(SEQ, BLK, width)
+        if i == 1:
+            down_items[1].second()
+            d_chunks[0].start()
+            d_chunks[1].start()
+    d_chunks[2].start()
+    for it in down_items:
+        it.done()
+    for it in in_items:
+        it.sent()
+
+    def pooled_part(f):
+        cols = slice(f * ff_part, (f + 1) * ff_part)
+        total = asum[0:1, cols]
+        high = total.astype(BF16)
+        rest = total - high.astype(F32)
+        middle = rest.astype(BF16)
+        low = (rest - middle.astype(F32)).astype(BF16)
+        for piece in (high, middle, low):
+            pp[0:1, :] += contract(jnp.broadcast_to(piece, (16, ff_part)), wd[cols, :], 1, 0)[
+                0:1, :
+            ]
+
+    i_chunks = [
+        Chunk(
+            lambda owner, f=f: wi.at[tile(owner, rows_w), pl.ds(f * ff_part, ff_part)],
+            i_dx.at[f],
+            i_dy.at[f],
+            i_rx.at[f],
+            i_ry.at[f],
+            i_za.at[f],
+            i_zb.at[f],
+            [(None, lambda c, f=f: gi_o.at[:, tile(2 * f + c, ff_part)])],
+        )
+        for f in range(SEQ)
+    ]
+    for f in range(SEQ):
+        f_cols = slice(f * ff_part, (f + 1) * ff_part)
+
+        @pl.loop(0, 4)
+        def _(i):
+            rows = tile(i, quarter)
+            upstream = grads[pl.ds(2 * i, 2)].reshape(quarter, width)
+            grad = contract(upstream, wd[f_cols, :], 1, 1) * slope[rows, f_cols].astype(F32)
+            grad = grad.astype(BF16)
+            gpre[rows, :] = grad
+            back = contract(grad, wi[:, f_cols], 1, 1)
+            if f == 0:
+                gn[rows, :] = back
+            else:
+                gn[rows, :] += back
+
+        pooled_part(f)
+
+        @pl.loop(0, width // (2 * BLK))
+        def _(i):
+            wi[tile(i, 2 * BLK), f_cols] = contract(
+                nrm2[:, tile(i, 2 * BLK)], gpre[...], 0, 0
+            ).astype(BF16)
+
+        if f < 3:
+            d_chunks[f].middle()
+        if f:
+            i_chunks[f - 1].middle()
+        i_chunks[f].start()
+
+    def pool_each(action):
+        for to in range(SEQ):
+            own = (chip == to) & (core == row)
+            dst = pool_recv.at[col * 2 + core]
+            copy = remote(pp, dst, pool_ss.at[to], pool_rs.at[col * 2 + core], (depth * 2 + row, to))
+            if action == "start":
+
+                @pl.when(own)
+                def _():
+                    pltpu.make_async_copy(pp, dst, pool_rs.at[col * 2 + core]).start()
+
+            @pl.when(jnp.logical_not(own))
+            def _():
+                if action == "start":
+                    copy.start()
+                else:
+                    copy.wait_send()
+
+    for i in range(SEQ):
+        swap_copy(i, part_ss, part_rs).wait_send()
+        n2_copy(i, n2_ss, n2_rs).wait_send()
+
+    @pl.loop(0, SEQ)
+    def _(i):
+        psend[i] = gn[tile(2 * i + 1 - core, BLK), :]
+        swap_copy(i, gn2_ss, gn2_rs).start()
+
+    sg[...] = jnp.zeros_like(sg)
+
+    def add_gain(first, value):
+        for i in range(width // BLK):
+            sg[first + i : first + i + 1, :] += value[:, i * BLK : (i + 1) * BLK]
+
+    @pl.loop(0, SEQ)
+    def _(i):
+        b = 2 * i + core
+        swap_copy(i, gn2_ss, gn2_rs).wait_recv()
+        normed = gn[tile(b, BLK), :] + precv[i]
+        hidden = hid[i]
+        scale = lax.rsqrt(jnp.mean(hidden * hidden, -1, keepdims=True) + EPS)
+        add_gain(8, jnp.sum(normed * hidden * scale, 0, keepdims=True))
+        scaled = normed * gains[1:2, :]
+        inner = jnp.mean(scaled * hidden, -1, keepdims=True)
+        result = grads[b].astype(F32) + scale * scaled - hidden * (scale * scale * scale) * inner
+        hid[i] = result
+        nrm2[tile(b, BLK), :] = result.astype(BF16)
+        n2_copy(i, gat_ss, gat_rs).start()
+
+    pool_each("start")
+    for i in range(SEQ):
+        n2_copy(i, gat_ss, gat_rs).wait_recv()
+
+    @pl.loop(0, 4)
+    def _(i):
+        rows = tile(i, quarter)
+        gmix[rows, :] = contract(nrm2[rows, :], wo[...], 1, 1).astype(BF16)
+
+    wo[...] = contract(mixed[...], nrm2[...], 0, 0).astype(BF16)
+
+    def rso_each(action):
+        for k in range(2):
+            for to in range(2):
+                target = core * 2 + k
+                own = (chip == target) & (core == to)
+                src = wo.at[pl.ds((2 * k + to) * wo_part, wo_part)]
+                dst = rs_o.at[chip]
+                copy = remote(
+                    src, dst, rso_ss.at[2 * k + to], rso_rs.at[chip], (depth * 2 + to, target)
+                )
+                if action == "start":
+
+                    @pl.when(own)
+                    def _():
+                        pltpu.make_async_copy(src, dst, rso_rs.at[chip]).start()
+
+                @pl.when(jnp.logical_not(own))
+                def _():
+                    if action == "start":
+                        copy.start()
+                    else:
+                        copy.wait_send()
+
+    class OutChunk(Chunk):
+        def bind(self):
+            self.bind_z(self.src.at[0], self.src.at[1])
+
+        def total(self):
+            for i in range(SEQ):
+                await_copy(self.src.at[i], rso_rs.at[i])
+            value = self.src[0].astype(F32)
+            for i in range(1, SEQ):
+                value = value + self.src[i].astype(F32)
+            self.reduced[...] = value.astype(BF16)
+
+        def plane_sends(self):
+            return []
+
+    o_chunk = OutChunk(
+        rs_o, None, None, None, None, o_za, o_zb, [(None, lambda c: go_o.at[tile(c, wo_part)])]
+    )
+    rso_each("start")
+
+    sub = lax.broadcasted_iota(jnp.int32, (16, tokens), 0)
+    key_block = lax.div(lax.broadcasted_iota(jnp.int32, (16, tokens), 1), BLK)
+    flip[BLK : BLK + 16, :] = (sub == key_block).astype(BF16)
+    near[...] = jnp.zeros_like(near)
+    far[...] = jnp.zeros_like(far)
+    ds_buf[0:BLK, :] = jnp.zeros((BLK, quarter), BF16)
+    ds_buf[tokens + BLK :, :] = jnp.zeros((BLK, quarter), BF16)
+
+    q_chunks = [
+        Chunk(
+            lambda owner, p=p: gqkv.at[p, tile(owner, rows_w)],
+            q_dx.at[p],
+            q_dy.at[p],
+            q_rx.at[p],
+            q_ry.at[p],
+            q_za.at[p],
+            q_zb.at[p],
+            [
+                (
+                    pl.ds(j * BLK, BLK),
+                    lambda c, p=p, o=o: o.at[:, tile(c * 3 + p, BLK)],
+                )
+                for j, o in enumerate((gq_o, gk_o, gv_o))
+            ],
+        )
+        for p in range(3)
+    ]
+    backward_table = {
+        0: [i_chunks[3].middle],
+        1: [d_chunks[0].z_one],
+        2: [d_chunks[1].z_one],
+        3: [d_chunks[2].z_one, d_chunks[0].z_two],
+        4: [d_chunks[1].z_two],
+        5: [q_chunks[0].middle, i_chunks[0].z_one, d_chunks[2].z_two, d_chunks[0].z_three],
+        6: [i_chunks[1].z_one, d_chunks[1].z_three],
+        7: [i_chunks[0].z_two, d_chunks[2].z_three, d_chunks[0].z_four],
+        8: [i_chunks[2].z_one, i_chunks[1].z_two, d_chunks[1].z_four],
+        9: [q_chunks[1].middle, i_chunks[3].z_one, i_chunks[0].z_three, d_chunks[2].z_four],
+        10: [i_chunks[2].z_two, i_chunks[1].z_three, o_chunk.z_one],
+        11: [i_chunks[3].z_two, i_chunks[2].z_three, i_chunks[0].z_four],
+    }
+
+    @pl.loop(0, 12)
+    def _(now):
+        pair, qb = lax.div(now, 4), lax.rem(now, 4)
+
+        @pl.when(qb == 0)
+        def _():
+            flip[0:BLK, :] = jnp.transpose(qkv[:, tile(3 + pair, BLK)])
+            prepare_keys(pair)
+            dk_acc[...] = jnp.zeros_like(dk_acc)
+            dv_acc[...] = jnp.zeros_like(dv_acc)
+
+        rows = tile(qb, quarter)
+        cols = tile(pair, BLK)
+        upstream = gmix[rows, cols]
+        product = jnp.transpose(upstream.astype(F32) * mixed[rows, cols].astype(F32))
+        parts = []
+        for h in range(2):
+            head = pair * 2 + h
+            logits, queries = scores(pair, qb, h)
+            probs = jnp.exp(logits - lse[pl.ds(head, 1), rows])
+            masked = jnp.where(mine_lanes[h], upstream, jnp.zeros_like(upstream))
+            grad_probs = contract(qkv[:, tile(6 + pair, BLK)], masked, 1, 1)
+            inner = jnp.sum(product[64 * h : 64 * h + 64, :], 0, keepdims=True)
+            grad_logits = (probs * (grad_probs - inner)).astype(BF16)
+            dv_acc[...] += contract(probs.astype(BF16), masked, 1, 0)
+            dk_acc[...] += contract(grad_logits, queries, 1, 0)
+            ds_buf[BLK : tokens + BLK, :] = grad_logits
+            result = contract(flip[...], grad_logits, 1, 0)
+            parts.append(result[64 * h : 64 * h + 64, :])
+            sums = result[BLK : BLK + 8, :]
+            block_row = lax.broadcasted_iota(jnp.int32, sums.shape, 0)
+            query_block = 2 * qb + lax.div(lax.broadcasted_iota(jnp.int32, sums.shape, 1), BLK)
+            gap = block_row - query_block
+            far[head, 0:8, :] += jnp.where(gap <= -2, sums, 0.0)
+            far[head, 8:16, :] += jnp.where(gap >= 2, sums, 0.0)
+            for i in range(2):
+                for off in range(3):
+                    start = pl.multiple_of((2 * qb + i + off) * BLK, BLK)
+                    near[head * 3 + off] += ds_buf[
+                        pl.ds(start, BLK), i * BLK : (i + 1) * BLK
+                    ].astype(F32)
+        dq = jnp.transpose(jnp.concatenate(parts, axis=0)).astype(BF16)
+        dqkv[rows, cols] = dq
+        dpair[rows, 0:BLK] = dq
+
+        @pl.when(qb == 3)
+        def _():
+            for j, acc in ((1, dk_acc), (2, dv_acc)):
+                value = acc[...].astype(BF16)
+                dqkv[:, tile(3 * j + pair, BLK)] = value
+                dpair[:, j * BLK : (j + 1) * BLK] = value
+
+            @pl.loop(0, width // (2 * BLK))
+            def _(i):
+                gqkv[pair, tile(i, 2 * BLK), :] = contract(
+                    nrm1[:, tile(i, 2 * BLK)], dpair[...], 0, 0
+                ).astype(BF16)
+
+            for p in range(3):
+
+                @pl.when(pair == p)
+                def _():
+                    q_chunks[p].start()
+
+        serve(now, backward_table)
+
+    for i in range(SEQ):
+        swap_copy(i, gn2_ss, gn2_rs).wait_send()
+
+    @pl.loop(0, 2)
+    def _(i):
+        result = contract(blocks_of(dqkv, i, 1 - core), wqkv[...], 1, 1)
+        for j in range(2):
+            psend[2 * i + j] = result[j * BLK : (j + 1) * BLK, :]
+            swap_copy(2 * i + j, gn1_ss, gn1_rs).start()
+
+    q_chunks[2].middle()
+    i_chunks[3].z_three()
+    i_chunks[1].z_four()
+    o_chunk.z_two()
+    q_chunks[0].z_one()
+
+    def gx_each(i, action):
+        own = (chip == i) & (core == row)
+        dst = gx_o.at[col, tile(core, BLK)]
+        copy = remote(
+            gx_send.at[i], dst, gx_ss.at[i], gx_rs.at[col * 2 + core], (depth * 2 + row, i)
+        )
+        if action == "start":
+
+            @pl.when(own)
+            def _():
+                pltpu.make_async_copy(gx_send.at[i], dst, gx_rs.at[col * 2 + core]).start()
+
+        @pl.when(jnp.logical_not(own))
+        def _():
+            if action == "start":
+                copy.start()
+            else:
+                copy.wait_send()
+
+    @pl.loop(0, 2)
+    def _(k):
+        both = contract(blocks_of(dqkv, k, core), wqkv[...], 1, 1)
+        for j in range(2):
+            i = 2 * k + j
+            swap_copy(i, gn1_ss, gn1_rs).wait_recv()
+            normed = both[j * BLK : (j + 1) * BLK, :] + precv[i]
+            source = xown[i].astype(F32)
+            scale = lax.rsqrt(jnp.mean(source * source, -1, keepdims=True) + EPS)
+            add_gain(0, jnp.sum(normed * source * scale, 0, keepdims=True))
+            scaled = normed * gains[0:1, :]
+            inner = jnp.mean(scaled * source, -1, keepdims=True)
+            result = hid[i] + scale * scaled - source * (scale * scale * scale) * inner
+            gx_send[i] = result.astype(BF16)
+            gx_each(i, "start")
+
+    i_chunks[2].z_four()
+    o_chunk.z_three()
+    q_chunks[0].z_two()
+    q_chunks[1].z_one()
+
+    diag_row = lax.broadcasted_iota(jnp.int32, (BLK, BLK), 0)
+    diag_col = lax.broadcasted_iota(jnp.int32, (BLK, BLK), 1)
+    upper = diag_col >= diag_row
+    mirror = (diag_row + diag_col == BLK - 1).astype(F32)
+    shift = lax.broadcasted_iota(jnp.int32, (1, BLK), 1) + 1
+    shift = jnp.where(shift == BLK, 0, shift)
+    ids = bucket_of(jnp.concatenate([-shift, BLK - shift], axis=1))
+    onehot = (lax.broadcasted_iota(jnp.int32, (BLK, 2 * BLK), 0) == ids).astype(F32)
+
+    @pl.loop(0, 6)
+    def _(h):
+        def skew(x):
+            return pltpu.roll(exact(mirror, x, 1, 0), 0, 1, stride=1, stride_axis=0)
+
+        tiles = [near[h * 3 + i] for i in range(3)]
+        at = [
+            jnp.sum(
+                skew(jnp.where(upper, tiles[i + 1], 0.0) + jnp.where(upper, 0.0, tiles[i])),
+                0,
+                keepdims=True,
+            )
+            for i in range(2)
+        ]
+        below = full_sum(jnp.where(upper, tiles[0], 0.0)) + full_sum(far[h, 0:8, :])
+        above = full_sum(jnp.where(upper, 0.0, tiles[2])) + full_sum(far[h, 8:16, :])
+        sums = exact(jnp.broadcast_to(jnp.concatenate(at, axis=1), (8, 2 * BLK)), onehot, 1, 1)
+        sums = sums[0:1, :] + jnp.where(lane == 15, below, 0.0) + jnp.where(lane == 31, above, 0.0)
+        sg[pl.ds(16 + core * 6 + h, 1), :] = sums
+
+    place = core * SEQ + chip
+
+    def sgp_each(action):
+        for step in range(SEQ):
+            for cross in range(2):
+                if step == 0 and cross == 0:
+                    continue
+                to_core = lax.rem(core + cross, 2)
+                copy = remote(
+                    sg,
+                    sg_plane.at[place],
+                    sgp_ss.at[step * 2 + cross],
+                    sgp_rs.at[place],
+                    (depth * 2 + to_core, ahead(step)),
+                )
+                if action == "start":
+                    copy.start()
+                else:
+                    copy.wait_send()
+
+    sgp_each("start")
+    pltpu.make_async_copy(sg, sg_plane.at[place], sgp_rs.at[place]).start()
+    q_chunks[2].z_one()
+    q_chunks[1].z_two()
+    q_chunks[0].z_three()
+    i_chunks[3].z_four()
+    o_chunk.z_four()
+    for i in range(8):
+        await_copy(sg_plane.at[i], sgp_rs.at[i])
+    total = sg_plane[0]
+    for i in range(1, 8):
+        total = total + sg_plane[i]
+    sg_depth[depth] = total
+
+    def sgz_copy(step):
+        return remote(
+            sg_depth.at[depth],
+            sg_depth.at[depth],
+            sgz_ss.at[step],
+            sgz_rs.at[depth],
+            z_dev(lax.rem(depth + step, DEPTH)),
+        )
+
+    for step in range(1, DEPTH):
+        sgz_copy(step).start()
+    q_chunks[2].z_two()
+    q_chunks[1].z_three()
+    q_chunks[0].z_four()
+    q_chunks[2].z_three()
+    q_chunks[1].z_four()
+    q_chunks[2].z_four()
+
+    for i in range(4):
+        await_copy(pool_recv.at[i], pool_rs.at[i])
+    for doc in range(2):
+        pooled_o[doc : doc + 1, :] = (
+            pool_recv[2 * doc, 0:1, :] + pool_recv[2 * doc + 1, 0:1, :]
+        ) / own_lengths[:, doc : doc + 1]
+    for step in range(1, DEPTH):
+        z = lax.rem(depth + DEPTH - step, DEPTH)
+        await_copy(sg_depth.at[z], sgz_rs.at[z])
+    total = sg_depth[0] + sg_depth[1] + sg_depth[2] + sg_depth[3]
+    for which in range(2):
+        wide[which : which + 1, :] = jnp.concatenate(
+            [total[8 * which + i : 8 * which + i + 1, :] for i in range(width // BLK)], axis=1
+        )
+    small_o[...] = pltpu.roll(wide[...], lax.rem(width - chip * rows_w, width), 1)[:, : small_o.shape[1]]
+    turned[:, 0:16] = jnp.transpose(total[16:32, :])
+    table_o[...] = turned[tile(chip, 8), :]
+
+    for i in range(4):
+        await_copy(gx_o.at[i // 2, pl.ds((i % 2) * BLK, BLK)], gx_rs.at[i])
+    for copy in pending:
+        copy.wait_send()
+    spread(inputs, x_slot, x_ss, x_rs, "wait")
+    spread(cotangent, c_slot, c_ss, c_rs, "wait")
+    for it in qkv_items + down_items:
+        it.sent()
+    wo_each("wait")
+    pool_each("wait")
+    rso_each("wait")
+    sgp_each("wait")
+    for i in range(SEQ):
+        n1_copy(i).wait_send()
+        g_copy(i).wait_send()
+        n2_copy(i, gat_ss, gat_rs).wait_send()
+        swap_copy(i, gn1_ss, gn1_rs).wait_send()
+        gx_each(i, "wait")
+    for step in range(1, DEPTH):
+        sgz_copy(step).wait_send()
+    for chunk in (*d_chunks, *i_chunks, o_chunk, *q_chunks):
+        chunk.finish()
+
+
+def widen_kernel(pooled, small, table, gx, gq, gk, gv, go, gi, gd, *outs):
+    pooled_out, one_out, two_out, table_out, *outs = outs
+    pooled_out[...] = pooled[...]
+    one_out[...] = small[0:1, : one_out.shape[1]]
+    two_out[...] = small[1:2, : two_out.shape[1]]
+    table_out[...] = table[:, : table_out.shape[1]]
+    for value, out in zip((gx, gq, gk, gv, go, gi, gd), outs):
+        out[...] = value[...].astype(F32)
 
 
 def on_device(
@@ -272,6 +1498,178 @@
     )
 
 
+def fused_on_device(
+    inputs,
+    w_query,
+    w_key,
+    w_value,
+    w_out,
+    w_ffn_in,
+    w_ffn_out,
+    attn_gain,
+    ffn_gain,
+    rel_bias,
+    doc_lengths,
+    cotangent,
+):
+    docs, shard_len, width = inputs.shape
+    rows_w, hidden_units = w_ffn_in.shape
+    tokens = shard_len * SEQ
+    half = width // 2
+    part = hidden_units // (2 * SEQ)
+    blocks = tokens // BLK
+    pairs = half // BLK
+    parts = part // BLK
+    heads = rel_bias.shape[1]
+    gains = jnp.stack([attn_gain, ffn_gain]).astype(F32)
+    anywhere = pl.BlockSpec(memory_space=pl.ANY)
+    vmem = pl.BlockSpec(memory_space=pltpu.VMEM)
+    smem = pl.BlockSpec(memory_space=pltpu.SMEM)
+    shape = jax.ShapeDtypeStruct
+    narrow = [
+        (docs, shard_len, width),
+        (rows_w, width),
+        (rows_w, width),
+        (rows_w, width),
+        (rows_w, width),
+        (rows_w, hidden_units),
+        (2 * part, width),
+    ]
+    out_shape = (
+        shape((docs, width), F32),
+        shape((8, 2 * BLK), F32),
+        shape((8, BLK), F32),
+        *(shape(s, BF16) for s in narrow),
+    )
+    quarter = tokens // 4
+    out_part = rows_w // 2
+
+    def sums(count, size, columns):
+        return [((count, size // 2, columns), BF16)] * 2 + [((count, size, columns), BF16)] * 4
+
+    scratch = [
+        ((SEQ, BLK, width), BF16),
+        ((blocks, BLK, width), BF16),
+        ((tokens, width), BF16),
+        ((width, 3 * half), BF16),
+        ((tokens, 3 * half), BF16),
+        ((tokens, half), BF16),
+        ((half, width), BF16),
+        ((SEQ, BLK, width), F32),
+        ((SEQ, BLK, width), F32),
+        ((SEQ, BLK, width), F32),
+        ((tokens, width), BF16),
+        ((width, SEQ * part), BF16),
+        ((SEQ * part, width), BF16),
+        ((tokens, SEQ * part), BF16),
+        ((tokens, SEQ * part), BF16),
+        ((tokens, part), BF16),
+        ((tokens, width), F32),
+        ((2 * pairs, 2 * tokens - BLK, BLK), F32),
+        ((3, 16, 2 * BLK), F32),
+        ((tokens, BLK), BF16),
+        ((2, tokens, BLK), BF16),
+        ((8, tokens), F32),
+        ((BLK + 16, tokens), BF16),
+        ((tokens, 3 * half), BF16),
+        ((tokens, 3 * BLK), BF16),
+        ((tokens, half), BF16),
+        ((tokens, BLK), F32),
+        ((tokens, BLK), F32),
+        ((tokens + 2 * BLK, quarter), BF16),
+        ((6 * pairs, BLK, BLK), F32),
+        ((2 * pairs, 16, quarter), F32),
+        ((pairs, width, 3 * BLK), BF16),
+        ((parts, SEQ, BLK, width), BF16),
+        *sums(parts, BLK, width),
+        *sums(SEQ, rows_w, part),
+        *sums(pairs, rows_w, 3 * BLK),
+        ((SEQ, out_part, width), BF16),
+        ((out_part, width), BF16),
+        ((out_part, width), BF16),
+        ((SEQ, BLK, width), BF16),
+        ((SEQ + 1, 48, BLK), F32),
+        ((8, width), F32),
+        ((8, width), F32),
+        ((8, SEQ * part), F32),
+        ((8, width), F32),
+        ((4, 8, width), F32),
+        ((32, BLK), F32),
+        ((8, 32, BLK), F32),
+        ((4, 32, BLK), F32),
+        ((BLK, BLK), F32),
+    ]
+    chunks = parts + SEQ + pairs + 1
+    pair_of = lambda *dims: [pltpu.SemaphoreType.DMA(dims)] * 2
+    semaphores = (
+        pair_of(5)
+        + pair_of(4)
+        + pair_of(4)
+        + pair_of(6, 5)
+        + pair_of(4)
+        + pair_of(4) * 8
+        + pair_of(chunks, 6)
+        + pair_of(4)
+        + pair_of(chunks, 6)
+        + pair_of(4)
+        + pair_of(8)
+        + pair_of(4)
+        + [pltpu.SemaphoreType.DMA((chunks, 3))]
+    )
+    results = pl.pallas_call(
+        fused_kernel,
+        out_shape=out_shape,
+        in_specs=[anywhere] * 8 + [vmem, vmem, smem],
+        out_specs=(vmem, vmem, vmem) + (anywhere,) * 7,
+        scratch_shapes=[pltpu.VMEM(*s) for s in scratch] + semaphores,
+        compiler_params=pltpu.CompilerParams(
+            collective_id=0, has_side_effects=True, vmem_limit_bytes=VMEM_LIMIT
+        ),
+        name="block",
+    )(
+        inputs,
+        cotangent,
+        w_query,
+        w_key,
+        w_value,
+        w_out,
+        w_ffn_in,
+        w_ffn_out,
+        gains,
+        rel_bias,
+        doc_lengths,
+    )
+
+    steps = 4
+
+    def rows_spec(s):
+        if len(s) == 3:
+            return pl.BlockSpec(
+                (1, s[1] * s[0] // steps, s[2]),
+                lambda i: (i // (steps // s[0]), i % (steps // s[0]), 0),
+            )
+        return pl.BlockSpec((s[0] // steps, s[1]), lambda i: (i, 0))
+
+    def whole_spec(s):
+        return pl.BlockSpec(s, lambda i: (0,) * len(s))
+
+    tiny = [(docs, width), (1, rows_w), (1, rows_w), (8, heads)]
+    pooled, one, two, table, gx, gq, gk, gv, go, gi, gd = pl.pallas_call(
+        widen_kernel,
+        out_shape=[shape(s, F32) for s in tiny + narrow],
+        grid=(steps,),
+        in_specs=[whole_spec(r.shape) for r in results[:3]] + [rows_spec(s) for s in narrow],
+        out_specs=[whole_spec(s) for s in tiny] + [rows_spec(s) for s in narrow],
+        compiler_params=pltpu.CompilerParams(vmem_limit_bytes=VMEM_LIMIT),
+        name="widen",
+    )(*results)
+    return (pooled, gx, gq, gk, gv, go, gi, gd, one[0], two[0], table)
+
+
+def fits(mesh):
+    return mesh.shape["dp"] == CORES * DEPTH and mesh.shape["seq"] == SEQ
+
+
 def solution(mesh):
     in_specs = (
         P("dp", "seq", None),
@@ -301,5 +1699,5 @@
         P("seq", None),
     )
     return jax.shard_map(
-        on_device, mesh=mesh, in_specs=in_specs, out_specs=out_specs, check_vma=False
-    )
+        fused_on_device if fits(mesh) else on_device, mesh=mesh, in_specs=in_specs, out_specs=out_specs, check_vma=False
+    )

time: 845 us -> 205 us (0.24)
  waiting for transfers between devices: 400 us -> 0 us
  Pallas kernels: 0 us -> 202 us
  matrix products: 163 us -> 0 us
  local copies, waits for them, and re-layouts: 112 us -> 1.32 us
  other arithmetic: 87.8 us -> 0.59 us
  blocking collectives: 58.6 us -> 0 us
  between operations: 16.7 us -> 0.81 us
    reduce_scatter x8 -> x0, waiting for transfers between devices: 220 us -> none  [the longest x1 60 us: on_device(): lax.psum_scatter(grad_in.astype(jnp.bfloat16), 'seq', scatter_dimension=0...]
    pallas_call x0 -> x2, Pallas kernels: none -> 202 us  [the longest x1 196 us: fused_on_device(): pl.pallas_call(fused_kernel, out_shape=out_shape, in_specs=[anywhere] * 8...]
    dot_general x26 -> x0, matrix products: 163 us -> none  [the longest x6 26.4 us: outer_sum(): lax.dot_general(left, right, (((0,), (0,)), ((), ())), preferred_element_...]
    all_gather x8 -> x0, waiting for transfers between devices: 128 us -> none  [the longest x1 50.7 us: on_device(): lax.all_gather(w_ffn_out, 'seq', axis=0, tiled=True)]
    psum x1 -> x0, waiting for transfers between devices: 48.3 us -> none  [on_device(): lax.psum(shards[0].astype(jnp.bfloat16), 'dp').astype(jnp.float32)]
    eq x1 -> x0, local copies, waits for them, and re-layouts: 46.5 us -> none  [on_device(): bucket_ids(query_pos, key_pos)[:, :, None] == bucket_range]
    reduce_sum x3 -> x0, other arithmetic: 46.1 us -> none  [the longest x1 30.5 us: on_device(): jnp.einsum('bhqk,qkn->nh', grad_logits, onehot, preferred_element_type=jn...]
    convert_element_type x17 -> x1, other arithmetic: 27.8 us -> 0.59 us  [fused_on_device(): gains = jnp.stack([attn_gain, ffn_gain]).astype(F32)]
  transfers between devices with their start and end apart: 17 -> 0, of which waited for: 12 -> 0; matrix products, arithmetic and copies ran while one was open for 36% -> 0% of each run, Pallas kernels for 0% -> 0%
where the time goes in v2:
time: 205 us; the launch traced here: 204 us
  Pallas kernels  202 us (99%)
    pallas_call x1, Pallas kernels, fused_on_device(): pl.pallas_call(fused_kernel, out_shape=out_shape, in_specs=[anywhere] * 8...  196 us
    pallas_call x1, Pallas kernels, fused_on_device(): pl.pallas_call(widen_kernel, out_shape=[shape(s, F32) for s in tiny + nar...  6 us

profile of v2, /device:TPU:0, one launch (start us, length us, event | category | flops | bytes accessed | tf_op | source)
XLA Modules:
  0.0 204.3 jit_solution(14013635386557234782)
XLA Ops:
  0.6 0.7 stack.9
  1.3 0.7 stack.10
  2.0 0.6 maximum_convert_fusion.gains_in
  2.5 195.6 %block.1 = (f32[2,768]{1,0:T(2,128)}, f32[8,256]{1,0:T(8,128)}, f32[8,128]{1,0:T(8,128)}, bf16[2,256,768]{2,1,0:T(8,128)(2,1)}, bf16[192,768]{1,0:T(8,128)(2,1)}...) custom-call(bf16[2,256,768]{2,1,0:T(8,128)(2,1)} %inputs.1, ...), custom_call_target="tpu_custom_call" | custom-call | tf_op jit(solution)/shard_map/block/pallas_call | solution.py:1619
  198.1 6.0 %widen.1 = (f32[2,768]{1,0:T(2,128)}, f32[1,192]{1,0:T(1,128)}, f32[1,192]{1,0:T(1,128)}, f32[8,12]{1,0:T(8,128)}, f32[2,256,768]{2,1,0:T(8,128)}, /*index=5*/f3...) custom-call(f32[2,768]{1,0:T(2,128)} %get-tuple-element.32.pooled, ...), custom_call_target="tpu_custom_call" | custom-call | tf_op jit(solution)/shard_map/widen/pallas_call | solution.py:1657

commit v3 on v2

--- a/solution.py
+++ b/solution.py
@@ -119,6 +119,7 @@
     go_o,
     gi_o,
     gd_o,
+    raised_o,
     xown,
     grads,
     nrm1,
@@ -134,20 +135,16 @@
     wd,
     act,
     slope,
-    gpre,
     gn,
     strip,
     vecs,
     maskc,
-    kaug,
-    lse,
+    gscale,
     flip,
     dqkv,
-    dpair,
     gmix,
     dk_acc,
     dv_acc,
-    ds_buf,
     near,
     far,
     gqkv,
@@ -173,7 +170,6 @@
     rs_o,
     o_za,
     o_zb,
-    gx_send,
     small_all,
     wide,
     gains,
@@ -223,6 +219,7 @@
     sgz_ss,
     sgz_rs,
     out_s,
+    raised_s,
 ):
     dp = lax.axis_index("dp")
     chip = lax.axis_index("seq")
@@ -235,8 +232,9 @@
     tokens, width = nrm1.shape
     half = width // 2
     rows_w = w_query.shape[0]
-    ff_part = gpre.shape[1]
-    quarter = tokens // 4
+    ff_part = gdn.shape[0] * BLK
+    quarter, middle_q = tokens // 4, tokens // 2
+    middle_w = width // 2
 
     def remote(src, dst, send, recv, device):
         return pltpu.make_async_remote_copy(
@@ -377,6 +375,66 @@
             await_copy(self.own, wg_ss.at[k, 0])
             await_copy(self.own, wg_ss.at[k, 1])
 
+    class SharedGather(Gather):
+        def part(self, owner, which):
+            ref = self.place(owner)
+            size = ref.shape[0] // 2
+            return ref.at[tile(which, size)]
+
+        def bind(self):
+            k = self.index
+            mine, theirs = lax.rem(depth, 2), 1 - lax.rem(depth, 2)
+            beside = ((depth + theirs - mine) * 2 + core, chip)
+            self.local, self.one = [], []
+            for src, cut in self.pieces:
+                size = src.shape[0] // 2
+                self.local.append(
+                    pltpu.make_async_copy(src, cut(self.place(chip)), wg_rs.at[k, 0])
+                )
+                dst = cut(self.part(chip, mine))
+                src = src.at[tile(mine, size)]
+                self.one.append(remote(src, dst, wg_ss.at[k, 0], wg_rs.at[k, 1], (dp, xn)))
+                self.one.append(remote(src, dst, wg_ss.at[k, 1], wg_rs.at[k, 2], (dp, yn)))
+            self.from_x, self.from_y = self.part(xn, mine), self.part(yn, mine)
+            far = self.part(dn, mine)
+            size = far.shape[0] // 2
+            cut = lambda ref, which: ref.at[pl.ds(which * size, size)]
+            via_x, via_y = cut(self.from_x, 1), cut(self.from_y, 0)
+            self.last = [cut(far, 1), cut(far, 0)]
+            self.two = [
+                remote(via_x, via_x, wg_ss.at[k, 2], wg_rs.at[k, 3], (dp, yn)),
+                remote(via_y, via_y, wg_ss.at[k, 3], wg_rs.at[k, 4], (dp, xn)),
+            ]
+            self.beside = [
+                remote(ref, ref, wg_ss.at[k, 4 + n], wg_rs.at[k, 5 + n], beside)
+                for n, ref in enumerate((self.from_x, self.from_y, far))
+            ]
+            self.own = self.place(chip)
+            self.half = self.part(chip, mine)
+
+        def second(self):
+            super().second()
+            for copy in self.beside[:2]:
+                copy.start()
+
+        def third(self):
+            k = self.index
+            await_copy(self.last[0], wg_rs.at[k, 3])
+            await_copy(self.last[1], wg_rs.at[k, 4])
+            self.beside[2].start()
+
+        def done(self):
+            await_copy(self.own, wg_rs.at[self.index, 0])
+            for copy in self.beside:
+                copy.wait_recv()
+
+        def sent(self):
+            k = self.index
+            for copy in self.two + self.beside:
+                copy.wait_send()
+            await_copy(self.half, wg_ss.at[k, 0])
+            await_copy(self.half, wg_ss.at[k, 1])
+
     core_cols = tile(core, half)
     whole = lambda ref: ref
     row_half = rows_w // 2
@@ -397,7 +455,7 @@
         )
 
     def in_item(index, part):
-        return Gather(
+        return SharedGather(
             index,
             [
                 (
@@ -411,7 +469,7 @@
 
     def down_item(index, part):
         size = ff_part // 2
-        return Gather(
+        return (SharedGather if part == 0 else Gather)(
             index,
             [(w_down.at[pl.ds(pl.multiple_of(core * ff_part + part * size, size), size)], whole)],
             lambda owner: wd.at[
@@ -471,18 +529,16 @@
         values = [vecs[i, pl.ds(core * 6 + h, 1), :] for i in range(3)]
         left = jnp.broadcast_to(values[0][:, BLK - 1 : BLK], (BLK, BLK))
         right = jnp.broadcast_to(values[2][:, BLK + 1 : BLK + 2], (BLK, BLK))
-        for i in range(6):
-            strip[h, i * BLK : (i + 1) * BLK, :] = left
-            strip[h, (i + 9) * BLK : (i + 10) * BLK, :] = right
+        strip[h, 0:BLK, :] = left
+        strip[h, 4 * BLK :, :] = right
         for i in range(3):
             skewed = pltpu.roll(
                 jnp.broadcast_to(values[i], (BLK, 2 * BLK)), 0, 1, stride=1, stride_axis=0
             )
-            strip[h, (i + 6) * BLK : (i + 7) * BLK, :] = skewed[:, :BLK]
-
-    maskc[...] = jnp.where(
-        lax.broadcasted_iota(jnp.int32, maskc.shape, 0).astype(F32) < length, 0.0, NEGATIVE
-    ).astype(BF16)
+            strip[h, (i + 1) * BLK : (i + 2) * BLK, :] = skewed[:, :BLK]
+
+    key_pos = lax.broadcasted_iota(jnp.int32, maskc.shape, 0).astype(F32)
+    maskc[...] = jnp.where((key_pos < length) | (lane > 0), 0.0, NEGATIVE).astype(BF16)
 
     def block_valid(b):
         pos = lax.broadcasted_iota(jnp.int32, (BLK, 1), 0) + b * BLK
@@ -500,8 +556,8 @@
         nrm1[tile(2 * i + core, BLK), :] = (source * scale * gains[0:1, :]).astype(BF16)
         n1_copy(i).start()
 
-    for it in qkv_items:
-        it.second()
+    qkv_items[0].second()
+    qkv_items[1].second()
     wo_each("start")
     for it in in_items:
         it.first()
@@ -517,24 +573,12 @@
 
     flip[BLK : BLK + 16, :] = jnp.ones((16, tokens), BF16)
     mine_lanes = [lane < 64, lane >= 64]
-    spare = [lane == 64, lane == 0]
-
-    def prepare_keys(pair):
-        keys = qkv[:, tile(3 + pair, BLK)]
-        for h in range(2):
-            kaug[h] = jnp.where(mine_lanes[h], keys, jnp.where(spare[h], maskc[...], 0))
-
-    def scores(pair, qb, h):
-        queries = qkv[tile(qb, quarter), tile(pair, BLK)]
-        plain = jnp.where(mine_lanes[h], queries, jnp.zeros_like(queries))
-        raised = jnp.where(spare[h], jnp.ones_like(queries), plain)
-        raw = contract(kaug[h], raised, 1, 1)
-        head = pair * 2 + h
-        biases = [
-            strip[head, pl.ds(pl.multiple_of((7 - 2 * qb - i) * BLK, BLK), tokens), :]
-            for i in range(2)
-        ]
-        return raw + jnp.concatenate(biases, axis=1), plain
+    slots = [ref.at[:, pl.ds(0, tokens)] for ref in (act, slope)]
+
+    def by_head(value):
+        return jnp.concatenate(
+            [jnp.where(lanes, value, jnp.zeros_like(value)) for lanes in mine_lanes], axis=0
+        )
 
     def serve(now, table):
         for when, actions in table.items():
@@ -544,77 +588,104 @@
                 for action in actions:
                     action()
 
-    def forward_in_tail():
-        in_items[1].second()
+    def keep(pair, qb):
+        return pltpu.make_async_copy(slots[qb], raised_o.at[2 * pair + qb], raised_s.at[qb])
+
+    def fetch(pair, qb):
+        return pltpu.make_async_copy(raised_o.at[2 * pair + qb], slots[qb], raised_s.at[qb])
+
+    def later_inputs():
         spread(cotangent, c_slot, c_ss, c_rs, "start")
         for it in down_items:
             it.first()
 
-    @pl.loop(0, 12)
-    def _(now):
-        pair, qb = lax.div(now, 4), lax.rem(now, 4)
-
-        @pl.when(qb == 0)
-        def _():
-            flip[0:BLK, :] = jnp.transpose(qkv[:, tile(6 + pair, BLK)])
-            prepare_keys(pair)
-
-        parts = []
-        for h in range(2):
-            logits, _ = scores(pair, qb, h)
+    forward_table = {
+        2: [in_items[0].second],
+        3: [in_items[1].second, later_inputs],
+        4: [in_items[0].third],
+    }
+
+    @pl.loop(0, 3)
+    def _(pair):
+        cols = tile(pair, BLK)
+        flip[0:BLK, :] = jnp.transpose(qkv[:, tile(6 + pair, BLK)])
+        keys = jnp.concatenate([qkv[:, tile(3 + pair, BLK)], maskc[...]], axis=1)
+        for qb in range(2):
+            rows = pl.ds(qb * middle_q, middle_q)
+            queries = by_head(qkv[rows, cols])
+            flag = jnp.broadcast_to(jnp.where(lane == 0, 1.0, 0.0).astype(BF16), queries.shape)
+            biases = [
+                jnp.concatenate(
+                    [
+                        strip[
+                            pair * 2 + h, pl.ds((min(max(kb - q, -2), 2) + 2) * BLK, BLK), :
+                        ]
+                        for kb in range(tokens // BLK)
+                    ],
+                    axis=0,
+                )
+                for h in range(2)
+                for q in range(qb * middle_q // BLK, (qb + 1) * middle_q // BLK)
+            ]
+            logits = contract(keys, jnp.concatenate([queries, flag], axis=1), 1, 1)
+            logits = logits + jnp.concatenate(biases, axis=1)
             highest = jnp.max(logits, 0, keepdims=True)
             raised = jnp.exp(logits - highest).astype(BF16)
+
+            @pl.when(pair > 0)
+            def _():
+                keep(pair - 1, qb).wait()
+
+            slots[qb][...] = raised
+            keep(pair, qb).start()
             result = contract(flip[...], raised, 1, 0)
-            total = result[BLK : BLK + 1, :]
-            lse[pl.ds(pair * 2 + h, 1), tile(qb, quarter)] = highest + jnp.log(total)
-            parts.append(result[64 * h : 64 * h + 64, :] / total)
-        mixed[tile(qb, quarter), tile(pair, BLK)] = jnp.transpose(
-            jnp.concatenate(parts, axis=0)
-        ).astype(BF16)
-        serve(now, {5: [in_items[0].second], 9: [forward_in_tail]})
+            inverse = 1.0 / result[BLK : BLK + 1, :]
+            scaled = result[0:BLK, :] * inverse
+            mixed[rows, cols] = jnp.transpose(
+                jnp.concatenate([scaled[0:64, 0:middle_q], scaled[64:BLK, middle_q:]], axis=0)
+            ).astype(BF16)
+            for h in range(2):
+                gscale[pl.ds(2 * pair + h, 1), rows] = inverse[:, h * middle_q : (h + 1) * middle_q]
+            serve(2 * pair + qb, forward_table)
 
     def swap_copy(i, send, recv):
         return remote(psend.at[i], precv.at[i], send.at[i], recv.at[i], other)
 
+    in_items[1].third()
     for k in range(4):
         await_copy(wo.at[pl.ds(k * wo_part, wo_part)], wo_rs.at[k])
 
-    def blocks_of(ref, i, parity):
+    def blocks_of(ref, parity):
         return jnp.concatenate(
-            [ref[tile(2 * (2 * i + j) + parity, BLK), :] for j in range(2)], axis=0
+            [ref[tile(2 * i + parity, BLK), :] for i in range(SEQ)], axis=0
         )
 
-    @pl.loop(0, 2)
-    def _(i):
-        result = contract(blocks_of(mixed, i, 1 - core), wo[...], 1, 0)
-        for j in range(2):
-            psend[2 * i + j] = result[j * BLK : (j + 1) * BLK, :]
-            swap_copy(2 * i + j, part_ss, part_rs).start()
+    def swap_out(result, send, recv):
+        for i in range(SEQ):
+            psend[i] = result[i * BLK : (i + 1) * BLK, :]
+            swap_copy(i, send, recv).start()
+
+    swap_out(contract(blocks_of(mixed, 1 - core), wo[...], 1, 0), part_ss, part_rs)
 
     def n2_copy(i, send, recv):
         block = nrm2.at[tile(2 * i + core, BLK)]
         return remote(block, block, send.at[i], recv.at[i], other)
 
     pp[...] = jnp.zeros_like(pp)
-
-    @pl.loop(0, 2)
-    def _(k):
-        result = contract(blocks_of(mixed, k, core), wo[...], 1, 0)
-        for j in range(2):
-            i = 2 * k + j
-            hidden = xown[i].astype(F32) + result[j * BLK : (j + 1) * BLK, :]
-            swap_copy(i, part_ss, part_rs).wait_recv()
-            hidden = hidden + precv[i]
-            hid[i] = hidden
-            scale = lax.rsqrt(jnp.mean(hidden * hidden, -1, keepdims=True) + EPS)
-            nrm2[tile(2 * i + core, BLK), :] = (hidden * scale * gains[1:2, :]).astype(BF16)
-            n2_copy(i, n2_ss, n2_rs).start()
-            pp[0:1, :] += jnp.sum(hidden * block_valid(2 * i + core), 0, keepdims=True)
-
-    for it in in_items:
-        it.done()
+    result = contract(blocks_of(mixed, core), wo[...], 1, 0)
+    for i in range(SEQ):
+        hidden = xown[i].astype(F32) + result[i * BLK : (i + 1) * BLK, :]
+        swap_copy(i, part_ss, part_rs).wait_recv()
+        hidden = hidden + precv[i]
+        hid[i] = hidden
+        scale = lax.rsqrt(jnp.mean(hidden * hidden, -1, keepdims=True) + EPS)
+        nrm2[tile(2 * i + core, BLK), :] = (hidden * scale * gains[1:2, :]).astype(BF16)
+        n2_copy(i, n2_ss, n2_rs).start()
+        pp[0:1, :] += jnp.sum(hidden * block_valid(2 * i + core), 0, keepdims=True)
     for i in range(SEQ):
         n2_copy(i, n2_ss, n2_rs).wait_recv()
+    for qb in range(2):
+        keep(2, qb).wait()
 
     def g_copy(i):
         block = grads.at[2 * i + core]
@@ -629,29 +700,33 @@
             g_copy(i).start()
 
     asum[...] = jnp.zeros_like(asum)
-
-    @pl.loop(0, 16)
-    def _(now):
-        f, i = lax.div(now, 4), lax.rem(now, 4)
-        rows, f_cols = tile(i, quarter), tile(f, ff_part)
-        value = contract(nrm2[rows, :], wi[:, f_cols], 1, 0)
-        square = value * value
-        tangent = jnp.tanh(GELU_C * (value + GELU_K * value * square))
-        half_up = 0.5 * (1.0 + tangent)
-        active = (value * half_up).astype(BF16)
-        act[rows, f_cols] = active
-        slope[rows, f_cols] = (
-            half_up
-            + 0.5
-            * value
-            * (1.0 - tangent * tangent)
-            * GELU_C
-            * (1.0 + 3.0 * GELU_K * square)
-        ).astype(BF16)
-        pos = lax.broadcasted_iota(jnp.int32, (8, quarter), 1) + i * quarter
-        valid = (pos.astype(F32) < length).astype(BF16)
-        asum[:, f_cols] += contract(valid, active, 1, 0)
-        serve(now, {11: [take_cotangent], 15: [down_items[0].second]})
+    wide_part = 2 * ff_part
+    for part in range(2):
+        part_cols = slice(part * wide_part, (part + 1) * wide_part)
+        if part == 1:
+            down_items[0].second()
+            take_cotangent()
+        in_items[part].done()
+
+        @pl.loop(0, 2)
+        def _(i):
+            rows = tile(i, middle_q)
+            value = contract(nrm2[rows, :], wi[:, part_cols], 1, 0)
+            square = value * value
+            tangent = jnp.tanh(value * (GELU_C + GELU_C * GELU_K * square))
+            half_up = 0.5 + 0.5 * tangent
+            active = (value * half_up).astype(BF16)
+            act[rows, part_cols] = active
+            slope[rows, part_cols] = (
+                half_up
+                + value
+                * (1.0 - tangent * tangent)
+                * (0.5 * GELU_C + 1.5 * GELU_C * GELU_K * square)
+            ).astype(BF16)
+            pos = lax.broadcasted_iota(jnp.int32, (8, middle_q), 1) + i * middle_q
+            valid = (pos.astype(F32) < length).astype(BF16)
+            asum[:, part_cols] += contract(valid, active, 1, 0)
+
 
     for i in range(SEQ):
         g_copy(i).wait_recv()
@@ -813,27 +888,27 @@
             axis=1,
         )
         gdn[i] = contract(columns, g_all(), 0, 0).astype(BF16).reshape(SEQ, BLK, width)
-        if i == 1:
+        if i == 0:
             down_items[1].second()
-            d_chunks[0].start()
-            d_chunks[1].start()
-    d_chunks[2].start()
+    down_items[0].third()
+    for chunk in d_chunks:
+        chunk.start()
     for it in down_items:
         it.done()
     for it in in_items:
         it.sent()
 
-    def pooled_part(f):
-        cols = slice(f * ff_part, (f + 1) * ff_part)
+    def pooled_part(cols):
         total = asum[0:1, cols]
         high = total.astype(BF16)
         rest = total - high.astype(F32)
         middle = rest.astype(BF16)
         low = (rest - middle.astype(F32)).astype(BF16)
-        for piece in (high, middle, low):
-            pp[0:1, :] += contract(jnp.broadcast_to(piece, (16, ff_part)), wd[cols, :], 1, 0)[
-                0:1, :
-            ]
+        pieces = jnp.concatenate(
+            [jnp.broadcast_to(piece, (16, piece.shape[1])) for piece in (high, middle, low)], axis=0
+        )
+        result = contract(pieces, wd[cols, :], 1, 0)
+        pp[0:1, :] += result[0:1, :] + result[16:17, :] + result[32:33, :]
 
     i_chunks = [
         Chunk(
@@ -848,36 +923,38 @@
         )
         for f in range(SEQ)
     ]
-    for f in range(SEQ):
-        f_cols = slice(f * ff_part, (f + 1) * ff_part)
-
-        @pl.loop(0, 4)
+    for part in range(2):
+        part_cols = slice(part * wide_part, (part + 1) * wide_part)
+
+        @pl.loop(0, 2)
         def _(i):
-            rows = tile(i, quarter)
-            upstream = grads[pl.ds(2 * i, 2)].reshape(quarter, width)
-            grad = contract(upstream, wd[f_cols, :], 1, 1) * slope[rows, f_cols].astype(F32)
-            grad = grad.astype(BF16)
-            gpre[rows, :] = grad
-            back = contract(grad, wi[:, f_cols], 1, 1)
-            if f == 0:
-                gn[rows, :] = back
-            else:
-                gn[rows, :] += back
-
-        pooled_part(f)
+            rows = tile(i, middle_q)
+            upstream = grads[pl.ds(4 * i, 4)].reshape(middle_q, width)
+            grad = contract(upstream, wd[part_cols, :], 1, 1) * slope[rows, part_cols].astype(F32)
+            slope[rows, part_cols] = grad.astype(BF16)
+
+        pooled_part(part_cols)
+
+    d_chunks[0].middle()
+
+    for i in range(SEQ):
+        swap_copy(i, part_ss, part_rs).wait_send()
+    swap_out(contract(blocks_of(slope, 1 - core), wi[...], 1, 1), gn2_ss, gn2_rs)
+    gn[...] = contract(blocks_of(slope, core), wi[...], 1, 1).reshape(SEQ, BLK, width)
+    d_chunks[1].middle()
+    for part in range(2):
+        part_cols = slice(part * wide_part, (part + 1) * wide_part)
 
         @pl.loop(0, width // (2 * BLK))
         def _(i):
-            wi[tile(i, 2 * BLK), f_cols] = contract(
-                nrm2[:, tile(i, 2 * BLK)], gpre[...], 0, 0
+            wi[tile(i, 2 * BLK), part_cols] = contract(
+                nrm2[:, tile(i, 2 * BLK)], slope[:, part_cols], 0, 0
             ).astype(BF16)
 
-        if f < 3:
-            d_chunks[f].middle()
-        if f:
-            i_chunks[f - 1].middle()
-        i_chunks[f].start()
-
+        if part == 1:
+            d_chunks[2].middle()
+        i_chunks[2 * part].start()
+        i_chunks[2 * part + 1].start()
     def pool_each(action):
         for to in range(SEQ):
             own = (chip == to) & (core == row)
@@ -896,15 +973,12 @@
                 else:
                     copy.wait_send()
 
+    def gat_copy(i):
+        block = act.at[tile(2 * i + core, BLK), pl.ds(0, width)]
+        return remote(block, block, gat_ss.at[i], gat_rs.at[i], other)
+
     for i in range(SEQ):
-        swap_copy(i, part_ss, part_rs).wait_send()
         n2_copy(i, n2_ss, n2_rs).wait_send()
-
-    @pl.loop(0, SEQ)
-    def _(i):
-        psend[i] = gn[tile(2 * i + 1 - core, BLK), :]
-        swap_copy(i, gn2_ss, gn2_rs).start()
-
     sg[...] = jnp.zeros_like(sg)
 
     def add_gain(first, value):
@@ -915,7 +989,7 @@
     def _(i):
         b = 2 * i + core
         swap_copy(i, gn2_ss, gn2_rs).wait_recv()
-        normed = gn[tile(b, BLK), :] + precv[i]
+        normed = gn[i] + precv[i]
         hidden = hid[i]
         scale = lax.rsqrt(jnp.mean(hidden * hidden, -1, keepdims=True) + EPS)
         add_gain(8, jnp.sum(normed * hidden * scale, 0, keepdims=True))
@@ -923,19 +997,40 @@
         inner = jnp.mean(scaled * hidden, -1, keepdims=True)
         result = grads[b].astype(F32) + scale * scaled - hidden * (scale * scale * scale) * inner
         hid[i] = result
-        nrm2[tile(b, BLK), :] = result.astype(BF16)
-        n2_copy(i, gat_ss, gat_rs).start()
+        act[tile(b, BLK), 0:width] = result.astype(BF16)
+        gat_copy(i).start()
 
     pool_each("start")
+    d_chunks[0].z_one()
     for i in range(SEQ):
-        n2_copy(i, gat_ss, gat_rs).wait_recv()
-
-    @pl.loop(0, 4)
+        gat_copy(i).wait_recv()
+
+    @pl.loop(0, 2)
     def _(i):
-        rows = tile(i, quarter)
-        gmix[rows, :] = contract(nrm2[rows, :], wo[...], 1, 1).astype(BF16)
-
-    wo[...] = contract(mixed[...], nrm2[...], 0, 0).astype(BF16)
+        rows = tile(i, middle_q)
+        inverse = jnp.concatenate(
+            [
+                jnp.transpose(
+                    jnp.concatenate(
+                        [
+                            jnp.broadcast_to(gscale[2 * p + h : 2 * p + h + 1, rows], (64, middle_q))
+                            for h in range(2)
+                        ],
+                        axis=0,
+                    )
+                )
+                for p in range(3)
+            ],
+            axis=1,
+        )
+        gmix[rows, :] = (contract(act[rows, 0:width], wo[...], 1, 1) * inverse).astype(BF16)
+
+    wo[...] = contract(mixed[...], act[:, 0:width], 0, 0).astype(BF16)
+    for i in range(SEQ):
+        gat_copy(i).wait_send()
+    for qb in range(2):
+        fetch(0, qb).start()
+    d_chunks[1].z_one()
 
     def rso_each(action):
         for k in range(2):
@@ -978,15 +1073,12 @@
     o_chunk = OutChunk(
         rs_o, None, None, None, None, o_za, o_zb, [(None, lambda c: go_o.at[tile(c, wo_part)])]
     )
-    rso_each("start")
 
     sub = lax.broadcasted_iota(jnp.int32, (16, tokens), 0)
     key_block = lax.div(lax.broadcasted_iota(jnp.int32, (16, tokens), 1), BLK)
     flip[BLK : BLK + 16, :] = (sub == key_block).astype(BF16)
     near[...] = jnp.zeros_like(near)
     far[...] = jnp.zeros_like(far)
-    ds_buf[0:BLK, :] = jnp.zeros((BLK, quarter), BF16)
-    ds_buf[tokens + BLK :, :] = jnp.zeros((BLK, quarter), BF16)
 
     q_chunks = [
         Chunk(
@@ -1008,113 +1100,120 @@
         for p in range(3)
     ]
     backward_table = {
-        0: [i_chunks[3].middle],
-        1: [d_chunks[0].z_one],
-        2: [d_chunks[1].z_one],
-        3: [d_chunks[2].z_one, d_chunks[0].z_two],
-        4: [d_chunks[1].z_two],
-        5: [q_chunks[0].middle, i_chunks[0].z_one, d_chunks[2].z_two, d_chunks[0].z_three],
-        6: [i_chunks[1].z_one, d_chunks[1].z_three],
-        7: [i_chunks[0].z_two, d_chunks[2].z_three, d_chunks[0].z_four],
-        8: [i_chunks[2].z_one, i_chunks[1].z_two, d_chunks[1].z_four],
-        9: [q_chunks[1].middle, i_chunks[3].z_one, i_chunks[0].z_three, d_chunks[2].z_four],
-        10: [i_chunks[2].z_two, i_chunks[1].z_three, o_chunk.z_one],
-        11: [i_chunks[3].z_two, i_chunks[2].z_three, i_chunks[0].z_four],
+        0: [i_chunks[0].middle, d_chunks[2].z_one, d_chunks[0].z_two],
+        1: [i_chunks[1].middle, i_chunks[2].middle, d_chunks[1].z_two],
+        2: [
+            lambda: rso_each("start"),
+            i_chunks[3].middle,
+            d_chunks[0].z_three,
+            d_chunks[2].z_two,
+            i_chunks[0].z_one,
+        ],
+        3: [d_chunks[1].z_three, i_chunks[1].z_one, i_chunks[0].z_two],
+        4: [
+            q_chunks[0].middle,
+            d_chunks[2].z_three,
+            d_chunks[0].z_four,
+            i_chunks[2].z_one,
+            i_chunks[1].z_two,
+        ],
+        5: [i_chunks[3].z_one, i_chunks[0].z_three, d_chunks[1].z_four, i_chunks[2].z_two],
     }
 
-    @pl.loop(0, 12)
-    def _(now):
-        pair, qb = lax.div(now, 4), lax.rem(now, 4)
-
-        @pl.when(qb == 0)
-        def _():
-            flip[0:BLK, :] = jnp.transpose(qkv[:, tile(3 + pair, BLK)])
-            prepare_keys(pair)
-            dk_acc[...] = jnp.zeros_like(dk_acc)
-            dv_acc[...] = jnp.zeros_like(dv_acc)
-
-        rows = tile(qb, quarter)
+    @pl.loop(0, 3)
+    def _(pair):
         cols = tile(pair, BLK)
-        upstream = gmix[rows, cols]
-        product = jnp.transpose(upstream.astype(F32) * mixed[rows, cols].astype(F32))
-        parts = []
-        for h in range(2):
-            head = pair * 2 + h
-            logits, queries = scores(pair, qb, h)
-            probs = jnp.exp(logits - lse[pl.ds(head, 1), rows])
-            masked = jnp.where(mine_lanes[h], upstream, jnp.zeros_like(upstream))
+        flip[0:BLK, :] = jnp.transpose(qkv[:, tile(3 + pair, BLK)])
+        for qb in range(2):
+            rows = pl.ds(qb * middle_q, middle_q)
+            upstream = gmix[rows, cols]
+            masked = by_head(upstream)
+            queries = by_head(qkv[rows, cols])
+            product = jnp.transpose(upstream.astype(F32) * mixed[rows, cols].astype(F32))
+            inner = jnp.concatenate(
+                [jnp.sum(product[64 * h : 64 * h + 64, :], 0, keepdims=True) for h in range(2)],
+                axis=1,
+            )
+            fetch(pair, qb).wait()
+            raised = slots[qb][...]
             grad_probs = contract(qkv[:, tile(6 + pair, BLK)], masked, 1, 1)
-            inner = jnp.sum(product[64 * h : 64 * h + 64, :], 0, keepdims=True)
-            grad_logits = (probs * (grad_probs - inner)).astype(BF16)
-            dv_acc[...] += contract(probs.astype(BF16), masked, 1, 0)
-            dk_acc[...] += contract(grad_logits, queries, 1, 0)
-            ds_buf[BLK : tokens + BLK, :] = grad_logits
+            grad_logits = (raised.astype(F32) * (grad_probs - inner)).astype(BF16)
+            grad_values = contract(raised, masked, 1, 0)
+            grad_keys = contract(grad_logits, queries, 1, 0)
+            if qb == 0:
+                dv_acc[...] = grad_values
+                dk_acc[...] = grad_keys
+            else:
+                dv_acc[...] += grad_values
+                dk_acc[...] += grad_keys
             result = contract(flip[...], grad_logits, 1, 0)
-            parts.append(result[64 * h : 64 * h + 64, :])
+            dqkv[rows, cols] = jnp.transpose(
+                jnp.concatenate([result[0:64, 0:middle_q], result[64:BLK, middle_q:]], axis=0)
+            ).astype(BF16)
             sums = result[BLK : BLK + 8, :]
             block_row = lax.broadcasted_iota(jnp.int32, sums.shape, 0)
-            query_block = 2 * qb + lax.div(lax.broadcasted_iota(jnp.int32, sums.shape, 1), BLK)
-            gap = block_row - query_block
-            far[head, 0:8, :] += jnp.where(gap <= -2, sums, 0.0)
-            far[head, 8:16, :] += jnp.where(gap >= 2, sums, 0.0)
-            for i in range(2):
+            block_col = lax.rem(
+                lax.div(lax.broadcasted_iota(jnp.int32, sums.shape, 1), BLK), middle_q // BLK
+            )
+            gap = block_row - block_col - qb * (middle_q // BLK)
+            far[pair, 0] += jnp.where(gap <= -2, sums, 0.0)
+            far[pair, 1] += jnp.where(gap >= 2, sums, 0.0)
+            for h in range(2):
                 for off in range(3):
-                    start = pl.multiple_of((2 * qb + i + off) * BLK, BLK)
-                    near[head * 3 + off] += ds_buf[
-                        pl.ds(start, BLK), i * BLK : (i + 1) * BLK
-                    ].astype(F32)
-        dq = jnp.transpose(jnp.concatenate(parts, axis=0)).astype(BF16)
-        dqkv[rows, cols] = dq
-        dpair[rows, 0:BLK] = dq
-
-        @pl.when(qb == 3)
-        def _():
-            for j, acc in ((1, dk_acc), (2, dv_acc)):
-                value = acc[...].astype(BF16)
-                dqkv[:, tile(3 * j + pair, BLK)] = value
-                dpair[:, j * BLK : (j + 1) * BLK] = value
-
-            @pl.loop(0, width // (2 * BLK))
-            def _(i):
-                gqkv[pair, tile(i, 2 * BLK), :] = contract(
-                    nrm1[:, tile(i, 2 * BLK)], dpair[...], 0, 0
-                ).astype(BF16)
-
-            for p in range(3):
-
-                @pl.when(pair == p)
-                def _():
-                    q_chunks[p].start()
-
-        serve(now, backward_table)
+                    total = near[(pair * 2 + h) * 3 + off]
+                    for i in range(middle_q // BLK):
+                        kb = qb * (middle_q // BLK) + i + off - 1
+                        if 0 <= kb < tokens // BLK:
+                            first = h * middle_q + i * BLK
+                            total = total + grad_logits[
+                                kb * BLK : (kb + 1) * BLK, first : first + BLK
+                            ].astype(F32)
+                    near[(pair * 2 + h) * 3 + off] = total
+
+            @pl.when(pair < 2)
+            def _():
+                fetch(pair + 1, qb).start()
+
+            if qb == 1:
+                dqkv[:, tile(3 + pair, BLK)] = dk_acc[...].astype(BF16)
+                dqkv[:, tile(6 + pair, BLK)] = dv_acc[...].astype(BF16)
+                right = jnp.concatenate(
+                    [dqkv[:, tile(3 * j + pair, BLK)] for j in range(3)], axis=1
+                )
+
+                @pl.loop(0, width // middle_w)
+                def _(i):
+                    gqkv[pair, tile(i, middle_w), :] = contract(
+                        nrm1[:, tile(i, middle_w)], right, 0, 0
+                    ).astype(BF16)
+
+                for p in range(3):
+
+                    @pl.when(pair == p)
+                    def _():
+                        q_chunks[p].start()
+
+            serve(2 * pair + qb, backward_table)
 
     for i in range(SEQ):
         swap_copy(i, gn2_ss, gn2_rs).wait_send()
 
-    @pl.loop(0, 2)
-    def _(i):
-        result = contract(blocks_of(dqkv, i, 1 - core), wqkv[...], 1, 1)
-        for j in range(2):
-            psend[2 * i + j] = result[j * BLK : (j + 1) * BLK, :]
-            swap_copy(2 * i + j, gn1_ss, gn1_rs).start()
-
-    q_chunks[2].middle()
-    i_chunks[3].z_three()
-    i_chunks[1].z_four()
-    o_chunk.z_two()
-    q_chunks[0].z_one()
+    swap_out(contract(blocks_of(dqkv, 1 - core), wqkv[...], 1, 1), gn1_ss, gn1_rs)
+    i_chunks[1].z_three()
+    d_chunks[2].z_four()
+    i_chunks[3].z_two()
 
     def gx_each(i, action):
         own = (chip == i) & (core == row)
         dst = gx_o.at[col, tile(core, BLK)]
         copy = remote(
-            gx_send.at[i], dst, gx_ss.at[i], gx_rs.at[col * 2 + core], (depth * 2 + row, i)
+            nrm2.at[pl.ds(i * BLK, BLK)], dst, gx_ss.at[i], gx_rs.at[col * 2 + core], (depth * 2 + row, i)
         )
         if action == "start":
 
             @pl.when(own)
             def _():
-                pltpu.make_async_copy(gx_send.at[i], dst, gx_rs.at[col * 2 + core]).start()
+                pltpu.make_async_copy(nrm2.at[pl.ds(i * BLK, BLK)], dst, gx_rs.at[col * 2 + core]).start()
 
         @pl.when(jnp.logical_not(own))
         def _():
@@ -1123,26 +1222,23 @@
             else:
                 copy.wait_send()
 
-    @pl.loop(0, 2)
-    def _(k):
-        both = contract(blocks_of(dqkv, k, core), wqkv[...], 1, 1)
-        for j in range(2):
-            i = 2 * k + j
-            swap_copy(i, gn1_ss, gn1_rs).wait_recv()
-            normed = both[j * BLK : (j + 1) * BLK, :] + precv[i]
-            source = xown[i].astype(F32)
-            scale = lax.rsqrt(jnp.mean(source * source, -1, keepdims=True) + EPS)
-            add_gain(0, jnp.sum(normed * source * scale, 0, keepdims=True))
-            scaled = normed * gains[0:1, :]
-            inner = jnp.mean(scaled * source, -1, keepdims=True)
-            result = hid[i] + scale * scaled - source * (scale * scale * scale) * inner
-            gx_send[i] = result.astype(BF16)
-            gx_each(i, "start")
-
-    i_chunks[2].z_four()
-    o_chunk.z_three()
-    q_chunks[0].z_two()
-    q_chunks[1].z_one()
+    both = contract(blocks_of(dqkv, core), wqkv[...], 1, 1)
+    for i in range(SEQ):
+        swap_copy(i, gn1_ss, gn1_rs).wait_recv()
+        normed = both[i * BLK : (i + 1) * BLK, :] + precv[i]
+        source = xown[i].astype(F32)
+        scale = lax.rsqrt(jnp.mean(source * source, -1, keepdims=True) + EPS)
+        add_gain(0, jnp.sum(normed * source * scale, 0, keepdims=True))
+        scaled = normed * gains[0:1, :]
+        inner = jnp.mean(scaled * source, -1, keepdims=True)
+        result = hid[i] + scale * scaled - source * (scale * scale * scale) * inner
+        nrm2[i * BLK : (i + 1) * BLK, :] = result.astype(BF16)
+
+    q_chunks[1].middle()
+    o_chunk.z_one()
+    q_chunks[0].z_one()
+    i_chunks[2].z_three()
+    i_chunks[0].z_four()
 
     diag_row = lax.broadcasted_iota(jnp.int32, (BLK, BLK), 0)
     diag_col = lax.broadcasted_iota(jnp.int32, (BLK, BLK), 1)
@@ -1157,6 +1253,10 @@
     def _(h):
         def skew(x):
             return pltpu.roll(exact(mirror, x, 1, 0), 0, 1, stride=1, stride_axis=0)
+
+        def far_of(h, side):
+            both = far[lax.div(h, 2), side]
+            return jnp.where(lax.rem(h, 2) == 0, both[:, 0:middle_q], both[:, middle_q:])
 
         tiles = [near[h * 3 + i] for i in range(3)]
         at = [
@@ -1167,8 +1267,8 @@
             )
             for i in range(2)
         ]
-        below = full_sum(jnp.where(upper, tiles[0], 0.0)) + full_sum(far[h, 0:8, :])
-        above = full_sum(jnp.where(upper, 0.0, tiles[2])) + full_sum(far[h, 8:16, :])
+        below = full_sum(jnp.where(upper, tiles[0], 0.0)) + full_sum(far_of(h, 0))
+        above = full_sum(jnp.where(upper, 0.0, tiles[2])) + full_sum(far_of(h, 1))
         sums = exact(jnp.broadcast_to(jnp.concatenate(at, axis=1), (8, 2 * BLK)), onehot, 1, 1)
         sums = sums[0:1, :] + jnp.where(lane == 15, below, 0.0) + jnp.where(lane == 31, above, 0.0)
         sg[pl.ds(16 + core * 6 + h, 1), :] = sums
@@ -1195,11 +1295,14 @@
 
     sgp_each("start")
     pltpu.make_async_copy(sg, sg_plane.at[place], sgp_rs.at[place]).start()
-    q_chunks[2].z_one()
-    q_chunks[1].z_two()
-    q_chunks[0].z_three()
-    i_chunks[3].z_four()
-    o_chunk.z_four()
+    q_chunks[2].middle()
+    for i in range(SEQ):
+        gx_each(i, "start")
+    i_chunks[1].z_four()
+    i_chunks[3].z_three()
+    o_chunk.z_two()
+    q_chunks[0].z_two()
+    q_chunks[1].z_one()
     for i in range(8):
         await_copy(sg_plane.at[i], sgp_rs.at[i])
     total = sg_plane[0]
@@ -1218,6 +1321,13 @@
 
     for step in range(1, DEPTH):
         sgz_copy(step).start()
+    i_chunks[2].z_four()
+    o_chunk.z_three()
+    q_chunks[2].z_one()
+    q_chunks[1].z_two()
+    q_chunks[0].z_three()
+    i_chunks[3].z_four()
+    o_chunk.z_four()
     q_chunks[2].z_two()
     q_chunks[1].z_three()
     q_chunks[0].z_four()
@@ -1258,7 +1368,6 @@
     for i in range(SEQ):
         n1_copy(i).wait_send()
         g_copy(i).wait_send()
-        n2_copy(i, gat_ss, gat_rs).wait_send()
         swap_copy(i, gn1_ss, gn1_rs).wait_send()
         gx_each(i, "wait")
     for step in range(1, DEPTH):
@@ -1540,8 +1649,8 @@
         shape((8, 2 * BLK), F32),
         shape((8, BLK), F32),
         *(shape(s, BF16) for s in narrow),
-    )
-    quarter = tokens // 4
+        shape((2 * pairs, tokens, tokens), BF16),
+    )
     out_part = rows_w // 2
 
     def sums(count, size, columns):
@@ -1563,22 +1672,18 @@
         ((SEQ * part, width), BF16),
         ((tokens, SEQ * part), BF16),
         ((tokens, SEQ * part), BF16),
-        ((tokens, part), BF16),
-        ((tokens, width), F32),
-        ((2 * pairs, 2 * tokens - BLK, BLK), F32),
+        ((SEQ, BLK, width), F32),
+        ((2 * pairs, 5 * BLK, BLK), F32),
         ((3, 16, 2 * BLK), F32),
         ((tokens, BLK), BF16),
-        ((2, tokens, BLK), BF16),
         ((8, tokens), F32),
         ((BLK + 16, tokens), BF16),
         ((tokens, 3 * half), BF16),
-        ((tokens, 3 * BLK), BF16),
         ((tokens, half), BF16),
         ((tokens, BLK), F32),
         ((tokens, BLK), F32),
-        ((tokens + 2 * BLK, quarter), BF16),
         ((6 * pairs, BLK, BLK), F32),
-        ((2 * pairs, 16, quarter), F32),
+        ((pairs, 2, 8, tokens), F32),
         ((pairs, width, 3 * BLK), BF16),
         ((parts, SEQ, BLK, width), BF16),
         *sums(parts, BLK, width),
@@ -1587,7 +1692,6 @@
         ((SEQ, out_part, width), BF16),
         ((out_part, width), BF16),
         ((out_part, width), BF16),
-        ((SEQ, BLK, width), BF16),
         ((SEQ + 1, 48, BLK), F32),
         ((8, width), F32),
         ((8, width), F32),
@@ -1605,7 +1709,7 @@
         pair_of(5)
         + pair_of(4)
         + pair_of(4)
-        + pair_of(6, 5)
+        + pair_of(6, 8)
         + pair_of(4)
         + pair_of(4) * 8
         + pair_of(chunks, 6)
@@ -1615,12 +1719,13 @@
         + pair_of(8)
         + pair_of(4)
         + [pltpu.SemaphoreType.DMA((chunks, 3))]
+        + [pltpu.SemaphoreType.DMA((2,))]
     )
     results = pl.pallas_call(
         fused_kernel,
         out_shape=out_shape,
         in_specs=[anywhere] * 8 + [vmem, vmem, smem],
-        out_specs=(vmem, vmem, vmem) + (anywhere,) * 7,
+        out_specs=(vmem, vmem, vmem) + (anywhere,) * 8,
         scratch_shapes=[pltpu.VMEM(*s) for s in scratch] + semaphores,
         compiler_params=pltpu.CompilerParams(
             collective_id=0, has_side_effects=True, vmem_limit_bytes=VMEM_LIMIT
@@ -1662,7 +1767,7 @@
         out_specs=[whole_spec(s) for s in tiny] + [rows_spec(s) for s in narrow],
         compiler_params=pltpu.CompilerParams(vmem_limit_bytes=VMEM_LIMIT),
         name="widen",
-    )(*results)
+    )(*results[:-1])
     return (pooled, gx, gq, gk, gv, go, gi, gd, one[0], two[0], table)
 
 

time: 205 us -> 172 us (0.84)
  Pallas kernels: 202 us -> 169 us
    pallas_call x1, Pallas kernels: 196 us -> 163 us  [fused_on_device(): pl.pallas_call(fused_kernel, out_shape=out_shape, in_specs=[anywhere] * 8...]
where the time goes in v3:
time: 172 us
  Pallas kernels  169 us (98%)
    pallas_call x1, Pallas kernels, fused_on_device(): pl.pallas_call(fused_kernel, out_shape=out_shape, in_specs=[anywhere] * 8...  163 us
    pallas_call x1, Pallas kernels, fused_on_device(): pl.pallas_call(widen_kernel, out_shape=[shape(s, F32) for s in tiny + nar...  6.12 us

profile of v3, /device:TPU:0, one launch (start us, length us, event | category | flops | bytes accessed | tf_op | source)
XLA Modules:
  0.0 171.8 jit_solution(17950385019513167752)
XLA Ops:
  0.6 0.7 stack.9
  1.3 0.7 stack.10
  2.0 0.6 maximum_convert_fusion.gains_in
  2.5 163.0 %block.1 = (f32[2,768]{1,0:T(2,128)}, f32[8,256]{1,0:T(8,128)}, f32[8,128]{1,0:T(8,128)}, bf16[2,256,768]{2,1,0:T(8,128)(2,1)}, bf16[192,768]{1,0:T(8,128)(2,1)}...) custom-call(bf16[2,256,768]{2,1,0:T(8,128)(2,1)} %inputs.1, ...), custom_call_target="tpu_custom_call" | custom-call | tf_op jit(solution)/shard_map/block/pallas_call | solution.py:1724
  165.5 6.1 %widen.1 = (f32[2,768]{1,0:T(2,128)}, f32[1,192]{1,0:T(1,128)}, f32[1,192]{1,0:T(1,128)}, f32[8,12]{1,0:T(8,128)}, f32[2,256,768]{2,1,0:T(8,128)}, /*index=5*/f3...) custom-call(f32[2,768]{1,0:T(2,128)} %get-tuple-element.32.pooled, ...), custom_call_target="tpu_custom_call" | custom-call | tf_op jit(solution)/shard_map/widen/pallas_call | solution.py:1762

commit v4 on v3

--- a/solution.py
+++ b/solution.py
@@ -91,6 +91,32 @@
     for threshold in THRESHOLDS:
         beyond = beyond + (distance >= threshold).astype(jnp.int32)
     return jnp.where(offset > 0, 16, 0) + jnp.where(distance < 8, distance, beyond)
+
+
+STEPS = dict(s="start", m="middle", z1="z_one", z2="z_two", z3="z_three", z4="z_four")
+SCHEDULE = {
+    "gdn0": [],
+    "gdn1": [("d1", "s"), ("d0", "s")],
+    "gdn2": [],
+    "wd": [],
+    "gact": [("d2", "s")],
+    "gn": [],
+    "gin0": [("d1", "m")],
+    "gin1": [("d2", "m"), ("i2", "s")],
+    "n2": [("d1", "z1"), ("i0", "s"), ("d0", "m")],
+    "op": [("d2", "z1"), ("i3", "s")],
+    "u0": [("i2", "m")],
+    "u1": [("d0", "z1"), ("i0", "m"), ("d2", "z2"), ("i1", "s"), ("d1", "z2")],
+    "u2": [],
+    "u3": [("i3", "m"), ("d0", "z2"), ("d2", "z3"), ("q1", "s"), ("i2", "z1")],
+    "u4": [("d1", "z3"), ("i1", "m"), ("q0", "s"), ("i0", "z1")],
+    "u5": [("i2", "z2"), ("i3", "z1"), ("d0", "z3")],
+    "sw": [("q1", "m")],
+    "b0": [("i0", "z2"), ("q2", "s")],
+    "b1": [("i2", "z3"), ("q0", "m"), ("i3", "z2"), ("q1", "z1")],
+    "g1": [("i0", "z3"), ("q2", "m"), ("i1", "z1"), ("q1", "z2"), ("o", "s"), ("i3", "z3"), ("q0", "z1"), ("i1", "z2"), ("q2", "z1"), ("i2", "z4"), ("q1", "z3"), ("q0", "z2"), ("d2", "z4"), ("sm", "s"), ("i3", "z4"), ("i1", "z3"), ("q2", "z2"), ("d1", "z4"), ("o", "z1"), ("q1", "z4"), ("q0", "z3"), ("gx", "s"), ("o", "z2"), ("q0", "z4"), ("q2", "z3"), ("q2", "z4"), ("o", "z3"), ("i1", "z4"), ("d0", "z4"), ("i0", "z4"), ("o", "z4")],
+    "end": [],
+}
 
 
 def full_sum(value):
@@ -414,6 +440,12 @@
 
         def second(self):
             super().second()
+            self.show()
+
+        def forward(self):
+            super().second()
+
+        def show(self):
             for copy in self.beside[:2]:
                 copy.start()
 
@@ -437,21 +469,19 @@
 
     core_cols = tile(core, half)
     whole = lambda ref: ref
-    row_half = rows_w // 2
-
-    def qkv_item(index, part):
-        return Gather(
+    pair_w = 3 * BLK
+
+    def qkv_item(index, pair):
+        return SharedGather(
             index,
             [
                 (
-                    w.at[pl.ds(part * row_half, row_half), core_cols],
-                    lambda ref, i=i: ref.at[:, pl.ds(i * half, half)],
+                    w.at[:, tile(core * 3 + pair, BLK)],
+                    lambda ref, i=i: ref.at[:, pl.ds(i * BLK, BLK)],
                 )
                 for i, w in enumerate((w_query, w_key, w_value))
             ],
-            lambda owner: wqkv.at[
-                pl.ds(pl.multiple_of(owner * rows_w + part * row_half, row_half), row_half)
-            ],
+            lambda owner: wqkv.at[tile(owner, rows_w), pl.ds(pair * pair_w, pair_w)],
         )
 
     def in_item(index, part):
@@ -477,9 +507,9 @@
             ],
         )
 
-    qkv_items = [qkv_item(0, 0), qkv_item(1, 1)]
-    in_items = [in_item(2, 0), in_item(3, 1)]
-    down_items = [down_item(4, 0), down_item(5, 1)]
+    qkv_items = [qkv_item(i, i) for i in range(3)]
+    in_items = [in_item(3, 0), in_item(4, 1)]
+    down_items = [down_item(5, 0), down_item(6, 1)]
     for it in qkv_items:
         it.first()
 
@@ -557,19 +587,17 @@
         n1_copy(i).start()
 
     qkv_items[0].second()
-    qkv_items[1].second()
+    for it in qkv_items[1:]:
+        it.forward()
     wo_each("start")
     for it in in_items:
         it.first()
-    for it in qkv_items:
-        it.done()
+    qkv_items[0].third()
+    for it in qkv_items[1:]:
+        it.show()
+        it.third()
     for i in range(SEQ):
         n1_copy(i).wait_recv()
-
-    @pl.loop(0, 4)
-    def _(i):
-        rows = tile(i, quarter)
-        qkv[rows, :] = contract(nrm1[rows, :], wqkv[...], 1, 0).astype(BF16)
 
     flip[BLK : BLK + 16, :] = jnp.ones((16, tokens), BF16)
     mine_lanes = [lane < 64, lane >= 64]
@@ -601,18 +629,27 @@
 
     forward_table = {
         2: [in_items[0].second],
-        3: [in_items[1].second, later_inputs],
-        4: [in_items[0].third],
+        3: [in_items[1].forward, later_inputs, in_items[0].third, in_items[1].show],
+        5: [in_items[1].third],
     }
 
     @pl.loop(0, 3)
     def _(pair):
         cols = tile(pair, BLK)
-        flip[0:BLK, :] = jnp.transpose(qkv[:, tile(6 + pair, BLK)])
-        keys = jnp.concatenate([qkv[:, tile(3 + pair, BLK)], maskc[...]], axis=1)
+        for p in range(3):
+
+            @pl.when(pair == p)
+            def _():
+                qkv_items[p].done()
+
+        qkv[:, tile(pair, pair_w)] = contract(
+            nrm1[...], wqkv[:, tile(pair, pair_w)], 1, 0
+        ).astype(BF16)
+        flip[0:BLK, :] = jnp.transpose(qkv[:, tile(3 * pair + 2, BLK)])
+        keys = jnp.concatenate([qkv[:, tile(3 * pair + 1, BLK)], maskc[...]], axis=1)
         for qb in range(2):
             rows = pl.ds(qb * middle_q, middle_q)
-            queries = by_head(qkv[rows, cols])
+            queries = by_head(qkv[rows, tile(3 * pair, BLK)])
             flag = jnp.broadcast_to(jnp.where(lane == 0, 1.0, 0.0).astype(BF16), queries.shape)
             biases = [
                 jnp.concatenate(
@@ -651,7 +688,6 @@
     def swap_copy(i, send, recv):
         return remote(psend.at[i], precv.at[i], send.at[i], recv.at[i], other)
 
-    in_items[1].third()
     for k in range(4):
         await_copy(wo.at[pl.ds(k * wo_part, wo_part)], wo_rs.at[k])
 
@@ -662,7 +698,7 @@
 
     def swap_out(result, send, recv):
         for i in range(SEQ):
-            psend[i] = result[i * BLK : (i + 1) * BLK, :]
+            psend[i] = result[i * BLK : (i + 1) * BLK, :].astype(BF16)
             swap_copy(i, send, recv).start()
 
     swap_out(contract(blocks_of(mixed, 1 - core), wo[...], 1, 0), part_ss, part_rs)
@@ -676,7 +712,7 @@
     for i in range(SEQ):
         hidden = xown[i].astype(F32) + result[i * BLK : (i + 1) * BLK, :]
         swap_copy(i, part_ss, part_rs).wait_recv()
-        hidden = hidden + precv[i]
+        hidden = hidden + precv[i].astype(F32)
         hid[i] = hidden
         scale = lax.rsqrt(jnp.mean(hidden * hidden, -1, keepdims=True) + EPS)
         nrm2[tile(2 * i + core, BLK), :] = (hidden * scale * gains[1:2, :]).astype(BF16)
@@ -882,34 +918,6 @@
         for i in range(ff_part // BLK)
     ]
 
-    for i in range(ff_part // BLK):
-        columns = jnp.concatenate(
-            [act[:, f * ff_part + i * BLK : f * ff_part + (i + 1) * BLK] for f in range(SEQ)],
-            axis=1,
-        )
-        gdn[i] = contract(columns, g_all(), 0, 0).astype(BF16).reshape(SEQ, BLK, width)
-        if i == 0:
-            down_items[1].second()
-    down_items[0].third()
-    for chunk in d_chunks:
-        chunk.start()
-    for it in down_items:
-        it.done()
-    for it in in_items:
-        it.sent()
-
-    def pooled_part(cols):
-        total = asum[0:1, cols]
-        high = total.astype(BF16)
-        rest = total - high.astype(F32)
-        middle = rest.astype(BF16)
-        low = (rest - middle.astype(F32)).astype(BF16)
-        pieces = jnp.concatenate(
-            [jnp.broadcast_to(piece, (16, piece.shape[1])) for piece in (high, middle, low)], axis=0
-        )
-        result = contract(pieces, wd[cols, :], 1, 0)
-        pp[0:1, :] += result[0:1, :] + result[16:17, :] + result[32:33, :]
-
     i_chunks = [
         Chunk(
             lambda owner, f=f: wi.at[tile(owner, rows_w), pl.ds(f * ff_part, ff_part)],
@@ -923,6 +931,150 @@
         )
         for f in range(SEQ)
     ]
+    q_chunks = [
+        Chunk(
+            lambda owner, p=p: gqkv.at[p, tile(owner, rows_w)],
+            q_dx.at[p],
+            q_dy.at[p],
+            q_rx.at[p],
+            q_ry.at[p],
+            q_za.at[p],
+            q_zb.at[p],
+            [
+                (
+                    pl.ds(j * BLK, BLK),
+                    lambda c, p=p, o=o: o.at[:, tile(c * 3 + p, BLK)],
+                )
+                for j, o in enumerate((gq_o, gk_o, gv_o))
+            ],
+        )
+        for p in range(3)
+    ]
+    def rso_each(action):
+        for k in range(2):
+            for to in range(2):
+                target = core * 2 + k
+                own = (chip == target) & (core == to)
+                src = wo.at[pl.ds((2 * k + to) * wo_part, wo_part)]
+                dst = rs_o.at[chip]
+                copy = remote(
+                    src, dst, rso_ss.at[2 * k + to], rso_rs.at[chip], (depth * 2 + to, target)
+                )
+                if action == "start":
+
+                    @pl.when(own)
+                    def _():
+                        pltpu.make_async_copy(src, dst, rso_rs.at[chip]).start()
+
+                @pl.when(jnp.logical_not(own))
+                def _():
+                    if action == "start":
+                        copy.start()
+                    else:
+                        copy.wait_send()
+
+    class OutChunk(Chunk):
+        def bind(self):
+            self.bind_z(self.src.at[0], self.src.at[1])
+
+        def total(self):
+            for i in range(SEQ):
+                await_copy(self.src.at[i], rso_rs.at[i])
+            value = self.src[0].astype(F32)
+            for i in range(1, SEQ):
+                value = value + self.src[i].astype(F32)
+            self.reduced[...] = value.astype(BF16)
+
+        def plane_sends(self):
+            return []
+
+    o_chunk = OutChunk(
+        rs_o, None, None, None, None, o_za, o_zb, [(None, lambda c: go_o.at[tile(c, wo_part)])]
+    )
+    def gx_each(i, action):
+        own = (chip == i) & (core == row)
+        dst = gx_o.at[col, tile(core, BLK)]
+        copy = remote(
+            nrm2.at[pl.ds(i * BLK, BLK)], dst, gx_ss.at[i], gx_rs.at[col * 2 + core], (depth * 2 + row, i)
+        )
+        if action == "start":
+
+            @pl.when(own)
+            def _():
+                pltpu.make_async_copy(nrm2.at[pl.ds(i * BLK, BLK)], dst, gx_rs.at[col * 2 + core]).start()
+
+        @pl.when(jnp.logical_not(own))
+        def _():
+            if action == "start":
+                copy.start()
+            else:
+                copy.wait_send()
+
+    def sgz_copy(step):
+        return remote(
+            sg_depth.at[depth],
+            sg_depth.at[depth],
+            sgz_ss.at[step],
+            sgz_rs.at[depth],
+            z_dev(lax.rem(depth + step, DEPTH)),
+        )
+
+    def small_along_z():
+        for i in range(8):
+            await_copy(sg_plane.at[i], sgp_rs.at[i])
+        total = sg_plane[0]
+        for i in range(1, 8):
+            total = total + sg_plane[i]
+        sg_depth[depth] = total
+        for step in range(1, DEPTH):
+            sgz_copy(step).start()
+
+    by_name = dict(
+        [(f"d{i}", c) for i, c in enumerate(d_chunks)]
+        + [(f"i{i}", c) for i, c in enumerate(i_chunks)]
+        + [(f"q{i}", c) for i, c in enumerate(q_chunks)]
+        + [("o", o_chunk)]
+    )
+
+    def after(block):
+        for name, step in SCHEDULE[block]:
+            if name == "gx":
+                for i in range(SEQ):
+                    gx_each(i, "start")
+            elif name == "sm":
+                small_along_z()
+            elif name == "o" and step == "s":
+                rso_each("start")
+            else:
+                getattr(by_name[name], STEPS[step])()
+
+    down_items[1].second()
+    down_items[0].third()
+    for i in range(ff_part // BLK):
+        columns = jnp.concatenate(
+            [act[:, f * ff_part + i * BLK : f * ff_part + (i + 1) * BLK] for f in range(SEQ)],
+            axis=1,
+        )
+        gdn[i] = contract(columns, g_all(), 0, 0).astype(BF16).reshape(SEQ, BLK, width)
+        after(f"gdn{i}")
+    for it in down_items:
+        it.done()
+    for it in in_items:
+        it.sent()
+    after("wd")
+
+    def pooled_part(cols):
+        total = asum[0:1, cols]
+        high = total.astype(BF16)
+        rest = total - high.astype(F32)
+        middle = rest.astype(BF16)
+        low = (rest - middle.astype(F32)).astype(BF16)
+        pieces = jnp.concatenate(
+            [jnp.broadcast_to(piece, (16, piece.shape[1])) for piece in (high, middle, low)], axis=0
+        )
+        result = contract(pieces, wd[cols, :], 1, 0)
+        pp[0:1, :] += result[0:1, :] + result[16:17, :] + result[32:33, :]
+
     for part in range(2):
         part_cols = slice(part * wide_part, (part + 1) * wide_part)
 
@@ -935,13 +1087,13 @@
 
         pooled_part(part_cols)
 
-    d_chunks[0].middle()
+    after("gact")
 
     for i in range(SEQ):
         swap_copy(i, part_ss, part_rs).wait_send()
     swap_out(contract(blocks_of(slope, 1 - core), wi[...], 1, 1), gn2_ss, gn2_rs)
     gn[...] = contract(blocks_of(slope, core), wi[...], 1, 1).reshape(SEQ, BLK, width)
-    d_chunks[1].middle()
+    after("gn")
     for part in range(2):
         part_cols = slice(part * wide_part, (part + 1) * wide_part)
 
@@ -951,10 +1103,7 @@
                 nrm2[:, tile(i, 2 * BLK)], slope[:, part_cols], 0, 0
             ).astype(BF16)
 
-        if part == 1:
-            d_chunks[2].middle()
-        i_chunks[2 * part].start()
-        i_chunks[2 * part + 1].start()
+        after(f"gin{part}")
     def pool_each(action):
         for to in range(SEQ):
             own = (chip == to) & (core == row)
@@ -989,7 +1138,7 @@
     def _(i):
         b = 2 * i + core
         swap_copy(i, gn2_ss, gn2_rs).wait_recv()
-        normed = gn[i] + precv[i]
+        normed = gn[i] + precv[i].astype(F32)
         hidden = hid[i]
         scale = lax.rsqrt(jnp.mean(hidden * hidden, -1, keepdims=True) + EPS)
         add_gain(8, jnp.sum(normed * hidden * scale, 0, keepdims=True))
@@ -1001,7 +1150,7 @@
         gat_copy(i).start()
 
     pool_each("start")
-    d_chunks[0].z_one()
+    after("n2")
     for i in range(SEQ):
         gat_copy(i).wait_recv()
 
@@ -1030,49 +1179,8 @@
         gat_copy(i).wait_send()
     for qb in range(2):
         fetch(0, qb).start()
-    d_chunks[1].z_one()
-
-    def rso_each(action):
-        for k in range(2):
-            for to in range(2):
-                target = core * 2 + k
-                own = (chip == target) & (core == to)
-                src = wo.at[pl.ds((2 * k + to) * wo_part, wo_part)]
-                dst = rs_o.at[chip]
-                copy = remote(
-                    src, dst, rso_ss.at[2 * k + to], rso_rs.at[chip], (depth * 2 + to, target)
-                )
-                if action == "start":
-
-                    @pl.when(own)
-                    def _():
-                        pltpu.make_async_copy(src, dst, rso_rs.at[chip]).start()
-
-                @pl.when(jnp.logical_not(own))
-                def _():
-                    if action == "start":
-                        copy.start()
-                    else:
-                        copy.wait_send()
-
-    class OutChunk(Chunk):
-        def bind(self):
-            self.bind_z(self.src.at[0], self.src.at[1])
-
-        def total(self):
-            for i in range(SEQ):
-                await_copy(self.src.at[i], rso_rs.at[i])
-            value = self.src[0].astype(F32)
-            for i in range(1, SEQ):
-                value = value + self.src[i].astype(F32)
-            self.reduced[...] = value.astype(BF16)
-
-        def plane_sends(self):
-            return []
-
-    o_chunk = OutChunk(
-        rs_o, None, None, None, None, o_za, o_zb, [(None, lambda c: go_o.at[tile(c, wo_part)])]
-    )
+    after("op")
+
 
     sub = lax.broadcasted_iota(jnp.int32, (16, tokens), 0)
     key_block = lax.div(lax.broadcasted_iota(jnp.int32, (16, tokens), 1), BLK)
@@ -1080,55 +1188,17 @@
     near[...] = jnp.zeros_like(near)
     far[...] = jnp.zeros_like(far)
 
-    q_chunks = [
-        Chunk(
-            lambda owner, p=p: gqkv.at[p, tile(owner, rows_w)],
-            q_dx.at[p],
-            q_dy.at[p],
-            q_rx.at[p],
-            q_ry.at[p],
-            q_za.at[p],
-            q_zb.at[p],
-            [
-                (
-                    pl.ds(j * BLK, BLK),
-                    lambda c, p=p, o=o: o.at[:, tile(c * 3 + p, BLK)],
-                )
-                for j, o in enumerate((gq_o, gk_o, gv_o))
-            ],
-        )
-        for p in range(3)
-    ]
-    backward_table = {
-        0: [i_chunks[0].middle, d_chunks[2].z_one, d_chunks[0].z_two],
-        1: [i_chunks[1].middle, i_chunks[2].middle, d_chunks[1].z_two],
-        2: [
-            lambda: rso_each("start"),
-            i_chunks[3].middle,
-            d_chunks[0].z_three,
-            d_chunks[2].z_two,
-            i_chunks[0].z_one,
-        ],
-        3: [d_chunks[1].z_three, i_chunks[1].z_one, i_chunks[0].z_two],
-        4: [
-            q_chunks[0].middle,
-            d_chunks[2].z_three,
-            d_chunks[0].z_four,
-            i_chunks[2].z_one,
-            i_chunks[1].z_two,
-        ],
-        5: [i_chunks[3].z_one, i_chunks[0].z_three, d_chunks[1].z_four, i_chunks[2].z_two],
-    }
+    backward_table = {i: [lambda i=i: after(f"u{i}")] for i in range(6)}
 
     @pl.loop(0, 3)
     def _(pair):
         cols = tile(pair, BLK)
-        flip[0:BLK, :] = jnp.transpose(qkv[:, tile(3 + pair, BLK)])
+        flip[0:BLK, :] = jnp.transpose(qkv[:, tile(3 * pair + 1, BLK)])
         for qb in range(2):
             rows = pl.ds(qb * middle_q, middle_q)
             upstream = gmix[rows, cols]
             masked = by_head(upstream)
-            queries = by_head(qkv[rows, cols])
+            queries = by_head(qkv[rows, tile(3 * pair, BLK)])
             product = jnp.transpose(upstream.astype(F32) * mixed[rows, cols].astype(F32))
             inner = jnp.concatenate(
                 [jnp.sum(product[64 * h : 64 * h + 64, :], 0, keepdims=True) for h in range(2)],
@@ -1136,7 +1206,7 @@
             )
             fetch(pair, qb).wait()
             raised = slots[qb][...]
-            grad_probs = contract(qkv[:, tile(6 + pair, BLK)], masked, 1, 1)
+            grad_probs = contract(qkv[:, tile(3 * pair + 2, BLK)], masked, 1, 1)
             grad_logits = (raised.astype(F32) * (grad_probs - inner)).astype(BF16)
             grad_values = contract(raised, masked, 1, 0)
             grad_keys = contract(grad_logits, queries, 1, 0)
@@ -1147,7 +1217,7 @@
                 dv_acc[...] += grad_values
                 dk_acc[...] += grad_keys
             result = contract(flip[...], grad_logits, 1, 0)
-            dqkv[rows, cols] = jnp.transpose(
+            dqkv[rows, tile(3 * pair, BLK)] = jnp.transpose(
                 jnp.concatenate([result[0:64, 0:middle_q], result[64:BLK, middle_q:]], axis=0)
             ).astype(BF16)
             sums = result[BLK : BLK + 8, :]
@@ -1175,11 +1245,9 @@
                 fetch(pair + 1, qb).start()
 
             if qb == 1:
-                dqkv[:, tile(3 + pair, BLK)] = dk_acc[...].astype(BF16)
-                dqkv[:, tile(6 + pair, BLK)] = dv_acc[...].astype(BF16)
-                right = jnp.concatenate(
-                    [dqkv[:, tile(3 * j + pair, BLK)] for j in range(3)], axis=1
-                )
+                dqkv[:, tile(3 * pair + 1, BLK)] = dk_acc[...].astype(BF16)
+                dqkv[:, tile(3 * pair + 2, BLK)] = dv_acc[...].astype(BF16)
+                right = dqkv[:, tile(pair, pair_w)]
 
                 @pl.loop(0, width // middle_w)
                 def _(i):
@@ -1187,59 +1255,12 @@
                         nrm1[:, tile(i, middle_w)], right, 0, 0
                     ).astype(BF16)
 
-                for p in range(3):
-
-                    @pl.when(pair == p)
-                    def _():
-                        q_chunks[p].start()
-
             serve(2 * pair + qb, backward_table)
 
     for i in range(SEQ):
         swap_copy(i, gn2_ss, gn2_rs).wait_send()
 
     swap_out(contract(blocks_of(dqkv, 1 - core), wqkv[...], 1, 1), gn1_ss, gn1_rs)
-    i_chunks[1].z_three()
-    d_chunks[2].z_four()
-    i_chunks[3].z_two()
-
-    def gx_each(i, action):
-        own = (chip == i) & (core == row)
-        dst = gx_o.at[col, tile(core, BLK)]
-        copy = remote(
-            nrm2.at[pl.ds(i * BLK, BLK)], dst, gx_ss.at[i], gx_rs.at[col * 2 + core], (depth * 2 + row, i)
-        )
-        if action == "start":
-
-            @pl.when(own)
-            def _():
-                pltpu.make_async_copy(nrm2.at[pl.ds(i * BLK, BLK)], dst, gx_rs.at[col * 2 + core]).start()
-
-        @pl.when(jnp.logical_not(own))
-        def _():
-            if action == "start":
-                copy.start()
-            else:
-                copy.wait_send()
-
-    both = contract(blocks_of(dqkv, core), wqkv[...], 1, 1)
-    for i in range(SEQ):
-        swap_copy(i, gn1_ss, gn1_rs).wait_recv()
-        normed = both[i * BLK : (i + 1) * BLK, :] + precv[i]
-        source = xown[i].astype(F32)
-        scale = lax.rsqrt(jnp.mean(source * source, -1, keepdims=True) + EPS)
-        add_gain(0, jnp.sum(normed * source * scale, 0, keepdims=True))
-        scaled = normed * gains[0:1, :]
-        inner = jnp.mean(scaled * source, -1, keepdims=True)
-        result = hid[i] + scale * scaled - source * (scale * scale * scale) * inner
-        nrm2[i * BLK : (i + 1) * BLK, :] = result.astype(BF16)
-
-    q_chunks[1].middle()
-    o_chunk.z_one()
-    q_chunks[0].z_one()
-    i_chunks[2].z_three()
-    i_chunks[0].z_four()
-
     diag_row = lax.broadcasted_iota(jnp.int32, (BLK, BLK), 0)
     diag_col = lax.broadcasted_iota(jnp.int32, (BLK, BLK), 1)
     upper = diag_col >= diag_row
@@ -1249,8 +1270,7 @@
     ids = bucket_of(jnp.concatenate([-shift, BLK - shift], axis=1))
     onehot = (lax.broadcasted_iota(jnp.int32, (BLK, 2 * BLK), 0) == ids).astype(F32)
 
-    @pl.loop(0, 6)
-    def _(h):
+    def bias_head(h):
         def skew(x):
             return pltpu.roll(exact(mirror, x, 1, 0), 0, 1, stride=1, stride_axis=0)
 
@@ -1272,6 +1292,31 @@
         sums = exact(jnp.broadcast_to(jnp.concatenate(at, axis=1), (8, 2 * BLK)), onehot, 1, 1)
         sums = sums[0:1, :] + jnp.where(lane == 15, below, 0.0) + jnp.where(lane == 31, above, 0.0)
         sg[pl.ds(16 + core * 6 + h, 1), :] = sums
+
+    after("sw")
+
+    @pl.loop(0, 3)
+    def _(h):
+        bias_head(h)
+
+    after("b0")
+
+    @pl.loop(3, 6)
+    def _(h):
+        bias_head(h)
+
+    after("b1")
+    both = contract(blocks_of(dqkv, core), wqkv[...], 1, 1)
+    for i in range(SEQ):
+        swap_copy(i, gn1_ss, gn1_rs).wait_recv()
+        normed = both[i * BLK : (i + 1) * BLK, :] + precv[i].astype(F32)
+        source = xown[i].astype(F32)
+        scale = lax.rsqrt(jnp.mean(source * source, -1, keepdims=True) + EPS)
+        add_gain(0, jnp.sum(normed * source * scale, 0, keepdims=True))
+        scaled = normed * gains[0:1, :]
+        inner = jnp.mean(scaled * source, -1, keepdims=True)
+        result = hid[i] + scale * scaled - source * (scale * scale * scale) * inner
+        nrm2[i * BLK : (i + 1) * BLK, :] = result.astype(BF16)
 
     place = core * SEQ + chip
 
@@ -1295,46 +1340,8 @@
 
     sgp_each("start")
     pltpu.make_async_copy(sg, sg_plane.at[place], sgp_rs.at[place]).start()
-    q_chunks[2].middle()
-    for i in range(SEQ):
-        gx_each(i, "start")
-    i_chunks[1].z_four()
-    i_chunks[3].z_three()
-    o_chunk.z_two()
-    q_chunks[0].z_two()
-    q_chunks[1].z_one()
-    for i in range(8):
-        await_copy(sg_plane.at[i], sgp_rs.at[i])
-    total = sg_plane[0]
-    for i in range(1, 8):
-        total = total + sg_plane[i]
-    sg_depth[depth] = total
-
-    def sgz_copy(step):
-        return remote(
-            sg_depth.at[depth],
-            sg_depth.at[depth],
-            sgz_ss.at[step],
-            sgz_rs.at[depth],
-            z_dev(lax.rem(depth + step, DEPTH)),
-        )
-
-    for step in range(1, DEPTH):
-        sgz_copy(step).start()
-    i_chunks[2].z_four()
-    o_chunk.z_three()
-    q_chunks[2].z_one()
-    q_chunks[1].z_two()
-    q_chunks[0].z_three()
-    i_chunks[3].z_four()
-    o_chunk.z_four()
-    q_chunks[2].z_two()
-    q_chunks[1].z_three()
-    q_chunks[0].z_four()
-    q_chunks[2].z_three()
-    q_chunks[1].z_four()
-    q_chunks[2].z_four()
-
+    after("g1")
+    after("end")
     for i in range(4):
         await_copy(pool_recv.at[i], pool_rs.at[i])
     for doc in range(2):
@@ -1664,8 +1671,8 @@
         ((tokens, 3 * half), BF16),
         ((tokens, half), BF16),
         ((half, width), BF16),
-        ((SEQ, BLK, width), F32),
-        ((SEQ, BLK, width), F32),
+        ((SEQ, BLK, width), BF16),
+        ((SEQ, BLK, width), BF16),
         ((SEQ, BLK, width), F32),
         ((tokens, width), BF16),
         ((width, SEQ * part), BF16),
@@ -1709,7 +1716,7 @@
         pair_of(5)
         + pair_of(4)
         + pair_of(4)
-        + pair_of(6, 8)
+        + pair_of(7, 8)
         + pair_of(4)
         + pair_of(4) * 8
         + pair_of(chunks, 6)

time: 172 us -> 157 us (0.913)
  Pallas kernels: 169 us -> 154 us
    pallas_call x1, Pallas kernels: 163 us -> 148 us  [fused_on_device(): pl.pallas_call(fused_kernel, out_shape=out_shape, in_specs=[anywhere] * 8...]
where the time goes in v4:
time: 157 us
  Pallas kernels  154 us (98%)
    pallas_call x1, Pallas kernels, fused_on_device(): pl.pallas_call(fused_kernel, out_shape=out_shape, in_specs=[anywhere] * 8...  148 us
    pallas_call x1, Pallas kernels, fused_on_device(): pl.pallas_call(widen_kernel, out_shape=[shape(s, F32) for s in tiny + nar...  6.12 us

profile of v4, /device:TPU:0, one launch (start us, length us, event | category | flops | bytes accessed | tf_op | source)
XLA Modules:
  0.0 156.6 jit_solution(15398514752106133120)
XLA Ops:
  0.6 0.7 stack.9
  1.3 0.7 stack.10
  2.0 0.6 maximum_convert_fusion.gains_in
  2.5 147.8 %block.1 = (f32[2,768]{1,0:T(2,128)}, f32[8,256]{1,0:T(8,128)}, f32[8,128]{1,0:T(8,128)}, bf16[2,256,768]{2,1,0:T(8,128)(2,1)}, bf16[192,768]{1,0:T(8,128)(2,1)}...) custom-call(bf16[2,256,768]{2,1,0:T(8,128)(2,1)} %inputs.1, ...), custom_call_target="tpu_custom_call" | custom-call | tf_op jit(solution)/shard_map/block/pallas_call | solution.py:1731
  150.4 6.1 %widen.1 = (f32[2,768]{1,0:T(2,128)}, f32[1,192]{1,0:T(1,128)}, f32[1,192]{1,0:T(1,128)}, f32[8,12]{1,0:T(8,128)}, f32[2,256,768]{2,1,0:T(8,128)}, /*index=5*/f3...) custom-call(f32[2,768]{1,0:T(2,128)} %get-tuple-element.32.pooled, ...), custom_call_target="tpu_custom_call" | custom-call | tf_op jit(solution)/shard_map/widen/pallas_call | solution.py:1769

commit v5 on v4

--- a/solution.py
+++ b/solution.py
@@ -95,26 +95,24 @@
 
 STEPS = dict(s="start", m="middle", z1="z_one", z2="z_two", z3="z_three", z4="z_four")
 SCHEDULE = {
-    "gdn0": [],
-    "gdn1": [("d1", "s"), ("d0", "s")],
-    "gdn2": [],
+    "gdn2": [("d2", "s"), ("d1", "s")],
     "wd": [],
-    "gact": [("d2", "s")],
-    "gn": [],
-    "gin0": [("d1", "m")],
-    "gin1": [("d2", "m"), ("i2", "s")],
-    "n2": [("d1", "z1"), ("i0", "s"), ("d0", "m")],
-    "op": [("d2", "z1"), ("i3", "s")],
-    "u0": [("i2", "m")],
-    "u1": [("d0", "z1"), ("i0", "m"), ("d2", "z2"), ("i1", "s"), ("d1", "z2")],
-    "u2": [],
-    "u3": [("i3", "m"), ("d0", "z2"), ("d2", "z3"), ("q1", "s"), ("i2", "z1")],
-    "u4": [("d1", "z3"), ("i1", "m"), ("q0", "s"), ("i0", "z1")],
-    "u5": [("i2", "z2"), ("i3", "z1"), ("d0", "z3")],
-    "sw": [("q1", "m")],
-    "b0": [("i0", "z2"), ("q2", "s")],
-    "b1": [("i2", "z3"), ("q0", "m"), ("i3", "z2"), ("q1", "z1")],
-    "g1": [("i0", "z3"), ("q2", "m"), ("i1", "z1"), ("q1", "z2"), ("o", "s"), ("i3", "z3"), ("q0", "z1"), ("i1", "z2"), ("q2", "z1"), ("i2", "z4"), ("q1", "z3"), ("q0", "z2"), ("d2", "z4"), ("sm", "s"), ("i3", "z4"), ("i1", "z3"), ("q2", "z2"), ("d1", "z4"), ("o", "z1"), ("q1", "z4"), ("q0", "z3"), ("gx", "s"), ("o", "z2"), ("q0", "z4"), ("q2", "z3"), ("q2", "z4"), ("o", "z3"), ("i1", "z4"), ("d0", "z4"), ("i0", "z4"), ("o", "z4")],
+    "gact": [("d2", "m")],
+    "gn": [("d1", "m")],
+    "gin0": [],
+    "gin1": [("d0", "s")],
+    "n2": [("i2", "s")],
+    "op": [("d1", "z1"), ("d2", "z1"), ("d0", "m")],
+    "u0": [("i3", "s")],
+    "u1": [("d1", "z2"), ("i2", "m"), ("d2", "z2"), ("i3", "m"), ("d0", "z1"), ("i0", "s")],
+    "u2": [("q0", "s"), ("d1", "z3"), ("d0", "z2"), ("i1", "s")],
+    "u3": [("d2", "z3"), ("i3", "z1")],
+    "u4": [("i0", "m"), ("d0", "z3"), ("q0", "m"), ("i3", "z2"), ("i2", "z1"), ("i1", "m")],
+    "u5": [("i0", "z1"), ("i2", "z2"), ("q2", "s")],
+    "sw": [],
+    "b0": [("q0", "z1"), ("q1", "s"), ("i3", "z3"), ("i0", "z2"), ("i1", "z1"), ("q2", "m"), ("i2", "z3"), ("q0", "z2"), ("d0", "z4"), ("q1", "m"), ("o", "s")],
+    "b1": [("d1", "z4"), ("i0", "z3"), ("i1", "z2"), ("q0", "z3"), ("q2", "z1")],
+    "g1": [("i3", "z4"), ("q2", "z2"), ("i1", "z3"), ("q1", "z1"), ("i0", "z4"), ("o", "z1"), ("q0", "z4"), ("q1", "z2"), ("q2", "z3"), ("o", "z2"), ("i2", "z4"), ("q1", "z3"), ("gx", "s"), ("sm", "s"), ("q2", "z4"), ("d2", "z4"), ("q1", "z4"), ("i1", "z4"), ("o", "z3"), ("o", "z4")],
     "end": [],
 }
 
@@ -132,7 +130,8 @@
     w_out,
     w_in,
     w_down,
-    gains_in,
+    gain_one,
+    gain_two,
     bias_in,
     lengths_in,
     pooled_o,
@@ -284,7 +283,8 @@
 
     lane = lax.broadcasted_iota(jnp.int32, (1, BLK), 1)
     wide[...] = jnp.zeros_like(wide)
-    wide[0:2, 0:rows_w] = gains_in[...]
+    wide[0:1, 0:rows_w] = gain_one[...].astype(F32).reshape(1, rows_w)
+    wide[1:2, 0:rows_w] = gain_two[...].astype(F32).reshape(1, rows_w)
     turned_gains = pltpu.roll(wide[...], chip * rows_w, 1)
     small_all[0] = jnp.zeros_like(small_all[0])
     for which in range(2):
@@ -320,9 +320,9 @@
         )
     send_now(mine, small_all.at[SEQ], small_ss.at[SEQ], small_rs.at[SEQ], other)
 
-    def spread(source, dest_of, send, recv, action):
-        for doc in range(2):
-            for to in range(2):
+    def spread(source, dest_of, send, recv, action, halves=(0, 1)):
+        for doc in (1 - col, col):
+            for to in halves:
                 block = source.at[doc, pl.ds(to * BLK, BLK)]
                 target = core * 2 + doc
                 own = (target == chip) & (core == to)
@@ -348,7 +348,6 @@
 
     x_slot = lambda to: xown.at[chip]
     c_slot = lambda to: grads.at[chip * 2 + to]
-    spread(inputs, x_slot, x_ss, x_rs, "start")
 
     class Gather:
         def __init__(self, index, pieces, place):
@@ -497,21 +496,23 @@
             lambda owner: wi.at[tile(owner, rows_w), pl.ds(part * 2 * ff_part, 2 * ff_part)],
         )
 
-    def down_item(index, part):
-        size = ff_part // 2
-        return (SharedGather if part == 0 else Gather)(
-            index,
-            [(w_down.at[pl.ds(pl.multiple_of(core * ff_part + part * size, size), size)], whole)],
-            lambda owner: wd.at[
-                pl.ds(pl.multiple_of(owner * ff_part + part * size, size), size)
-            ],
+    def down_item(kind, index, first, size):
+        unit = ff_part // 4
+        at = lambda base: pl.ds(pl.multiple_of(base + first * unit, unit), size * unit)
+        return kind(
+            index, [(w_down.at[at(core * ff_part)], whole)], lambda owner: wd.at[at(owner * ff_part)]
         )
 
     qkv_items = [qkv_item(i, i) for i in range(3)]
     in_items = [in_item(3, 0), in_item(4, 1)]
-    down_items = [down_item(5, 0), down_item(6, 1)]
+    down_items = [
+        down_item(SharedGather, 5, 0, 2),
+        down_item(Gather, 6, 2, 1),
+        down_item(Gather, 7, 3, 1),
+    ]
     for it in qkv_items:
         it.first()
+    spread(inputs, x_slot, x_ss, x_rs, "start")
 
     wo_part = rows_w // 2
     wo_src = w_out.at[tile(core, wo_part)]
@@ -574,6 +575,9 @@
         pos = lax.broadcasted_iota(jnp.int32, (BLK, 1), 0) + b * BLK
         return (pos.astype(F32) < length).astype(F32)
 
+    for it in qkv_items:
+        it.second()
+
     def n1_copy(i):
         block = nrm1.at[tile(2 * i + core, BLK)]
         return remote(block, block, n1_ss.at[i], n1_rs.at[i], other)
@@ -586,18 +590,14 @@
         nrm1[tile(2 * i + core, BLK), :] = (source * scale * gains[0:1, :]).astype(BF16)
         n1_copy(i).start()
 
-    qkv_items[0].second()
-    for it in qkv_items[1:]:
-        it.forward()
-    wo_each("start")
     for it in in_items:
         it.first()
-    qkv_items[0].third()
-    for it in qkv_items[1:]:
-        it.show()
+    for it in qkv_items:
         it.third()
     for i in range(SEQ):
         n1_copy(i).wait_recv()
+    in_items[0].second()
+    spread(cotangent, c_slot, c_ss, c_rs, "start", (0,))
 
     flip[BLK : BLK + 16, :] = jnp.ones((16, tokens), BF16)
     mine_lanes = [lane < 64, lane >= 64]
@@ -623,14 +623,13 @@
         return pltpu.make_async_copy(raised_o.at[2 * pair + qb], slots[qb], raised_s.at[qb])
 
     def later_inputs():
-        spread(cotangent, c_slot, c_ss, c_rs, "start")
-        for it in down_items:
-            it.first()
+        down_items[0].first()
+        spread(cotangent, c_slot, c_ss, c_rs, "start", (1,))
 
     forward_table = {
-        2: [in_items[0].second],
-        3: [in_items[1].forward, later_inputs, in_items[0].third, in_items[1].show],
-        5: [in_items[1].third],
+        0: [in_items[1].second, lambda: wo_each("start")],
+        1: [in_items[0].third, later_inputs],
+        3: [in_items[1].third],
     }
 
     @pl.loop(0, 3)
@@ -718,6 +717,9 @@
         nrm2[tile(2 * i + core, BLK), :] = (hidden * scale * gains[1:2, :]).astype(BF16)
         n2_copy(i, n2_ss, n2_rs).start()
         pp[0:1, :] += jnp.sum(hidden * block_valid(2 * i + core), 0, keepdims=True)
+    down_items[0].second()
+    for it in down_items[1:]:
+        it.first()
     for i in range(SEQ):
         n2_copy(i, n2_ss, n2_rs).wait_recv()
     for qb in range(2):
@@ -740,8 +742,8 @@
     for part in range(2):
         part_cols = slice(part * wide_part, (part + 1) * wide_part)
         if part == 1:
-            down_items[0].second()
             take_cotangent()
+            down_items[0].third()
         in_items[part].done()
 
         @pl.loop(0, 2)
@@ -1048,15 +1050,15 @@
             else:
                 getattr(by_name[name], STEPS[step])()
 
-    down_items[1].second()
-    down_items[0].third()
+    for it in down_items[1:]:
+        it.second()
     for i in range(ff_part // BLK):
         columns = jnp.concatenate(
             [act[:, f * ff_part + i * BLK : f * ff_part + (i + 1) * BLK] for f in range(SEQ)],
             axis=1,
         )
         gdn[i] = contract(columns, g_all(), 0, 0).astype(BF16).reshape(SEQ, BLK, width)
-        after(f"gdn{i}")
+    after("gdn2")
     for it in down_items:
         it.done()
     for it in in_items:
@@ -1637,7 +1639,6 @@
     pairs = half // BLK
     parts = part // BLK
     heads = rel_bias.shape[1]
-    gains = jnp.stack([attn_gain, ffn_gain]).astype(F32)
     anywhere = pl.BlockSpec(memory_space=pl.ANY)
     vmem = pl.BlockSpec(memory_space=pltpu.VMEM)
     smem = pl.BlockSpec(memory_space=pltpu.SMEM)
@@ -1716,7 +1717,7 @@
         pair_of(5)
         + pair_of(4)
         + pair_of(4)
-        + pair_of(7, 8)
+        + pair_of(8, 8)
         + pair_of(4)
         + pair_of(4) * 8
         + pair_of(chunks, 6)
@@ -1731,7 +1732,7 @@
     results = pl.pallas_call(
         fused_kernel,
         out_shape=out_shape,
-        in_specs=[anywhere] * 8 + [vmem, vmem, smem],
+        in_specs=[anywhere] * 8 + [vmem, vmem, vmem, smem],
         out_specs=(vmem, vmem, vmem) + (anywhere,) * 8,
         scratch_shapes=[pltpu.VMEM(*s) for s in scratch] + semaphores,
         compiler_params=pltpu.CompilerParams(
@@ -1747,7 +1748,8 @@
         w_out,
         w_ffn_in,
         w_ffn_out,
-        gains,
+        attn_gain,
+        ffn_gain,
         rel_bias,
         doc_lengths,
     )

time: 157 us -> 154 us (0.981)
  no operation moved by 1% of the time
where the time goes in v5:
time: 154 us; the launch traced here: 153 us
  Pallas kernels  153 us (99%)
    pallas_call x1, Pallas kernels, fused_on_device(): pl.pallas_call(fused_kernel, out_shape=out_shape, in_specs=[anywhere] * 8...  146 us
    pallas_call x1, Pallas kernels, fused_on_device(): pl.pallas_call(widen_kernel, out_shape=[shape(s, F32) for s in tiny + nar...  6.12 us

profile of v5, /device:TPU:0, one launch (start us, length us, event | category | flops | bytes accessed | tf_op | source)
XLA Modules:
  0.0 153.4 jit_solution(14300353063925385682)
XLA Ops:
  0.6 146.5 %block.1 = (f32[2,768]{1,0:T(2,128)}, f32[8,256]{1,0:T(8,128)}, f32[8,128]{1,0:T(8,128)}, bf16[2,256,768]{2,1,0:T(8,128)(2,1)}, bf16[192,768]{1,0:T(8,128)(2,1)}...) custom-call(bf16[2,256,768]{2,1,0:T(8,128)(2,1)} %inputs.1, ...), custom_call_target="tpu_custom_call" | custom-call | tf_op jit(solution)/shard_map/block/pallas_call | solution.py:1732
  147.1 6.1 %widen.1 = (f32[2,768]{1,0:T(2,128)}, f32[1,192]{1,0:T(1,128)}, f32[1,192]{1,0:T(1,128)}, f32[8,12]{1,0:T(8,128)}, f32[2,256,768]{2,1,0:T(8,128)}, /*index=5*/f3...) custom-call(f32[2,768]{1,0:T(2,128)} %get-tuple-element.32.pooled, ...), custom_call_target="tpu_custom_call" | custom-call | tf_op jit(solution)/shard_map/widen/pallas_call | solution.py:1771

commit v6 on v5

--- a/solution.py
+++ b/solution.py
@@ -1342,6 +1342,13 @@
 
     sgp_each("start")
     pltpu.make_async_copy(sg, sg_plane.at[place], sgp_rs.at[place]).start()
+    for copy in pending:
+        copy.wait_send()
+    spread(inputs, x_slot, x_ss, x_rs, "wait")
+    spread(cotangent, c_slot, c_ss, c_rs, "wait")
+    for it in qkv_items + down_items:
+        it.sent()
+    wo_each("wait")
     after("g1")
     after("end")
     for i in range(4):
@@ -1364,13 +1371,6 @@
 
     for i in range(4):
         await_copy(gx_o.at[i // 2, pl.ds((i % 2) * BLK, BLK)], gx_rs.at[i])
-    for copy in pending:
-        copy.wait_send()
-    spread(inputs, x_slot, x_ss, x_rs, "wait")
-    spread(cotangent, c_slot, c_ss, c_rs, "wait")
-    for it in qkv_items + down_items:
-        it.sent()
-    wo_each("wait")
     pool_each("wait")
     rso_each("wait")
     sgp_each("wait")
@@ -1754,7 +1754,7 @@
         doc_lengths,
     )
 
-    steps = 4
+    steps = 2
 
     def rows_spec(s):
         if len(s) == 3:

time: 154 us -> 153 us (level)
  no operation moved by 1% of the time
where the time goes in v6:
time: 153 us
  Pallas kernels  152 us (99%)
    pallas_call x1, Pallas kernels, fused_on_device(): pl.pallas_call(fused_kernel, out_shape=out_shape, in_specs=[anywhere] * 8...  146 us
    pallas_call x1, Pallas kernels, fused_on_device(): pl.pallas_call(widen_kernel, out_shape=[shape(s, F32) for s in tiny + nar...  5.35 us

profile of v6, /device:TPU:0, one launch (start us, length us, event | category | flops | bytes accessed | tf_op | source)
XLA Modules:
  0.0 152.6 jit_solution(41154518845870767)
XLA Ops:
  0.6 146.5 %block.1 = (f32[2,768]{1,0:T(2,128)}, f32[8,256]{1,0:T(8,128)}, f32[8,128]{1,0:T(8,128)}, bf16[2,256,768]{2,1,0:T(8,128)(2,1)}, bf16[192,768]{1,0:T(8,128)(2,1)}...) custom-call(bf16[2,256,768]{2,1,0:T(8,128)(2,1)} %inputs.1, ...), custom_call_target="tpu_custom_call" | custom-call | tf_op jit(solution)/shard_map/block/pallas_call | solution.py:1732
  147.1 5.3 %widen.1 = (f32[2,768]{1,0:T(2,128)}, f32[1,192]{1,0:T(1,128)}, f32[1,192]{1,0:T(1,128)}, f32[8,12]{1,0:T(8,128)}, f32[2,256,768]{2,1,0:T(8,128)}, /*index=5*/f3...) custom-call(f32[2,768]{1,0:T(2,128)} %get-tuple-element.32.pooled, ...), custom_call_target="tpu_custom_call" | custom-call | tf_op jit(solution)/shard_map/widen/pallas_call | solution.py:1771

commit v7 on v6

--- a/solution.py
+++ b/solution.py
@@ -97,10 +97,10 @@
 SCHEDULE = {
     "gdn2": [("d2", "s"), ("d1", "s")],
     "wd": [],
-    "gact": [("d2", "m")],
+    "gact": [("d2", "m"), ("d0", "s")],
     "gn": [("d1", "m")],
     "gin0": [],
-    "gin1": [("d0", "s")],
+    "gin1": [],
     "n2": [("i2", "s")],
     "op": [("d1", "z1"), ("d2", "z1"), ("d0", "m")],
     "u0": [("i3", "s")],
@@ -553,7 +553,7 @@
     for off in (-1, 0, 1):
         ids = bucket_of(off * BLK - minus)
         onehot = (lax.broadcasted_iota(jnp.int32, (32, 2 * BLK), 0) == ids).astype(BF16)
-        vecs[off + 1] = contract(table, onehot, 0, 0)[0:16, :]
+        vecs[off + 1] = contract(table, onehot, 0, 0)[0:24, :]
 
     @pl.loop(0, 6)
     def _(h):
@@ -1321,6 +1321,7 @@
         nrm2[i * BLK : (i + 1) * BLK, :] = result.astype(BF16)
 
     place = core * SEQ + chip
+    sg_sent = sg.at[pl.ds(0, sg_plane.shape[1])]
 
     def sgp_each(action):
         for step in range(SEQ):
@@ -1329,7 +1330,7 @@
                     continue
                 to_core = lax.rem(core + cross, 2)
                 copy = remote(
-                    sg,
+                    sg_sent,
                     sg_plane.at[place],
                     sgp_ss.at[step * 2 + cross],
                     sgp_rs.at[place],
@@ -1341,7 +1342,7 @@
                     copy.wait_send()
 
     sgp_each("start")
-    pltpu.make_async_copy(sg, sg_plane.at[place], sgp_rs.at[place]).start()
+    pltpu.make_async_copy(sg_sent, sg_plane.at[place], sgp_rs.at[place]).start()
     for copy in pending:
         copy.wait_send()
     spread(inputs, x_slot, x_ss, x_rs, "wait")
@@ -1387,7 +1388,7 @@
 
 def widen_kernel(pooled, small, table, gx, gq, gk, gv, go, gi, gd, *outs):
     pooled_out, one_out, two_out, table_out, *outs = outs
-    pooled_out[...] = pooled[...]
+    pooled_out[...] = pooled[0 : pooled_out.shape[0], :]
     one_out[...] = small[0:1, : one_out.shape[1]]
     two_out[...] = small[1:2, : two_out.shape[1]]
     table_out[...] = table[:, : table_out.shape[1]]
@@ -1653,7 +1654,7 @@
         (2 * part, width),
     ]
     out_shape = (
-        shape((docs, width), F32),
+        shape((8, width), F32),
         shape((8, 2 * BLK), F32),
         shape((8, BLK), F32),
         *(shape(s, BF16) for s in narrow),
@@ -1682,9 +1683,9 @@
         ((tokens, SEQ * part), BF16),
         ((SEQ, BLK, width), F32),
         ((2 * pairs, 5 * BLK, BLK), F32),
-        ((3, 16, 2 * BLK), F32),
+        ((3, 24, 2 * BLK), F32),
         ((tokens, BLK), BF16),
-        ((8, tokens), F32),
+        ((16, tokens), F32),
         ((BLK + 16, tokens), BF16),
         ((tokens, 3 * half), BF16),
         ((tokens, half), BF16),
@@ -1706,7 +1707,7 @@
         ((8, SEQ * part), F32),
         ((8, width), F32),
         ((4, 8, width), F32),
-        ((32, BLK), F32),
+        ((40, BLK), F32),
         ((8, 32, BLK), F32),
         ((4, 32, BLK), F32),
         ((BLK, BLK), F32),

time: 153 us -> 153 us (level)
  no operation moved by 1% of the time
where the time goes in v7:
time: 153 us; the launch traced here: 152 us
  Pallas kernels  151 us (99%)
    pallas_call x1, Pallas kernels, fused_on_device(): pl.pallas_call(fused_kernel, out_shape=out_shape, in_specs=[anywhere] * 8...  146 us
    pallas_call x1, Pallas kernels, fused_on_device(): pl.pallas_call(widen_kernel, out_shape=[shape(s, F32) for s in tiny + nar...  5.36 us

profile of v7, /device:TPU:0, one launch (start us, length us, event | category | flops | bytes accessed | tf_op | source)
XLA Modules:
  0.0 152.2 jit_solution(5798387240435065387)
XLA Ops:
  0.6 146.0 %block.1 = (f32[8,768]{1,0:T(8,128)}, f32[8,256]{1,0:T(8,128)}, f32[8,128]{1,0:T(8,128)}, bf16[2,256,768]{2,1,0:T(8,128)(2,1)}, bf16[192,768]{1,0:T(8,128)(2,1)}...) custom-call(bf16[2,256,768]{2,1,0:T(8,128)(2,1)} %inputs.1, ...), custom_call_target="tpu_custom_call" | custom-call | tf_op jit(solution)/shard_map/block/pallas_call | solution.py:1733
  146.7 5.4 %widen.1 = (f32[2,768]{1,0:T(2,128)}, f32[1,192]{1,0:T(1,128)}, f32[1,192]{1,0:T(1,128)}, f32[8,12]{1,0:T(8,128)}, f32[2,256,768]{2,1,0:T(8,128)}, /*index=5*/f3...) custom-call(f32[8,768]{1,0:T(8,128)} %get-tuple-element.32.pooled, ...), custom_call_target="tpu_custom_call" | custom-call | tf_op jit(solution)/shard_map/widen/pallas_call | solution.py:1772

commit v8 on v7

--- a/solution.py
+++ b/solution.py
@@ -1755,15 +1755,7 @@
         doc_lengths,
     )
 
-    steps = 2
-
-    def rows_spec(s):
-        if len(s) == 3:
-            return pl.BlockSpec(
-                (1, s[1] * s[0] // steps, s[2]),
-                lambda i: (i // (steps // s[0]), i % (steps // s[0]), 0),
-            )
-        return pl.BlockSpec((s[0] // steps, s[1]), lambda i: (i, 0))
+    steps = 1
 
     def whole_spec(s):
         return pl.BlockSpec(s, lambda i: (0,) * len(s))
@@ -1773,8 +1765,8 @@
         widen_kernel,
         out_shape=[shape(s, F32) for s in tiny + narrow],
         grid=(steps,),
-        in_specs=[whole_spec(r.shape) for r in results[:3]] + [rows_spec(s) for s in narrow],
-        out_specs=[whole_spec(s) for s in tiny] + [rows_spec(s) for s in narrow],
+        in_specs=[whole_spec(r.shape) for r in results[:3]] + [whole_spec(s) for s in narrow],
+        out_specs=[whole_spec(s) for s in tiny] + [whole_spec(s) for s in narrow],
         compiler_params=pltpu.CompilerParams(vmem_limit_bytes=VMEM_LIMIT),
         name="widen",
     )(*results[:-1])

time: 153 us -> 153 us (level)
  no operation moved by 1% of the time
where the time goes in v8:
time: 153 us; the launch traced here: 152 us
  Pallas kernels  152 us (99%)
    pallas_call x1, Pallas kernels, fused_on_device(): pl.pallas_call(fused_kernel, out_shape=out_shape, in_specs=[anywhere] * 8...  146 us
    pallas_call x1, Pallas kernels, fused_on_device(): pl.pallas_call(widen_kernel, out_shape=[shape(s, F32) for s in tiny + nar...  5.77 us

profile of v8, /device:TPU:0, one launch (start us, length us, event | category | flops | bytes accessed | tf_op | source)
XLA Modules:
  0.0 152.4 jit_solution(238169226369550339)
XLA Ops:
  0.6 146.0 %block.1 = (f32[8,768]{1,0:T(8,128)}, f32[8,256]{1,0:T(8,128)}, f32[8,128]{1,0:T(8,128)}, bf16[2,256,768]{2,1,0:T(8,128)(2,1)}, bf16[192,768]{1,0:T(8,128)(2,1)}...) custom-call(bf16[2,256,768]{2,1,0:T(8,128)(2,1)} %inputs.1, ...), custom_call_target="tpu_custom_call" | custom-call | tf_op jit(solution)/shard_map/block/pallas_call | solution.py:1733
  146.7 5.8 %widen.1 = (f32[2,768]{1,0:T(2,128)}, f32[1,192]{1,0:T(1,128)}, f32[1,192]{1,0:T(1,128)}, f32[8,12]{1,0:T(8,128)}, f32[2,256,768]{2,1,0:T(8,128)}, /*index=5*/f3...) custom-call(f32[8,768]{1,0:T(8,128)} %get-tuple-element.32.pooled, ...), custom_call_target="tpu_custom_call" | custom-call | tf_op jit(solution)/shard_map/widen/pallas_call | solution.py:1764
